TPU v7x, 32 devices: a whole 2x2x4 slice. The times are simulated.
32 devices in a mesh: fsdp: 16 (over z, y, core), expert: 2 (over x).
Axes of the slice: x: 2, y: 2, z: 4, core: 2. Of those that a mesh axis runs over, the one named last changes fastest.
Arguments:
- tokens: bfloat16 [2048, 5120], P('expert', 'fsdp'), may hold values from -6 to 6
- out_grad: bfloat16 [2048, 5120], P('expert', 'fsdp'), may hold values from -6 to 6
- slot_rows: int32 [2, 2, 24], P('expert'), may hold values from 0 to 1023, as said below
- expert_counts: int32 [2, 2], P('expert'), may hold values from 1 to 24, as said below
- route_prob: float32 [2, 48], P('expert'), may hold values from 0.05 to 0.9
- w_gate: bfloat16 [2, 5120, 1536], P('expert', 'fsdp'), may hold values from -0.078125 to 0.078125
- w_up: bfloat16 [2, 5120, 1536], P('expert', 'fsdp'), may hold values from -0.078125 to 0.078125
- w_down: bfloat16 [2, 5120, 1536], P('expert', 'fsdp'), may hold values from -0.15625 to 0.15625
Outputs:
- token_grad: bfloat16 [2048, 5120], P('expert', 'fsdp')
- gate_grad: float32 [2, 5120, 1536], P('expert', 'fsdp')
- up_grad: float32 [2, 5120, 1536], P('expert', 'fsdp')
- down_grad: float32 [2, 5120, 1536], P('expert', 'fsdp')
- prob_grad: float32 [2, 48], P('expert', 'fsdp')
Inputs may be any that keep to these rules, and one draw needn't show every extreme that they name: `slot_rows`: for each token group and expert the 24 listed rows are distinct. `expert_counts`: in every draw one expert has all 24 slots live from every token group.
All inputs are finite; a program needn't handle non-finite values.
Results may differ from a plain program's by a relative error of at most 0.0055.
Values may be sent and summed in bfloat16 or wider, within the bound.
No kernel may reach another device: no remote copies, remote signals or barrier semaphores. Data moves between devices by JAX's collectives and lax.ppermute only.
A program may use at most 64 MiB of HBM per device.

v0:
```python
import jax
import jax.numpy as jnp
from jax import lax
from jax.sharding import PartitionSpec as P


def hidden_backward(gate_sum, up_sum, down_sum, row_prob, live_mask):
    sigmoid_gate = jax.nn.sigmoid(gate_sum)
    silu_gate = gate_sum * sigmoid_gate
    hidden = lax.optimization_barrier((silu_gate * up_sum).astype(jnp.bfloat16)).astype(jnp.float32)
    row_scale = (row_prob * live_mask)[:, None]
    scaled_hidden = (hidden * row_scale).astype(jnp.bfloat16)
    hidden_grad = down_sum * row_scale
    up_act_grad = (hidden_grad * silu_gate).astype(jnp.bfloat16)
    gate_act_grad = (
        hidden_grad * up_sum * sigmoid_gate * (1.0 + gate_sum * (1.0 - sigmoid_gate))
    ).astype(jnp.bfloat16)
    prob_grad = live_mask * jnp.sum(hidden * down_sum, axis=1)
    return (scaled_hidden, gate_act_grad, up_act_grad, prob_grad)


def local(tokens, out_grad, slot_rows, expert_counts, route_prob, w_gate, w_up, w_down):
    sent_rows = slot_rows[0]
    recv_tokens, recv_grads = (
        lax.all_to_all(tokens[sent_rows], "expert", split_axis=0, concat_axis=0, tiled=True),
        lax.all_to_all(out_grad[sent_rows], "expert", split_axis=0, concat_axis=0, tiled=True),
    )
    source_count, slot_count, feature_count = recv_tokens.shape
    total_rows = source_count * slot_count
    token_rows = recv_tokens.reshape(total_rows, feature_count)
    grad_rows = recv_grads.reshape(total_rows, feature_count)
    live_mask = (
        (jnp.arange(slot_count, dtype=jnp.int32)[None, :] < expert_counts[0][:, None])
        .reshape(total_rows)
        .astype(jnp.float32)
    )
    row_prob = route_prob[0]
    gate_part = jnp.dot(token_rows, w_gate[0], preferred_element_type=jnp.float32)
    up_part = jnp.dot(token_rows, w_up[0], preferred_element_type=jnp.float32)
    down_part = jnp.dot(grad_rows, w_down[0], preferred_element_type=jnp.float32)
    gate_sum, up_sum, down_sum = lax.psum((gate_part, up_part, down_part), "fsdp")
    scaled_hidden, gate_act_grad, up_act_grad, prob_full = hidden_backward(
        gate_sum, up_sum, down_sum, row_prob, live_mask
    )
    share_rows = total_rows // lax.axis_size("fsdp")
    prob_grad = lax.dynamic_slice_in_dim(prob_full, lax.axis_index("fsdp") * share_rows, share_rows)
    over_rows = (((0,), (0,)), ((), ()))
    gate_grad = lax.dot_general(
        token_rows, gate_act_grad, over_rows, preferred_element_type=jnp.float32
    )
    up_grad = lax.dot_general(
        token_rows, up_act_grad, over_rows, preferred_element_type=jnp.float32
    )
    down_grad = lax.dot_general(
        grad_rows, scaled_hidden, over_rows, preferred_element_type=jnp.float32
    )
    over_hidden = (((1,), (1,)), ((), ()))
    slot_grad = (
        lax.dot_general(gate_act_grad, w_gate[0], over_hidden, preferred_element_type=jnp.float32)
        + lax.dot_general(up_act_grad, w_up[0], over_hidden, preferred_element_type=jnp.float32)
    ).astype(jnp.bfloat16)
    returned = lax.all_to_all(
        slot_grad.reshape(source_count, slot_count, feature_count),
        "expert",
        split_axis=0,
        concat_axis=0,
        tiled=True,
    )
    token_count = tokens.shape[0]
    route_table = (
        sent_rows.reshape(-1)[None, :] == jnp.arange(token_count, dtype=jnp.int32)[:, None]
    ).astype(jnp.bfloat16)
    token_grad = jnp.dot(
        route_table, returned.reshape(-1, feature_count), preferred_element_type=jnp.float32
    ).astype(jnp.bfloat16)
    return (token_grad, gate_grad[None], up_grad[None], down_grad[None], prob_grad[None])


def solution(mesh):
    return jax.shard_map(
        local,
        mesh=mesh,
        in_specs=(
            P("expert", "fsdp"),
            P("expert", "fsdp"),
            P("expert", None, None),
            P("expert", None),
            P("expert", None),
            P("expert", "fsdp", None),
            P("expert", "fsdp", None),
            P("expert", "fsdp", None),
        ),
        out_specs=(
            P("expert", "fsdp"),
            P("expert", "fsdp", None),
            P("expert", "fsdp", None),
            P("expert", "fsdp", None),
            P("expert", "fsdp"),
        ),
        check_vma=False,
    )
```

profile of v0, /device:TPU:0, one launch (start us, length us, event | category | flops | bytes accessed | tf_op | source)
XLA Modules:
  0.0 147.3 jit_solution(14712813689028504468)
XLA Ops:
  7.2 0.0 copy-start
  7.2 0.0 copy-start.3
  7.2 0.8 compare_select_fusion
  8.0 0.1 reshape.76
  8.1 1.4 copy.14
  9.5 0.0 copy-start.1
  9.5 1.3 gather_fusion.1
  10.8 4.2 %all-to-all-start.1 = ((bf16[2,24,320]{2,1,0:T(8,128)(2,1)}), bf16[2,24,320]{2,1,0:T(8,128)(2,1)S(1)}, u32[]{:S(2)}, u32[]{:S(2)}) async-start(bf16[2,24,320]{2,1,0:T(8,128)(2,1)} %bitcast.6), calls=%async_computation.1 | async-start | bytes 73728 | tf_op jit(solution)/shard_map/all_to_all | solution.py:25
  15.0 0.8 eq.15
  15.8 0.0 copy-done.3
  15.8 0.4 copy.13
  16.2 1.3 gather_fusion
  17.4 0.0 copy-start.2
  17.4 1.6 %all-to-all-done.1 = bf16[2,24,320]{2,1,0:T(8,128)(2,1)S(1)} async-done(((bf16[2,24,320]{2,1,0:T(8,128)(2,1)}), bf16[2,24,320]{2,1,0:T(8,128)(2,1)S(1)}, u32[]{:S(2)}, u32[]{:S(2)}) %all-to-all-start.1) | async-done | bytes 30752 | tf_op jit(solution)/shard_map/all_to_all | solution.py:25
  19.0 3.3 %all-to-all-start = ((bf16[2,24,320]{2,1,0:T(8,128)(2,1)}), bf16[2,24,320]{2,1,0:T(8,128)(2,1)S(1)}, u32[]{:S(2)}, u32[]{:S(2)}) async-start(bf16[2,24,320]{2,1,0:T(8,128)(2,1)} %bitcast.1), calls=%async_computation | async-start | bytes 73728 | tf_op jit(solution)/shard_map/all_to_all | solution.py:26
  22.3 0.0 all-reduce.3.cloned.1.call-start
  22.3 0.0 copy-done
  22.3 1.0 fusion.3
  23.3 0.0 copy-done.1
  23.3 0.0 copy-start.4
  23.3 0.0 copy-start.5
  23.3 1.0 fusion.6
  24.4 1.9 %all-to-all-done = bf16[2,24,320]{2,1,0:T(8,128)(2,1)S(1)} async-done(((bf16[2,24,320]{2,1,0:T(8,128)(2,1)}), bf16[2,24,320]{2,1,0:T(8,128)(2,1)S(1)}, u32[]{:S(2)}, u32[]{:S(2)}) %all-to-all-start) | async-done | bytes 30752 | tf_op jit(solution)/shard_map/all_to_all | solution.py:26
  26.2 0.0 copy-done.2
  26.2 1.0 fusion.8
  27.2 0.0 all-reduce.3.cloned.1.call-update
  27.3 0.0 copy-done.4
  27.3 0.1 iota_compare_fusion.2
  27.3 0.1 lt.42
  27.4 0.0 copy-done.5
  27.4 95.5 %all-reduce.3.cloned.1.call-done = (f32[48,1536]{1,0:T(8,128)}, f32[48,1536]{1,0:T(8,128)}, f32[48,1536]{1,0:T(8,128)}) async-done(((f32[48,1536]{1,0:T(8,128)}, f32[48,1536]{1,0:T(8,128)}, f32[48,1536]{1,0:T(8,128)}), (f32[48,1536]{1,0:T(8,128)}, f32[48,1536]{1,0:T(8,128)}, f32[48,1536]{1,0:T(8,128)})) %all-reduce.3.cloned.1.call-update) | async-done | bytes 884752 | tf_op jit(solution)/shard_map/psum | solution.py:41
  122.9 1.3 multiply_convert_fusion.1
  124.3 1.1 fusion.11
  125.4 1.7 %convolution_bitcast_fusion = f32[1,320,1536]{2,1,0:T(8,128)} fusion(bf16[48,320]{1,0:T(8,128)(2,1)S(1)} %bitcast.50, bf16[48,1536]{1,0:T(8,128)(2,1)S(1)} %get-tuple-element.10, f32[48]{0:T(128)S(1)} %bitcast_select_fusion), kind=kOutput, calls=%fused_computation.2 | convolution fusion | flops 47407104 | bytes 2144448 | tf_op jit(solution)/shard_map/dot_general | solution.py:54
  127.1 0.4 fusion.1
  127.5 1.7 %convolution_bitcast_fusion.2 = f32[1,320,1536]{2,1,0:T(8,128)} fusion(bf16[48,320]{1,0:T(8,128)(2,1)S(1)} %bitcast.47, bf16[48,1536]{1,0:T(8,128)(2,1)S(1)} %get-tuple-element.9), kind=kOutput, calls=%fused_computation.4 | convolution fusion | flops 47185920 | bytes 2144256 | tf_op jit(solution)/shard_map/dot_general | solution.py:48
  129.3 1.7 %convolution_bitcast_fusion.1 = f32[1,320,1536]{2,1,0:T(8,128)} fusion(bf16[48,320]{1,0:T(8,128)(2,1)S(1)} %bitcast.48, bf16[48,1536]{1,0:T(8,128)(2,1)S(1)} %get-tuple-element.8), kind=kOutput, calls=%fused_computation.3 | convolution fusion | flops 47185920 | bytes 2144256 | tf_op jit(solution)/shard_map/dot_general | solution.py:51
  131.0 1.0 fusion
  132.0 3.3 %all-to-all-start.2 = ((bf16[2,24,320]{2,1,0:T(8,128)(2,1)}), bf16[2,24,320]{2,1,0:T(8,128)(2,1)S(1)}, u32[]{:S(2)}, u32[]{:S(2)}) async-start(bf16[2,24,320]{2,1,0:T(8,128)(2,1)} %bitcast.10), calls=%async_computation.2 | async-start | bytes 73728 | tf_op jit(solution)/shard_map/all_to_all | solution.py:62
  135.3 0.6 dynamic-slice_bitcast_fusion
  135.9 3.4 %all-to-all-done.2 = bf16[2,24,320]{2,1,0:T(8,128)(2,1)S(1)} async-done(((bf16[2,24,320]{2,1,0:T(8,128)(2,1)}), bf16[2,24,320]{2,1,0:T(8,128)(2,1)S(1)}, u32[]{:S(2)}, u32[]{:S(2)}) %all-to-all-start.2) | async-done | bytes 30752 | tf_op jit(solution)/shard_map/all_to_all | solution.py:62
  139.2 1.2 convolution_convert_fusion
  (3 shorter events, 0.0 us)
Async XLA Ops:
  7.2 15.2 %copy-start = (bf16[1,320,1536]{2,1,0:T(8,128)(2,1)S(1)}, bf16[1,320,1536]{2,1,0:T(8,128)(2,1)}, u32[]{:S(2)}) copy-start(bf16[1,320,1536]{2,1,0:T(8,128)(2,1)} %param.13) | copy-start | bytes 2949124
  7.2 8.6 %copy-start.3 = (bf16[1024,320]{0,1:T(8,128)(2,1)S(1)}, bf16[1024,320]{0,1:T(8,128)(2,1)}, u32[]{:S(2)}) copy-start(bf16[1024,320]{0,1:T(8,128)(2,1)} %param.9) | copy-start | bytes 1966084
  9.5 13.8 %copy-start.1 = (bf16[1,320,1536]{2,1,0:T(8,128)(2,1)S(1)}, bf16[1,320,1536]{2,1,0:T(8,128)(2,1)}, u32[]{:S(2)}) copy-start(bf16[1,320,1536]{2,1,0:T(8,128)(2,1)} %param.14) | copy-start | bytes 2949124
  10.8 8.2 %all-to-all-start.1 = ((bf16[2,24,320]{2,1,0:T(8,128)(2,1)}), bf16[2,24,320]{2,1,0:T(8,128)(2,1)S(1)}, u32[]{:S(2)}, u32[]{:S(2)}) async-start(bf16[2,24,320]{2,1,0:T(8,128)(2,1)} %bitcast.6), calls=%async_computation.1 | async-start | bytes 73728 | tf_op jit(solution)/shard_map/all_to_all | solution.py:25
  17.4 8.8 %copy-start.2 = (bf16[1,320,1536]{2,1,0:T(8,128)(2,1)S(1)}, bf16[1,320,1536]{2,1,0:T(8,128)(2,1)}, u32[]{:S(2)}) copy-start(bf16[1,320,1536]{2,1,0:T(8,128)(2,1)} %param.15) | copy-start | bytes 2949124
  19.0 7.2 %all-to-all-start = ((bf16[2,24,320]{2,1,0:T(8,128)(2,1)}), bf16[2,24,320]{2,1,0:T(8,128)(2,1)S(1)}, u32[]{:S(2)}, u32[]{:S(2)}) async-start(bf16[2,24,320]{2,1,0:T(8,128)(2,1)} %bitcast.1), calls=%async_computation | async-start | bytes 73728 | tf_op jit(solution)/shard_map/all_to_all | solution.py:26
  22.3 100.7 %all-reduce.3.cloned.1.call-start = ((), (), s32[]{:S(2)}) async-start(), calls=%async_computation.3 | async-start | bytes 1769472 | tf_op jit(solution)/shard_map/psum | solution.py:41
  23.3 3.9 %copy-start.4 = (s32[1,2]{1,0:T(1,128)S(1)}, s32[1,2]{1,0:T(1,128)}, u32[]{:S(2)}) copy-start(s32[1,2]{1,0:T(1,128)} %param.11) | copy-start | bytes 28
  23.3 4.1 %copy-start.5 = (f32[1,48]{1,0:T(1,128)S(1)}, f32[1,48]{1,0:T(1,128)}, u32[]{:S(2)}) copy-start(f32[1,48]{1,0:T(1,128)} %param.12) | copy-start | bytes 580
  132.0 7.2 %all-to-all-start.2 = ((bf16[2,24,320]{2,1,0:T(8,128)(2,1)}), bf16[2,24,320]{2,1,0:T(8,128)(2,1)S(1)}, u32[]{:S(2)}, u32[]{:S(2)}) async-start(bf16[2,24,320]{2,1,0:T(8,128)(2,1)} %bitcast.10), calls=%async_computation.2 | async-start | bytes 73728 | tf_op jit(solution)/shard_map/all_to_all | solution.py:62
Sparse Core Ops, SparseCore 0:
  27.5 95.4 all-reduce.2
where the time goes:
time: 148 us; the launch traced here: 147 us
  waiting for transfers between devices  102 us (69%)
  between operations  14.1 us (10%)
  matrix products  10.9 us (7%)
  starting transfers between devices  10.8 us (7%)
  local copies, waits for them, and re-layouts  5.9 us (4%)
  other arithmetic  3.32 us (2%)
    psum x1, waiting for transfers between devices, local(): lax.psum((gate_part, up_part, down_part), 'fsdp')  95.5 us
    all_to_all x1, starting transfers between devices, local(): lax.all_to_all(tokens[sent_rows], 'expert', split_axis=0, concat_axis=0,...  4.21 us
    all_to_all x1, waiting for transfers between devices, local(): lax.all_to_all(slot_grad.reshape(source_count, slot_count, feature_count)...  3.36 us
    all_to_all x1, starting transfers between devices, local(): lax.all_to_all(out_grad[sent_rows], 'expert', split_axis=0, concat_axis=0...  3.26 us
    all_to_all x1, starting transfers between devices, local(): lax.all_to_all(slot_grad.reshape(source_count, slot_count, feature_count)...  3.26 us
  transfers between devices with their start and end apart: 4, of which 4 were waited for; matrix products, arithmetic and copies ran while one was open for 4% of the time, Pallas kernels for 0%

commit v1 on v0

v1 whole, which is shorter than its diff:
```python
import jax
import jax.numpy as jnp
from jax import lax
from jax.experimental import pallas as pl
from jax.experimental.pallas import tpu as pltpu
from jax.sharding import PartitionSpec as P

BF16 = jnp.bfloat16
F32 = jnp.float32
VMEM = pl.BlockSpec(memory_space=pltpu.VMEM)
SMEM = pl.BlockSpec(memory_space=pltpu.SMEM)
PARAMS = pltpu.CompilerParams(vmem_limit_bytes=40 * 2**20)


def dot(a, b, contract):
    return lax.dot_general(a, b, ((contract[0:1], contract[1:2]), ((), ())), preferred_element_type=F32)


def gather_kernel(order, slot_rows, tokens_t, grads_t, rows_out, onehot_out, onehot_f):
    experts, slots = slot_rows.shape
    count = tokens_t.shape[1]
    lane = lax.broadcasted_iota(jnp.int32, (8, count), 1)
    sub = lax.broadcasted_iota(jnp.int32, (8, count), 0)
    for j in range(experts):
        for base in range(0, slots, 8):
            picked = jnp.zeros((8, count), jnp.int32)
            for r in range(8):
                picked = jnp.where(sub == r, slot_rows[order[j], base + r], picked)
            onehot_f[pl.ds(j * slots + base, 8), :] = (picked == lane).astype(F32)
    onehot = onehot_f[...].astype(BF16)
    onehot_out[...] = onehot
    for kind, source in enumerate((tokens_t, grads_t)):
        rows = dot(onehot, source[...], (1, 1))
        for j in range(experts):
            rows_out[j, kind] = rows[j * slots : (j + 1) * slots].astype(BF16)


def stacked_rows(blocks, kind):
    return jnp.concatenate([block[kind].astype(F32) for block in blocks], axis=0).astype(BF16)


def partial_kernel(where, own, recv, w_gate, w_up, w_down, out):
    blocks = [own] + [recv.at[j] for j in range(recv.shape[0])]
    tok, grad = stacked_rows(blocks, 0), stacked_rows(blocks, 1)
    chunk_rows, width = out.shape[1] // 3, out.shape[2]
    for jy in range(2):
        column = where[0] + ((where[1] & 1) ^ jy) * width
        at = pl.ds(pl.multiple_of(column, 128), width)
        for q, (x, w) in enumerate(((tok, w_gate), (tok, w_up), (grad, w_down))):
            sums = dot(x, w[0, :, at], (1, 0))
            for part in range(2):
                chunk = ((where[1] >> 1) ^ part) * 2 + jy
                out[chunk, pl.ds(q * chunk_rows, chunk_rows), :] = sums[part * chunk_rows : (part + 1) * chunk_rows]


def hidden_kernel(order, part, counts, prob, sums, recv, out):
    experts = counts.shape[0]
    slots = prob.shape[1] // experts
    total_rows = prob.shape[1]
    rows = sums.shape[0] // 3
    padded = out.shape[0] // 3
    width = sums.shape[1]
    total = sums[...] + recv[...]
    gate, up, down = total[:rows], total[rows : 2 * rows], total[2 * rows :]
    row = lax.broadcasted_iota(jnp.int32, (rows, 1), 0) + part[0] * rows
    slot = row
    place = jnp.zeros((rows, 1), jnp.int32)
    live_count = jnp.zeros((rows, 1), jnp.int32)
    for j in range(experts):
        inside = (row >= j * slots) & (row < (j + 1) * slots)
        slot = jnp.where(inside, row - j * slots, slot)
        place = jnp.where(inside, order[j] * slots + row - j * slots, place)
        live_count = jnp.where(inside, counts[order[j]], live_count)
    live = (slot < live_count).astype(F32)
    diagonal = lax.broadcasted_iota(jnp.int32, (rows, total_rows), 1) == place
    row_prob = jnp.sum(jnp.where(diagonal, prob[...], 0.0), axis=1, keepdims=True)
    scale = row_prob * live
    sigmoid = jax.nn.sigmoid(gate)
    silu = gate * sigmoid
    hidden = (silu * up).astype(BF16).astype(F32)
    hidden_grad = down * scale
    prob_grad = live * jnp.sum(hidden * down, axis=1, keepdims=True)
    prob_row = jnp.sum(jnp.where(diagonal, prob_grad, 0.0), axis=0, keepdims=True)
    high = prob_row.astype(BF16).astype(F32)
    tail = jnp.concatenate([high, prob_row - high, jnp.zeros((padded - rows - 2, total_rows), F32)], axis=0)
    tail = jnp.concatenate([tail, jnp.zeros((padded - rows, width - total_rows), F32)], axis=1)
    zeros = jnp.zeros((padded - rows, width), F32)
    gate_act_grad = hidden_grad * up * sigmoid * (1.0 + gate * (1.0 - sigmoid))
    for q, (x, end) in enumerate(((hidden * scale, tail), (gate_act_grad, zeros), (hidden_grad * silu, zeros))):
        out[pl.ds(q * padded, padded), :] = jnp.concatenate([x, end], axis=0).astype(BF16)


def piece(near, far, where, side, jy, q, rows):
    acts = far if side else near
    padded = acts.shape[1] // 3
    at = pl.ds(q * padded, padded)
    halves = [acts[((where[1] >> 1) ^ part) * 2 + jy, at, :].astype(F32)[: rows // 2] for part in range(2)]
    return jnp.concatenate(halves, axis=0).astype(BF16)


def piece_column(where, side, jy, width):
    base = where[0] if side == 0 else 2 * width - where[0]
    return base + ((where[1] & 1) ^ jy) * width


def slot_kernel(where, near, far, w_gate, w_up, out, prob_out):
    width = near.shape[2]
    slots = out.shape[1]
    rows = out.shape[0] * slots
    padded = near.shape[1] // 3
    total = jnp.zeros((rows, out.shape[2]), F32)
    tail = jnp.zeros((padded - rows // 2, width), F32)
    for side in range(2):
        for jy in range(2):
            at = pl.ds(pl.multiple_of(piece_column(where, side, jy, width), 128), width)
            for q, w in ((1, w_gate), (2, w_up)):
                total += dot(piece(near, far, where, side, jy, q, rows), w[0, :, at], (1, 1))
            for jz in range(2):
                acts = far if side else near
                tail += acts[jz * 2 + jy, pl.ds(0, padded), :].astype(F32)[rows // 2 :]
    for j in range(out.shape[0]):
        out[j] = total[j * slots : (j + 1) * slots].astype(BF16)
    prob_out[...] = tail[0:1] + tail[1:2]


def weight_grad_kernel(where, own, recv, near, far, gate_grad, up_grad, down_grad):
    blocks = [own] + [recv.at[j] for j in range(recv.shape[0])]
    tok, grad = stacked_rows(blocks, 0), stacked_rows(blocks, 1)
    rows = tok.shape[0]
    for i in range(4):
        @pl.when(pl.program_id(0) == i)
        def _(i=i):
            side, jy = i // 2, i % 2
            for q, x, out in ((0, grad, down_grad), (1, tok, gate_grad), (2, tok, up_grad)):
                out[0] = dot(x, piece(near, far, where, side, jy, q, rows), (0, 0))


def token_grad_kernel(own, recv, onehot, out):
    blocks = [own[...]] + [recv[j] for j in range(recv.shape[0])]
    slot_grad = jnp.concatenate([block.astype(F32) for block in blocks], axis=0).astype(BF16)
    out[...] = dot(slot_grad, onehot[...], (0, 0)).astype(BF16)


def local(tokens, out_grad, slot_rows, expert_counts, route_prob, w_gate, w_up, w_down):
    fsdp, experts = lax.axis_size("fsdp"), lax.axis_size("expert")
    steps = fsdp.bit_length() - 1
    me, my_expert = lax.axis_index("fsdp"), lax.axis_index("expert")
    token_count, features = tokens.shape
    _, _, slots = slot_rows.shape
    rows = experts * slots
    hidden = w_gate.shape[2]
    half, quarter = hidden // 2, hidden // 4
    side, corner = me & 1, (me >> 1) & 3
    where = jnp.stack([side * half, corner]).astype(jnp.int32)
    other = jnp.stack([(1 - side) * half, corner]).astype(jnp.int32)

    def swap(x, mask):
        return lax.ppermute(x, "fsdp", [(i, i ^ mask) for i in range(fsdp)])

    def to_expert(x):
        if experts == 2:
            return x[0], lax.ppermute(x[1], "expert", [(0, 1), (1, 0)])[None]
        moved = lax.all_to_all(x, "expert", split_axis=0, concat_axis=0, tiled=True)
        return moved[0], moved[1:]

    if experts == 2:
        order = jnp.stack([my_expert, 1 - my_expert]).astype(jnp.int32)
    else:
        order = jnp.arange(experts, dtype=jnp.int32)

    rows_out, onehot = pl.pallas_call(
        gather_kernel,
        out_shape=(
            jax.ShapeDtypeStruct((experts, 2, slots, features), BF16),
            jax.ShapeDtypeStruct((rows, token_count), BF16),
        ),
        in_specs=[SMEM, SMEM, VMEM, VMEM],
        out_specs=(VMEM, VMEM),
        scratch_shapes=[pltpu.VMEM((rows, token_count), F32)],
        compiler_params=PARAMS,
        name="gather_rows",
    )(order, slot_rows[0], tokens.T, out_grad.T)
    own, recv = to_expert(rows_out)

    def partial(which):
        return pl.pallas_call(
            partial_kernel,
            out_shape=jax.ShapeDtypeStruct((4, 3 * rows // 2, quarter), F32),
            in_specs=[SMEM] + [VMEM] * 5,
            out_specs=VMEM,
            compiler_params=PARAMS,
            cost_estimate=pl.CostEstimate(
                flops=6 * rows * features * half, bytes_accessed=3 * features * half * 2, transcendentals=0
            ),
            name="partial_sums",
        )(which, own, recv, w_gate, w_up, w_down)

    sent = partial(other)
    arrived = swap(sent, 1)
    kept = partial(where)
    total = kept + arrived
    total = total[0] + swap(total[1], 2) + swap(total[2], 4) + swap(total[3], 6)
    for b in range(3, steps):
        arrived = swap(total, 1 << b)
        if b < steps - 1:
            total = total + arrived
    padded = (rows // 2 + 2 + 15) // 16 * 16
    acts = pl.pallas_call(
        hidden_kernel,
        out_shape=jax.ShapeDtypeStruct((3 * padded, quarter), BF16),
        in_specs=[SMEM, SMEM, SMEM, VMEM, VMEM, VMEM],
        out_specs=VMEM,
        compiler_params=PARAMS,
        name="hidden",
    )(order, (corner >> 1)[None], expert_counts[0], route_prob, total, arrived)
    near = jnp.stack([acts, swap(acts, 2), swap(acts, 4), swap(acts, 6)])
    far = swap(near, 1)

    slot_grad, prob_row = pl.pallas_call(
        slot_kernel,
        out_shape=(
            jax.ShapeDtypeStruct((experts, slots, features), BF16),
            jax.ShapeDtypeStruct((1, quarter), F32),
        ),
        in_specs=[SMEM, VMEM, VMEM, VMEM, VMEM],
        out_specs=(VMEM, VMEM),
        compiler_params=PARAMS,
        name="slot_grad",
    )(where, near, far, w_gate, w_up)
    slot_own, slot_recv = to_expert(slot_grad)

    grad_shape = jax.ShapeDtypeStruct((1, features, hidden), F32)

    def grad_place(i, where):
        base = jnp.where(i < 2, where[0], half - where[0]) // quarter
        return 0, 0, base + ((where[1] & 1) ^ (i & 1))

    grad_spec = pl.BlockSpec((1, features, quarter), grad_place)
    whole = lambda x: pl.BlockSpec(x.shape, lambda i, where: (0,) * x.ndim)
    gate_grad, up_grad, down_grad = pl.pallas_call(
        weight_grad_kernel,
        out_shape=(grad_shape,) * 3,
        grid_spec=pltpu.PrefetchScalarGridSpec(
            num_scalar_prefetch=1,
            grid=(4,),
            in_specs=[whole(x) for x in (own, recv, near, far)],
            out_specs=(grad_spec,) * 3,
        ),
        compiler_params=PARAMS,
        cost_estimate=pl.CostEstimate(
            flops=6 * rows * features * hidden, bytes_accessed=12 * features * hidden, transcendentals=0
        ),
        name="weight_grads",
    )(where, own, recv, near, far)

    token_grad = pl.pallas_call(
        token_grad_kernel,
        out_shape=jax.ShapeDtypeStruct((features, token_count), BF16),
        in_specs=[VMEM] * 3,
        out_specs=VMEM,
        compiler_params=PARAMS,
        name="token_grad",
    )(slot_own, slot_recv, onehot).T
    share = rows // fsdp
    prob_grad = lax.dynamic_slice_in_dim(prob_row, me * share, share, axis=1)
    return (token_grad, gate_grad, up_grad, down_grad, prob_grad)


def solution(mesh):
    return jax.shard_map(
        local,
        mesh=mesh,
        in_specs=(
            P("expert", "fsdp"),
            P("expert", "fsdp"),
            P("expert", None, None),
            P("expert", None),
            P("expert", None),
            P("expert", "fsdp", None),
            P("expert", "fsdp", None),
            P("expert", "fsdp", None),
        ),
        out_specs=(
            P("expert", "fsdp"),
            P("expert", "fsdp", None),
            P("expert", "fsdp", None),
            P("expert", "fsdp", None),
            P("expert", "fsdp"),
        ),
        check_vma=False,
    )
```

time: 148 us -> 52.1 us (0.35)
  waiting for transfers between devices: 102 us -> 18 us
  between operations: 14.1 us -> 0.77 us
  matrix products: 10.9 us -> 0 us
  Pallas kernels: 0 us -> 10.1 us
  starting transfers between devices: 10.8 us -> 14.5 us
  other arithmetic: 3.32 us -> 1.37 us
    psum x1 -> x0, waiting for transfers between devices: 95.5 us -> none  [local(): lax.psum((gate_part, up_part, down_part), 'fsdp')]
    ppermute x0 -> x11, waiting for transfers between devices: none -> 18 us  [the longest x9 16.2 us: swap(): return lax.ppermute(x, 'fsdp', [(i, i ^ mask) for i in range(fsdp)])]
    ppermute x0 -> x11, starting transfers between devices: none -> 14.5 us  [the longest x9 10 us: swap(): return lax.ppermute(x, 'fsdp', [(i, i ^ mask) for i in range(fsdp)])]
    dot_general x9 -> x0, matrix products: 10.9 us -> none  [the longest x1 1.74 us: local(): lax.dot_general(grad_rows, scaled_hidden, over_rows, preferred_element_ty...]
    all_to_all x3 -> x0, starting transfers between devices: 10.7 us -> none  [the longest x1 4.21 us: local(): lax.all_to_all(tokens[sent_rows], 'expert', split_axis=0, concat_axis=0,...]
    pallas_call x0 -> x7, Pallas kernels: none -> 10.1 us  [the longest x1 4.08 us: local(): pl.pallas_call(weight_grad_kernel, out_shape=(grad_shape,) * 3, grid_spec...]
    all_to_all x3 -> x0, waiting for transfers between devices: 6.79 us -> none  [the longest x1 3.36 us: local(): lax.all_to_all(slot_grad.reshape(source_count, slot_count, feature_count)...]
    unnamed x14 -> x24, local copies, waits for them, and re-layouts: 1.82 us -> 6.37 us
  transfers between devices with their start and end apart: 4 -> 11, of which waited for: 4 -> 10; matrix products, arithmetic and copies ran while one was open for 4% -> 1% of each run, Pallas kernels for 0% -> 10%
where the time goes in v1:
time: 52.1 us; the launch traced here: 51.8 us
  waiting for transfers between devices  18 us (35%)
  starting transfers between devices  14.5 us (28%)
  Pallas kernels  10.1 us (19%)
  local copies, waits for them, and re-layouts  6.99 us (13%)
  other arithmetic  1.37 us (3%)
  between operations  0.77 us (1%)
    ppermute x9, waiting for transfers between devices, swap(): return lax.ppermute(x, 'fsdp', [(i, i ^ mask) for i in range(fsdp)])  16.2 us
    ppermute x9, starting transfers between devices, swap(): return lax.ppermute(x, 'fsdp', [(i, i ^ mask) for i in range(fsdp)])  10 us
    unnamed x24, local copies, waits for them, and re-layouts  6.37 us
    ppermute x2, starting transfers between devices, to_expert(): return (x[0], lax.ppermute(x[1], 'expert', [(0, 1), (1, 0)])[None])  4.49 us
    pallas_call x1, Pallas kernels, local(): pl.pallas_call(weight_grad_kernel, out_shape=(grad_shape,) * 3, grid_spec...  4.08 us
    ppermute x2, waiting for transfers between devices, to_expert(): return (x[0], lax.ppermute(x[1], 'expert', [(0, 1), (1, 0)])[None])  1.86 us
    pallas_call x2, Pallas kernels, partial(): pl.pallas_call(partial_kernel, out_shape=jax.ShapeDtypeStruct((4, 3 * row...  1.85 us
    pallas_call x1, Pallas kernels, local(): pl.pallas_call(slot_kernel, out_shape=(jax.ShapeDtypeStruct((experts, slo...  1.23 us
  transfers between devices with their start and end apart: 11, of which 10 were waited for; matrix products, arithmetic and copies ran while one was open for 1% of the time, Pallas kernels for 10%

profile of v1, /device:TPU:0, one launch (start us, length us, event | category | flops | bytes accessed | tf_op | source)
XLA Modules:
  0.0 51.8 jit_solution(15754347752101395101)
XLA Ops:
  0.6 0.0 copy-start
  0.6 0.1 pad_add_fusion.1.order
  0.7 0.0 copy-start.5
  0.7 1.2 %copy-done.5 = bf16[1024,320]{0,1:T(8,128)(2,1)S(1)} copy-done((bf16[1024,320]{0,1:T(8,128)(2,1)S(1)}, bf16[1024,320]{0,1:T(8,128)(2,1)}, u32[]{:S(2)}) %copy-start.5) | copy-done | bytes 655384
  1.9 0.0 copy-start.6
  1.9 1.1 %copy-done.6 = bf16[1024,320]{0,1:T(8,128)(2,1)S(1)} copy-done((bf16[1024,320]{0,1:T(8,128)(2,1)S(1)}, bf16[1024,320]{0,1:T(8,128)(2,1)}, u32[]{:S(2)}) %copy-start.6) | copy-done | bytes 655384
  3.0 0.0 copy-start.9
  3.0 0.7 %copy-done.9 = s32[1,2,24]{2,1,0:T(2,128)S(1)} copy-done((s32[1,2,24]{2,1,0:T(2,128)S(1)}, s32[1,2,24]{2,1,0:T(2,128)}, u32[]{:S(2)}) %copy-start.9) | copy-done | bytes 216
  3.6 1.0 %gather_rows.1 = (bf16[2,2,24,320]{3,2,1,0:T(8,128)(2,1)S(1)}, bf16[48,1024]{1,0:T(8,128)(2,1)S(1)}) custom-call(s32[2]{0:T(128)S(1)} %pad_add_fusion.1.order, s32[2,24]{1,0:T(2,128)S(1)} %bitcast.46, bf16[320,1024]{1,0:T(8,128)(2,1)S(1)} %bitcast.39, bf16[320,1024]{1,0:T(8,128)(2,1)S(1)} %bitcast.40), custom_call_target="tpu_custom_call" | custom-call | tf_op jit(solution)/shard_map/gather_rows/pallas_call | solution.py:171
  4.7 0.0 copy-start.7
  4.7 0.6 %copy-done.7 = bf16[48,1024]{1,0:T(8,128)(2,1)} copy-done((bf16[48,1024]{1,0:T(8,128)(2,1)}, bf16[48,1024]{1,0:T(8,128)(2,1)S(1)}, u32[]{:S(2)}) %copy-start.7) | copy-done | bytes 98328
  5.3 2.9 %collective-permute-start = (bf16[2,24,320]{2,1,0:T(8,128)(2,1)S(1)}, bf16[2,24,320]{2,1,0:T(8,128)(2,1)S(1)}, u32[]{:S(2)}, u32[]{:S(2)}) collective-permute-start(bf16[2,24,320]{2,1,0:T(8,128)(2,1)S(1)} %get-tuple-element.22), channel_id=1, source_target_pairs={{0,1},{1,0},{2,3},{3,2},{4,5},{5,4},{6,7},{7,6},{8,9},{9,8},{10,11... | collective-permute-start | bytes 92168 | tf_op jit(solution)/shard_map/ppermute | solution.py:162
  8.3 0.1 pad_add_fusion.2.where
  8.4 1.9 %collective-permute-done = bf16[2,24,320]{2,1,0:T(8,128)(2,1)S(1)} collective-permute-done((bf16[2,24,320]{2,1,0:T(8,128)(2,1)S(1)}, bf16[2,24,320]{2,1,0:T(8,128)(2,1)S(1)}, u32[]{:S(2)}, u32[]{:S(2)}) %collective-permute-start) | collective-permute-done | bytes 30752 | tf_op jit(solution)/shard_map/ppermute | solution.py:162
  10.2 0.0 copy-done
  10.2 0.0 copy-start.1
  10.2 1.2 %copy-done.1 = bf16[1,320,1536]{2,1,0:T(8,128)(2,1)S(1)} copy-done((bf16[1,320,1536]{2,1,0:T(8,128)(2,1)S(1)}, bf16[1,320,1536]{2,1,0:T(8,128)(2,1)}, u32[]{:S(2)}) %copy-start.1) | copy-done | bytes 983064
  11.4 0.0 copy-start.3
  11.4 1.2 %copy-done.3 = bf16[1,320,1536]{2,1,0:T(8,128)(2,1)S(1)} copy-done((bf16[1,320,1536]{2,1,0:T(8,128)(2,1)S(1)}, bf16[1,320,1536]{2,1,0:T(8,128)(2,1)}, u32[]{:S(2)}) %copy-start.3) | copy-done | bytes 983064
  12.6 0.0 copy-start.2
  12.6 0.0 copy-start.4
  12.6 0.9 %partial_sums.3 = f32[4,72,384]{2,1,0:T(8,128)S(1)} custom-call(s32[2]{0:T(128)S(1)} %pad_add_fusion.2.where, bf16[2,24,320]{2,1,0:T(8,128)(2,1)S(1)} %get-tuple-element.23.own, bf16[1,2,24,320]{3,2,1,0:T(8,128)(2,1)S(1)} %bitcast.41, bf16[1,320,1536]{2,1,0:T(8,128)(2,1)S(1)} %copy-done, bf16[1,320,1536]{2,1,0:T(8,128)(2,1)S(1)} %copy-done.1, ...), custom_call_target="tpu_custom_call" | custom-call | flops 70778880 | bytes 1474560 | tf_op jit(solution)/shard_map/partial_sums/pallas_call | solution.py:186
  13.6 0.1 collective-permute-start.1
  13.6 0.1 pad_add_fusion.where
  13.7 0.1 copy-done.2
  13.8 0.3 copy-done.4
  14.1 0.9 %partial_sums.2 = f32[4,72,384]{2,1,0:T(8,128)S(1)} custom-call(s32[2]{0:T(128)S(1)} %pad_add_fusion.where, bf16[2,24,320]{2,1,0:T(8,128)(2,1)S(1)} %get-tuple-element.23.own, bf16[1,2,24,320]{3,2,1,0:T(8,128)(2,1)S(1)} %bitcast.42, bf16[1,320,1536]{2,1,0:T(8,128)(2,1)S(1)} %copy-done, bf16[1,320,1536]{2,1,0:T(8,128)(2,1)S(1)} %copy-done.2, ...), custom_call_target="tpu_custom_call" | custom-call | flops 70778880 | bytes 1474560 | tf_op jit(solution)/shard_map/partial_sums/pallas_call | solution.py:186
  15.0 0.0 copy-start.10
  15.1 0.0 copy-start.11
  15.1 0.5 collective-permute-done.1
  15.5 1.1 %add.15 = f32[4,72,384]{2,1,0:T(8,128)S(1)} add(f32[4,72,384]{2,1,0:T(8,128)S(1)} %partial_sums.2, f32[4,72,384]{2,1,0:T(8,128)} %collective-permute-done.1) | non-fusion elementwise | flops 110592 | bytes 1327104 | tf_op jit(solution)/shard_map/add | solution.py:201
  16.6 2.1 %collective-permute-start.2 = (f32[72,384]{1,0:T(8,128)S(1)}, f32[72,384]{1,0:T(8,128)S(1)}, u32[]{:S(2)}, u32[]{:S(2)}) collective-permute-start(f32[72,384]{1,0:T(8,128)S(1)} %get-tuple-element.19), channel_id=1, source_target_pairs={{0,4},{2,6},{4,0},{6,2},{8,12},{10,14},{12,8},{14,10},{16,20},{18,... | collective-permute-start | bytes 331784 | tf_op jit(solution)/shard_map/ppermute | solution.py:158
  18.8 1.6 %collective-permute-start.3 = (f32[72,384]{1,0:T(8,128)S(1)}, f32[72,384]{1,0:T(8,128)S(1)}, u32[]{:S(2)}, u32[]{:S(2)}) collective-permute-start(f32[72,384]{1,0:T(8,128)S(1)} %get-tuple-element.21), channel_id=1, source_target_pairs={{0,8},{2,10},{4,12},{6,14},{8,0},{10,2},{12,4},{14,6},{16,24},{18,... | collective-permute-start | bytes 331784 | tf_op jit(solution)/shard_map/ppermute | solution.py:158
  20.3 0.0 collective-permute-start.4
  20.3 1.8 %collective-permute-done.2 = f32[72,384]{1,0:T(8,128)S(1)} collective-permute-done((f32[72,384]{1,0:T(8,128)S(1)}, f32[72,384]{1,0:T(8,128)S(1)}, u32[]{:S(2)}, u32[]{:S(2)}) %collective-permute-start.2) | collective-permute-done | bytes 110624 | tf_op jit(solution)/shard_map/ppermute | solution.py:158
  22.1 2.6 %collective-permute-done.3 = f32[72,384]{1,0:T(8,128)S(1)} collective-permute-done((f32[72,384]{1,0:T(8,128)S(1)}, f32[72,384]{1,0:T(8,128)S(1)}, u32[]{:S(2)}, u32[]{:S(2)}) %collective-permute-start.3) | collective-permute-done | bytes 110624 | tf_op jit(solution)/shard_map/ppermute | solution.py:158
  24.7 1.3 %collective-permute-done.4 = f32[72,384]{1,0:T(8,128)S(1)} collective-permute-done((f32[72,384]{1,0:T(8,128)S(1)}, f32[72,384]{1,0:T(8,128)S(1)}, u32[]{:S(2)}, u32[]{:S(2)}) %collective-permute-start.4) | collective-permute-done | bytes 110624 | tf_op jit(solution)/shard_map/ppermute | solution.py:158
  26.0 2.7 %collective-permute-start.5 = (f32[72,384]{1,0:T(8,128)S(1)}, f32[72,384]{1,0:T(8,128)S(1)}, u32[]{:S(2)}, u32[]{:S(2)}) collective-permute-start(f32[72,384]{1,0:T(8,128)S(1)} %fusion.2.sums), channel_id=1, source_target_pairs={{0,16},{2,18},{4,20},{6,22},{8,24},{10,26},{12,28},{14,30},{16,0},... | collective-permute-start | bytes 331784 | tf_op jit(solution)/shard_map/ppermute | solution.py:158
  28.7 4.4 %collective-permute-done.5.recv = f32[72,384]{1,0:T(8,128)S(1)} collective-permute-done((f32[72,384]{1,0:T(8,128)S(1)}, f32[72,384]{1,0:T(8,128)S(1)}, u32[]{:S(2)}, u32[]{:S(2)}) %collective-permute-start.5) | collective-permute-done | bytes 110624 | tf_op jit(solution)/shard_map/ppermute | solution.py:158
  33.0 0.0 copy-done.10
  33.0 0.0 copy-done.11
  33.0 0.7 %hidden.1 = bf16[96,384]{1,0:T(8,128)(2,1)S(1)} custom-call(s32[2]{0:T(128)S(1)} %pad_add_fusion.1.order, s32[1]{0:T(128)} %bitcast.4.part, s32[2]{0:T(128)S(1)} %bitcast.47, f32[1,48]{1,0:T(1,128)S(1)} %copy-done.11, f32[72,384]{1,0:T(8,128)S(1)} %fusion.2.sums, f32[72,384]{1,0:T(8,128)S(1)} %collective-permute-done.5.recv), custom_call_target="tpu_custom_call" | custom-call | tf_op jit(solution)/shard_map/hidden/pallas_call | solution.py:208
  33.7 0.0 copy-start.8
  33.7 1.8 %collective-permute-start.6 = (bf16[96,384]{1,0:T(8,128)(2,1)S(1)}, bf16[96,384]{1,0:T(8,128)(2,1)S(1)}, u32[]{:S(2)}, u32[]{:S(2)}) collective-permute-start(bf16[96,384]{1,0:T(8,128)(2,1)S(1)} %hidden.1), channel_id=1, source_target_pairs={{0,4},{2,6},{4,0},{6,2},{8,12},{10,14},{12,8},{14,10},{16,20},{18,... | collective-permute-start | bytes 221192 | tf_op jit(solution)/shard_map/ppermute | solution.py:158
  35.5 0.7 %collective-permute-start.7 = (bf16[96,384]{1,0:T(8,128)(2,1)S(1)}, bf16[96,384]{1,0:T(8,128)(2,1)S(1)}, u32[]{:S(2)}, u32[]{:S(2)}) collective-permute-start(bf16[96,384]{1,0:T(8,128)(2,1)S(1)} %hidden.1), channel_id=1, source_target_pairs={{0,8},{2,10},{4,12},{6,14},{8,0},{10,2},{12,4},{14,6},{16,24},{18,... | collective-permute-start | bytes 221192 | tf_op jit(solution)/shard_map/ppermute | solution.py:158
  36.2 1.1 %collective-permute-start.8 = (bf16[96,384]{1,0:T(8,128)(2,1)S(1)}, bf16[96,384]{1,0:T(8,128)(2,1)S(1)}, u32[]{:S(2)}, u32[]{:S(2)}) collective-permute-start(bf16[96,384]{1,0:T(8,128)(2,1)S(1)} %hidden.1), channel_id=1, source_target_pairs={{0,12},{2,14},{4,8},{6,10},{8,4},{10,6},{12,0},{14,2},{16,28},{18,... | collective-permute-start | bytes 221192 | tf_op jit(solution)/shard_map/ppermute | solution.py:158
  37.3 0.9 %collective-permute-done.6 = bf16[96,384]{1,0:T(8,128)(2,1)S(1)} collective-permute-done((bf16[96,384]{1,0:T(8,128)(2,1)S(1)}, bf16[96,384]{1,0:T(8,128)(2,1)S(1)}, u32[]{:S(2)}, u32[]{:S(2)}) %collective-permute-start.6) | collective-permute-done | bytes 73760 | tf_op jit(solution)/shard_map/ppermute | solution.py:158
  38.2 1.7 %collective-permute-done.7 = bf16[96,384]{1,0:T(8,128)(2,1)S(1)} collective-permute-done((bf16[96,384]{1,0:T(8,128)(2,1)S(1)}, bf16[96,384]{1,0:T(8,128)(2,1)S(1)}, u32[]{:S(2)}, u32[]{:S(2)}) %collective-permute-start.7) | collective-permute-done | bytes 73760 | tf_op jit(solution)/shard_map/ppermute | solution.py:158
  39.8 1.6 %collective-permute-done.8 = bf16[96,384]{1,0:T(8,128)(2,1)S(1)} collective-permute-done((bf16[96,384]{1,0:T(8,128)(2,1)S(1)}, bf16[96,384]{1,0:T(8,128)(2,1)S(1)}, u32[]{:S(2)}, u32[]{:S(2)}) %collective-permute-start.8) | collective-permute-done | bytes 73760 | tf_op jit(solution)/shard_map/ppermute | solution.py:158
  41.5 0.1 collective-permute-start.9
  41.5 1.6 %collective-permute-done.9.far = bf16[4,96,384]{2,1,0:T(8,128)(2,1)S(1)} collective-permute-done((bf16[4,96,384]{2,1,0:T(8,128)(2,1)S(1)}, bf16[4,96,384]{2,1,0:T(8,128)(2,1)S(1)}, u32[]{:S(2)}, u32[]{:S(2)}) %collective-permute-start.9) | collective-permute-done | bytes 294944 | tf_op jit(solution)/shard_map/ppermute | solution.py:158
  43.1 1.2 %slot_grad.1 = (bf16[2,24,320]{2,1,0:T(8,128)(2,1)S(1)}, f32[1,384]{1,0:T(1,128)S(1)}) custom-call(s32[2]{0:T(128)S(1)} %pad_add_fusion.where, bf16[4,96,384]{2,1,0:T(8,128)(2,1)S(1)} %pad_maximum_fusion.near, bf16[4,96,384]{2,1,0:T(8,128)(2,1)S(1)} %collective-permute-done.9.far, bf16[1,320,1536]{2,1,0:T(8,128)(2,1)S(1)} %copy-done, ...), custom_call_target="tpu_custom_call" | custom-call | tf_op jit(solution)/shard_map/slot_grad/pallas_call | solution.py:219
  44.4 1.6 %collective-permute-start.10 = (bf16[24,320]{1,0:T(8,128)(2,1)S(1)}, bf16[24,320]{1,0:T(8,128)(2,1)S(1)}, u32[]{:S(2)}, u32[]{:S(2)}) collective-permute-start(bf16[24,320]{1,0:T(8,128)(2,1)S(1)} %get-tuple-element.24), channel_id=1, source_target_pairs={{0,1},{1,0},{2,3},{3,2},{4,5},{5,4},{6,7},{7,6},{8,9},{9,8},{10,11... | collective-permute-start | bytes 46088 | tf_op jit(solution)/shard_map/ppermute | solution.py:162
  45.9 0.6 %constant_dynamic-slice_fusion = f32[1,3]{1,0:T(1,128)} fusion(f32[1,384]{1,0:T(1,128)S(1)} %get-tuple-element.18, s32[]{:T(128)S(6)} %select_n.3), kind=kLoop, calls=%fused_computation.15 | loop fusion | bytes 28 | tf_op jit(solution)/shard_map/dynamic_slice | solution.py:265
  46.5 4.1 %weight_grads.1 = (f32[1,320,1536]{2,1,0:T(8,128)}, f32[1,320,1536]{2,1,0:T(8,128)}, f32[1,320,1536]{2,1,0:T(8,128)}) custom-call(s32[2]{0:T(128)S(1)} %pad_add_fusion.where, bf16[2,24,320]{2,1,0:T(8,128)(2,1)S(1)} %get-tuple-element.23.own, bf16[1,2,24,320]{3,2,1,0:T(8,128)(2,1)S(1)} %bitcast.43, bf16[4,96,384]{2,1,0:T(8,128)(2,1)S(1)} %pad_maximum_fusion.near, ...), custom_call_target="tpu_custom_call" | custom-call | flops 141557760 | bytes 5898240 | tf_op jit(solution)/shard_map/weight_grads/pallas_call | solution.py:240
  50.6 0.0 collective-permute-done.10
  50.6 0.0 copy-done.8
  50.6 1.2 %token_grad.1 = bf16[320,1024]{1,0:T(8,128)(2,1)} custom-call(bf16[24,320]{1,0:T(8,128)(2,1)S(1)} %get-tuple-element.25.own, bf16[1,24,320]{2,1,0:T(8,128)(2,1)S(1)} %bitcast.45, bf16[48,1024]{1,0:T(8,128)(2,1)S(1)} %copy-done.8), custom_call_target="tpu_custom_call" | custom-call | tf_op jit(solution)/shard_map/token_grad/pallas_call | solution.py:256
  (5 shorter events, 0.1 us)
Async XLA Ops:
  0.6 9.6 %copy-start = (bf16[1,320,1536]{2,1,0:T(8,128)(2,1)S(1)}, bf16[1,320,1536]{2,1,0:T(8,128)(2,1)}, u32[]{:S(2)}) copy-start(bf16[1,320,1536]{2,1,0:T(8,128)(2,1)} %w_gate.5) | copy-start | bytes 2949124
  0.7 1.2 %copy-start.5 = (bf16[1024,320]{0,1:T(8,128)(2,1)S(1)}, bf16[1024,320]{0,1:T(8,128)(2,1)}, u32[]{:S(2)}) copy-start(bf16[1024,320]{0,1:T(8,128)(2,1)} %param.8) | copy-start | bytes 1966084
  1.9 1.1 %copy-start.6 = (bf16[1024,320]{0,1:T(8,128)(2,1)S(1)}, bf16[1024,320]{0,1:T(8,128)(2,1)}, u32[]{:S(2)}) copy-start(bf16[1024,320]{0,1:T(8,128)(2,1)} %param.9) | copy-start | bytes 1966084
  3.0 0.7 %copy-start.9 = (s32[1,2,24]{2,1,0:T(2,128)S(1)}, s32[1,2,24]{2,1,0:T(2,128)}, u32[]{:S(2)}) copy-start(s32[1,2,24]{2,1,0:T(2,128)} %param.10) | copy-start | bytes 580
  4.7 0.6 %copy-start.7 = (bf16[48,1024]{1,0:T(8,128)(2,1)}, bf16[48,1024]{1,0:T(8,128)(2,1)S(1)}, u32[]{:S(2)}) copy-start(bf16[48,1024]{1,0:T(8,128)(2,1)S(1)} %get-tuple-element.14.onehot) | copy-start | bytes 294916
  5.3 4.9 %collective-permute-start = (bf16[2,24,320]{2,1,0:T(8,128)(2,1)S(1)}, bf16[2,24,320]{2,1,0:T(8,128)(2,1)S(1)}, u32[]{:S(2)}, u32[]{:S(2)}) collective-permute-start(bf16[2,24,320]{2,1,0:T(8,128)(2,1)S(1)} %get-tuple-element.22), channel_id=1, source_target_pairs={{0,1},{1,0},{2,3},{3,2},{4,5},{5,4},{6,7},{7,6},{8,9},{9,8},{10,11... | collective-permute-start | bytes 92168 | tf_op jit(solution)/shard_map/ppermute | solution.py:162
  10.2 1.2 %copy-start.1 = (bf16[1,320,1536]{2,1,0:T(8,128)(2,1)S(1)}, bf16[1,320,1536]{2,1,0:T(8,128)(2,1)}, u32[]{:S(2)}) copy-start(bf16[1,320,1536]{2,1,0:T(8,128)(2,1)} %w_up.5) | copy-start | bytes 2949124
  11.4 1.2 %copy-start.3 = (bf16[1,320,1536]{2,1,0:T(8,128)(2,1)S(1)}, bf16[1,320,1536]{2,1,0:T(8,128)(2,1)}, u32[]{:S(2)}) copy-start(bf16[1,320,1536]{2,1,0:T(8,128)(2,1)} %w_down.3) | copy-start | bytes 2949124
  12.6 1.2 %copy-start.2 = (bf16[1,320,1536]{2,1,0:T(8,128)(2,1)S(1)}, bf16[1,320,1536]{2,1,0:T(8,128)(2,1)}, u32[]{:S(2)}) copy-start(bf16[1,320,1536]{2,1,0:T(8,128)(2,1)} %w_up.5) | copy-start | bytes 2949124
  12.6 1.5 %copy-start.4 = (bf16[1,320,1536]{2,1,0:T(8,128)(2,1)S(1)}, bf16[1,320,1536]{2,1,0:T(8,128)(2,1)}, u32[]{:S(2)}) copy-start(bf16[1,320,1536]{2,1,0:T(8,128)(2,1)} %w_down.3) | copy-start | bytes 2949124
  13.6 2.0 %collective-permute-start.1 = (f32[4,72,384]{2,1,0:T(8,128)S(1)}, f32[4,72,384]{2,1,0:T(8,128)}, u32[]{:S(2)}, u32[]{:S(2)}) collective-permute-start(f32[4,72,384]{2,1,0:T(8,128)S(1)} %partial_sums.3), channel_id=1, source_target_pairs={{0,2},{2,0},{4,6},{6,4},{8,10},{10,8},{12,14},{14,12},{16,18},{18,... | collective-permute-start | bytes 1327112 | tf_op jit(solution)/shard_map/ppermute | solution.py:158
  15.0 18.0 %copy-start.10 = (s32[1,2]{1,0:T(1,128)S(1)}, s32[1,2]{1,0:T(1,128)}, u32[]{:S(2)}) copy-start(s32[1,2]{1,0:T(1,128)} %param.11) | copy-start | bytes 28
  15.1 18.0 %copy-start.11 = (f32[1,48]{1,0:T(1,128)S(1)}, f32[1,48]{1,0:T(1,128)}, u32[]{:S(2)}) copy-start(f32[1,48]{1,0:T(1,128)} %prob.1) | copy-start | bytes 580
  16.6 5.5 %collective-permute-start.2 = (f32[72,384]{1,0:T(8,128)S(1)}, f32[72,384]{1,0:T(8,128)S(1)}, u32[]{:S(2)}, u32[]{:S(2)}) collective-permute-start(f32[72,384]{1,0:T(8,128)S(1)} %get-tuple-element.19), channel_id=1, source_target_pairs={{0,4},{2,6},{4,0},{6,2},{8,12},{10,14},{12,8},{14,10},{16,20},{18,... | collective-permute-start | bytes 331784 | tf_op jit(solution)/shard_map/ppermute | solution.py:158
  18.8 5.9 %collective-permute-start.3 = (f32[72,384]{1,0:T(8,128)S(1)}, f32[72,384]{1,0:T(8,128)S(1)}, u32[]{:S(2)}, u32[]{:S(2)}) collective-permute-start(f32[72,384]{1,0:T(8,128)S(1)} %get-tuple-element.21), channel_id=1, source_target_pairs={{0,8},{2,10},{4,12},{6,14},{8,0},{10,2},{12,4},{14,6},{16,24},{18,... | collective-permute-start | bytes 331784 | tf_op jit(solution)/shard_map/ppermute | solution.py:158
  20.3 5.6 %collective-permute-start.4 = (f32[72,384]{1,0:T(8,128)S(1)}, f32[72,384]{1,0:T(8,128)S(1)}, u32[]{:S(2)}, u32[]{:S(2)}) collective-permute-start(f32[72,384]{1,0:T(8,128)S(1)} %get-tuple-element.20), channel_id=1, source_target_pairs={{0,12},{2,14},{4,8},{6,10},{8,4},{10,6},{12,0},{14,2},{16,28},{18,... | collective-permute-start | bytes 331784 | tf_op jit(solution)/shard_map/ppermute | solution.py:158
  26.0 7.0 %collective-permute-start.5 = (f32[72,384]{1,0:T(8,128)S(1)}, f32[72,384]{1,0:T(8,128)S(1)}, u32[]{:S(2)}, u32[]{:S(2)}) collective-permute-start(f32[72,384]{1,0:T(8,128)S(1)} %fusion.2.sums), channel_id=1, source_target_pairs={{0,16},{2,18},{4,20},{6,22},{8,24},{10,26},{12,28},{14,30},{16,0},... | collective-permute-start | bytes 331784 | tf_op jit(solution)/shard_map/ppermute | solution.py:158
  33.7 16.9 %copy-start.8 = (bf16[48,1024]{1,0:T(8,128)(2,1)S(1)}, bf16[48,1024]{1,0:T(8,128)(2,1)}, u32[]{:S(2)}) copy-start(bf16[48,1024]{1,0:T(8,128)(2,1)} %copy-done.7) | copy-start | bytes 294916
  33.7 4.4 %collective-permute-start.6 = (bf16[96,384]{1,0:T(8,128)(2,1)S(1)}, bf16[96,384]{1,0:T(8,128)(2,1)S(1)}, u32[]{:S(2)}, u32[]{:S(2)}) collective-permute-start(bf16[96,384]{1,0:T(8,128)(2,1)S(1)} %hidden.1), channel_id=1, source_target_pairs={{0,4},{2,6},{4,0},{6,2},{8,12},{10,14},{12,8},{14,10},{16,20},{18,... | collective-permute-start | bytes 221192 | tf_op jit(solution)/shard_map/ppermute | solution.py:158
  35.5 4.4 %collective-permute-start.7 = (bf16[96,384]{1,0:T(8,128)(2,1)S(1)}, bf16[96,384]{1,0:T(8,128)(2,1)S(1)}, u32[]{:S(2)}, u32[]{:S(2)}) collective-permute-start(bf16[96,384]{1,0:T(8,128)(2,1)S(1)} %hidden.1), channel_id=1, source_target_pairs={{0,8},{2,10},{4,12},{6,14},{8,0},{10,2},{12,4},{14,6},{16,24},{18,... | collective-permute-start | bytes 221192 | tf_op jit(solution)/shard_map/ppermute | solution.py:158
  36.2 5.3 %collective-permute-start.8 = (bf16[96,384]{1,0:T(8,128)(2,1)S(1)}, bf16[96,384]{1,0:T(8,128)(2,1)S(1)}, u32[]{:S(2)}, u32[]{:S(2)}) collective-permute-start(bf16[96,384]{1,0:T(8,128)(2,1)S(1)} %hidden.1), channel_id=1, source_target_pairs={{0,12},{2,14},{4,8},{6,10},{8,4},{10,6},{12,0},{14,2},{16,28},{18,... | collective-permute-start | bytes 221192 | tf_op jit(solution)/shard_map/ppermute | solution.py:158
  41.5 1.6 %collective-permute-start.9 = (bf16[4,96,384]{2,1,0:T(8,128)(2,1)S(1)}, bf16[4,96,384]{2,1,0:T(8,128)(2,1)S(1)}, u32[]{:S(2)}, u32[]{:S(2)}) collective-permute-start(bf16[4,96,384]{2,1,0:T(8,128)(2,1)S(1)} %pad_maximum_fusion.near), channel_id=1, source_target_pairs={{0,2},{2,0},{4,6},{6,4},{8,10},{10,8},{12,14},{14,12},{16,18},{18,... | collective-permute-start | bytes 884744 | tf_op jit(solution)/shard_map/ppermute | solution.py:158
  44.4 6.2 %collective-permute-start.10 = (bf16[24,320]{1,0:T(8,128)(2,1)S(1)}, bf16[24,320]{1,0:T(8,128)(2,1)S(1)}, u32[]{:S(2)}, u32[]{:S(2)}) collective-permute-start(bf16[24,320]{1,0:T(8,128)(2,1)S(1)} %get-tuple-element.24), channel_id=1, source_target_pairs={{0,1},{1,0},{2,3},{3,2},{4,5},{5,4},{6,7},{7,6},{8,9},{9,8},{10,11... | collective-permute-start | bytes 46088 | tf_op jit(solution)/shard_map/ppermute | solution.py:162

commit v2 on v1

v2 whole, which is shorter than its diff:
```python
import functools

import jax
import jax.numpy as jnp
from jax import lax
from jax.experimental import pallas as pl
from jax.experimental.pallas import tpu as pltpu
from jax.sharding import PartitionSpec as P

BF16 = jnp.bfloat16
F32 = jnp.float32
VMEM = pl.BlockSpec(memory_space=pltpu.VMEM)
HBM = pl.BlockSpec(memory_space=pltpu.HBM)
SMEM = pl.BlockSpec(memory_space=pltpu.SMEM)
PARAMS = pltpu.CompilerParams(vmem_limit_bytes=40 * 2**20)


def in_hbm(x):
    return pltpu.with_memory_space_constraint(x, pltpu.HBM)


def dot(a, b, contract):
    return lax.dot_general(a, b, ((contract[0:1], contract[1:2]), ((), ())), preferred_element_type=F32)


def place(side, jy, width):
    me = lax.axis_index("fsdp")
    half = (me & 1) ^ side
    return pl.multiple_of((half * 2 + (((me >> 1) & 1) ^ jy)) * width, 128)


def row_part():
    return (lax.axis_index("fsdp") >> 2) & 1


def first_expert(experts):
    return lax.axis_index("expert") if experts == 2 else 0


def gather_kernel(slot_rows_hbm, tokens_hbm, grads_hbm, rows_out, onehot_out, slot_rows, tokens_t, grads_t, onehot_f, sems):
    copies = [
        pltpu.make_async_copy(source, to, sems.at[i])
        for i, (source, to) in enumerate(((slot_rows_hbm, slot_rows), (tokens_hbm, tokens_t), (grads_hbm, grads_t)))
    ]
    for copy in copies:
        copy.start()
    experts, slots = slot_rows.shape
    count = tokens_t.shape[1]
    first = first_expert(experts)
    lane = lax.broadcasted_iota(jnp.int32, (8, count), 1)
    sub = lax.broadcasted_iota(jnp.int32, (8, count), 0)
    copies[0].wait()
    for j in range(experts):
        expert = lax.rem(first + j, experts)
        for base in range(0, slots, 8):
            picked = jnp.zeros((8, count), jnp.int32)
            for r in range(8):
                picked = jnp.where(sub == r, slot_rows[expert, base + r], picked)
            onehot_f[pl.ds(j * slots + base, 8), :] = (picked == lane).astype(F32)
    onehot = onehot_f[...].astype(BF16)
    onehot_out[...] = onehot
    for kind, source in enumerate((tokens_t, grads_t)):
        copies[1 + kind].wait()
        rows = dot(onehot, source[...], (1, 1))
        for j in range(experts):
            rows_out[j, kind] = rows[j * slots : (j + 1) * slots].astype(BF16)


def load_kernel(after, w_gate, w_up, w_down, gate_out, up_out, down_out, sems):
    del after
    copies = [
        pltpu.make_async_copy(w.at[0], to, sems.at[i])
        for i, (w, to) in enumerate(((w_gate, gate_out), (w_up, up_out), (w_down, down_out)))
    ]
    for copy in copies:
        copy.start()
    for copy in copies:
        copy.wait()


def stacked_rows(own, recv, kind):
    blocks = [own[kind]] + [recv[j, kind] for j in range(recv.shape[0])]
    return jnp.concatenate([block.astype(F32) for block in blocks], axis=0)


def partial_kernel(side, own, recv, w_gate, w_up, w_down, out, *turned):
    tok, grad = stacked_rows(own, recv, 0), stacked_rows(own, recv, 1)
    chunk_rows, width = out.shape[1] // 3, out.shape[2]
    part0 = row_part()
    for to, x in zip(turned, (tok, grad)):
        padded = to.shape[1] // 2
        zeros = jnp.zeros((padded - chunk_rows, x.shape[1]), F32)
        low, high = x[:chunk_rows], x[chunk_rows:]
        near, far = jnp.where(part0 == 0, low, high), jnp.where(part0 == 0, high, low)
        to[...] = jnp.concatenate([near, zeros, far, zeros], axis=0).T.astype(BF16)
    tok, grad = tok.astype(BF16), grad.astype(BF16)
    for jy in range(2):
        at = pl.ds(place(side, jy, width), width)
        for q, (x, w) in enumerate(((tok, w_gate), (tok, w_up), (grad, w_down))):
            sums = dot(x, w[:, at], (1, 0))
            for part in range(2):
                chunk = (part0 ^ part) * 2 + jy
                out[chunk, pl.ds(q * chunk_rows, chunk_rows), :] = sums[part * chunk_rows : (part + 1) * chunk_rows]


def add_kernel(kept, arrived, *outs):
    for j, out in enumerate(outs):
        out[...] = kept[j] + arrived[j]


def hidden_kernel(counts, prob, sums, recv, out):
    experts = counts.shape[0]
    slots = prob.shape[1] // experts
    total_rows = prob.shape[1]
    rows = sums.shape[0] // 3
    padded = out.shape[0] // 3
    width = sums.shape[1]
    total = sums[...] + recv[...]
    gate, up, down = total[:rows], total[rows : 2 * rows], total[2 * rows :]
    row = lax.broadcasted_iota(jnp.int32, (rows, 1), 0) + row_part() * rows
    slot = row
    home = jnp.zeros((rows, 1), jnp.int32)
    first = first_expert(experts)
    live_count = jnp.zeros((rows, 1), jnp.int32)
    for j in range(experts):
        inside = (row >= j * slots) & (row < (j + 1) * slots)
        slot = jnp.where(inside, row - j * slots, slot)
        source = lax.rem(first + j, experts)
        home = jnp.where(inside, source * slots + row - j * slots, home)
        live_count = jnp.where(inside, counts[source], live_count)
    live = (slot < live_count).astype(F32)
    diagonal = lax.broadcasted_iota(jnp.int32, (rows, total_rows), 1) == home
    row_prob = jnp.sum(jnp.where(diagonal, prob[...], 0.0), axis=1, keepdims=True)
    scale = row_prob * live
    sigmoid = jax.nn.sigmoid(gate)
    silu = gate * sigmoid
    hidden = (silu * up).astype(BF16).astype(F32)
    hidden_grad = down * scale
    prob_grad = live * jnp.sum(hidden * down, axis=1, keepdims=True)
    prob_row = jnp.sum(jnp.where(diagonal, prob_grad, 0.0), axis=0, keepdims=True)
    high = prob_row.astype(BF16).astype(F32)
    tail = jnp.concatenate([high, prob_row - high, jnp.zeros((padded - rows - 2, total_rows), F32)], axis=0)
    tail = jnp.concatenate([tail, jnp.zeros((padded - rows, width - total_rows), F32)], axis=1)
    zeros = jnp.zeros((padded - rows, width), F32)
    gate_act_grad = hidden_grad * up * sigmoid * (1.0 + gate * (1.0 - sigmoid))
    for q, (x, end) in enumerate(((hidden * scale, tail), (gate_act_grad, zeros), (hidden_grad * silu, zeros))):
        out[pl.ds(q * padded, padded), :] = jnp.concatenate([x, end], axis=0).astype(BF16)


def both_parts(a, b, q):
    padded = a.shape[0] // 3
    return jnp.concatenate([a[pl.ds(q * padded, padded), :], b[pl.ds(q * padded, padded), :]], axis=0)


def slot_part(a, b, w_gate, w_up, column):
    at = pl.ds(column, a.shape[1])
    return dot(both_parts(a, b, 1), w_gate[:, at], (1, 1)) + dot(both_parts(a, b, 2), w_up[:, at], (1, 1))


def near_slot_kernel(near0, near1, near2, near3, w_gate, w_up, out):
    width = near0.shape[1]
    out[...] = slot_part(near0, near2, w_gate, w_up, place(0, 0, width)) + slot_part(
        near1, near3, w_gate, w_up, place(0, 1, width)
    )


def slot_kernel(before, far, w_gate, w_up, out):
    width = far.shape[2]
    padded = far.shape[1] // 3
    experts, slots, _ = out.shape
    total = before[...]
    for jy in range(2):
        total += slot_part(far.at[jy], far.at[2 + jy], w_gate, w_up, place(1, jy, width))
    for part in range(2):
        for j in range(experts // 2):
            start = part * padded + j * slots
            out[(row_part() ^ part) * (experts // 2) + j] = total[start : start + slots].astype(BF16)


def weight_grad_kernel(chunk_rows, near0, near1, near2, near3, far, tok_t, grad_t, gate_grad, up_grad, down_grad, prob_out, held, sems):
    width = far.shape[2]
    padded = far.shape[1] // 3
    pieces = [(near0, near2), (near1, near3), (far.at[0], far.at[2]), (far.at[1], far.at[3])]
    copies = []
    for i, (a, b) in enumerate(pieces):
        for q, x, out in ((0, grad_t, down_grad), (1, tok_t, gate_grad), (2, tok_t, up_grad)):
            n = len(copies)
            held[n] = dot(x[...], both_parts(a, b, q), (1, 0))
            to = out.at[0, :, pl.ds(place(i // 2, i % 2, width), width)]
            copy = pltpu.make_async_copy(held.at[n], to, sems.at[n])
            copy.start()
            copies.append(copy)
    tail = jnp.zeros((16, width), F32)
    for a, b in pieces:
        tail += a[pl.ds(padded - 16, 16), :].astype(F32) + b[pl.ds(padded - 16, 16), :].astype(F32)
    start = 16 - (padded - chunk_rows)
    prob = jnp.broadcast_to(tail[start : start + 1] + tail[start + 1 : start + 2], (8, width))
    share = prob_out.shape[1]
    shift = lax.rem(width - lax.axis_index("fsdp") * share, width)
    prob_out[...] = pltpu.roll(prob, shift, 1)[:1, :share]
    for copy in copies:
        copy.wait()


def token_grad_kernel(own, recv, onehot, out):
    blocks = [own[...]] + [recv[j] for j in range(recv.shape[0])]
    slot_grad = jnp.concatenate([block.astype(F32) for block in blocks], axis=0).astype(BF16)
    out[...] = dot(slot_grad, onehot[...], (0, 0)).astype(BF16)


def local(tokens, out_grad, slot_rows, expert_counts, route_prob, w_gate, w_up, w_down):
    fsdp, experts = lax.axis_size("fsdp"), lax.axis_size("expert")
    steps = fsdp.bit_length() - 1
    token_count, features = tokens.shape
    _, _, slots = slot_rows.shape
    rows = experts * slots
    hidden = w_gate.shape[2]
    half, quarter = hidden // 2, hidden // 4
    def swap(x, mask):
        return lax.ppermute(x, "fsdp", [(i, i ^ mask) for i in range(fsdp)])

    def to_expert(x):
        if experts == 2:
            return x[0], lax.ppermute(x[1], "expert", [(0, 1), (1, 0)])[None]
        moved = lax.all_to_all(x, "expert", split_axis=0, concat_axis=0, tiled=True)
        return moved[0], moved[1:]

    rows_out, onehot = pl.pallas_call(
        gather_kernel,
        out_shape=(
            jax.ShapeDtypeStruct((experts, 2, slots, features), BF16),
            jax.ShapeDtypeStruct((rows, token_count), BF16),
        ),
        in_specs=[HBM] * 3,
        out_specs=(VMEM, VMEM),
        scratch_shapes=[
            pltpu.SMEM((experts, slots), jnp.int32),
            pltpu.VMEM((features, token_count), BF16),
            pltpu.VMEM((features, token_count), BF16),
            pltpu.VMEM((rows, token_count), F32),
            pltpu.SemaphoreType.DMA((3,)),
        ],
        compiler_params=PARAMS,
        name="gather_rows",
    )(*(in_hbm(x) for x in (slot_rows[0], tokens.T, out_grad.T)))
    own, recv = to_expert(rows_out)
    weights = pl.pallas_call(
        load_kernel,
        out_shape=(jax.ShapeDtypeStruct((features, hidden), BF16),) * 3,
        in_specs=[VMEM] + [HBM] * 3,
        out_specs=(VMEM,) * 3,
        scratch_shapes=[pltpu.SemaphoreType.DMA((3,))],
        compiler_params=PARAMS,
        cost_estimate=pl.CostEstimate(flops=0, bytes_accessed=6 * features * hidden, transcendentals=0),
        name="load_weights",
    )(own, *(in_hbm(w) for w in (w_gate, w_up, w_down)))
    padded = (rows // 2 + 2 + 15) // 16 * 16

    def partial(side, turned):
        turned_shape = jax.ShapeDtypeStruct((features, 2 * padded), BF16)
        shapes = (jax.ShapeDtypeStruct((4, 3 * rows // 2, quarter), F32),) + (turned_shape,) * turned
        return pl.pallas_call(
            functools.partial(partial_kernel, side),
            out_shape=shapes,
            in_specs=[VMEM] * 5,
            out_specs=(VMEM,) * len(shapes),
            compiler_params=PARAMS,
            cost_estimate=pl.CostEstimate(
                flops=6 * rows * features * half, bytes_accessed=3 * features * half * 2, transcendentals=0
            ),
            name="partial_sums",
        )(own, recv, *weights)

    arrived = swap(partial(1, 0)[0], 1)
    kept, tok_t, grad_t = partial(0, 2)
    chunk_shape = jax.ShapeDtypeStruct((3 * rows // 2, quarter), F32)
    chunks = pl.pallas_call(
        add_kernel,
        out_shape=(chunk_shape,) * 4,
        in_specs=[VMEM] * 2,
        out_specs=(VMEM,) * 4,
        compiler_params=PARAMS,
        name="add",
    )(kept, arrived)
    total = chunks[0] + swap(chunks[1], 2) + swap(chunks[2], 4) + swap(chunks[3], 6)
    for b in range(3, steps):
        arrived = swap(total, 1 << b)
        if b < steps - 1:
            total = total + arrived
    acts = pl.pallas_call(
        hidden_kernel,
        out_shape=jax.ShapeDtypeStruct((3 * padded, quarter), BF16),
        in_specs=[SMEM, VMEM, VMEM, VMEM],
        out_specs=VMEM,
        compiler_params=PARAMS,
        name="hidden",
    )(expert_counts[0], route_prob, total, arrived)
    near = [acts, swap(acts, 2), swap(acts, 4), swap(acts, 6)]
    far = swap(jnp.stack(near), 1)

    near_slot = pl.pallas_call(
        near_slot_kernel,
        out_shape=jax.ShapeDtypeStruct((2 * padded, features), F32),
        in_specs=[VMEM] * 6,
        out_specs=VMEM,
        compiler_params=PARAMS,
        cost_estimate=pl.CostEstimate(
            flops=2 * rows * features * hidden, bytes_accessed=2 * features * hidden, transcendentals=0
        ),
        name="near_slot",
    )(*near, weights[0], weights[1])
    slot_grad = pl.pallas_call(
        slot_kernel,
        out_shape=jax.ShapeDtypeStruct((experts, slots, features), BF16),
        in_specs=[VMEM] * 4,
        out_specs=VMEM,
        compiler_params=PARAMS,
        name="slot_grad",
    )(near_slot, far, weights[0], weights[1])
    slot_own, slot_recv = to_expert(slot_grad)
    grad_shape = jax.ShapeDtypeStruct((1, features, hidden), F32)
    gate_grad, up_grad, down_grad, prob_grad = pl.pallas_call(
        functools.partial(weight_grad_kernel, rows // 2),
        out_shape=(grad_shape,) * 3 + (jax.ShapeDtypeStruct((1, rows // fsdp), F32),),
        in_specs=[VMEM] * 7,
        out_specs=(HBM,) * 3 + (VMEM,),
        scratch_shapes=[pltpu.VMEM((12, features, quarter), F32), pltpu.SemaphoreType.DMA((12,))],
        compiler_params=PARAMS,
        cost_estimate=pl.CostEstimate(
            flops=6 * rows * features * hidden, bytes_accessed=12 * features * hidden, transcendentals=0
        ),
        name="weight_grads",
    )(*near, far, tok_t, grad_t)

    token_grad = pl.pallas_call(
        token_grad_kernel,
        out_shape=jax.ShapeDtypeStruct((features, token_count), BF16),
        in_specs=[VMEM] * 3,
        out_specs=VMEM,
        compiler_params=PARAMS,
        name="token_grad",
    )(slot_own, slot_recv, onehot).T
    return (token_grad, gate_grad, up_grad, down_grad, prob_grad)


def solution(mesh):
    return jax.shard_map(
        local,
        mesh=mesh,
        in_specs=(
            P("expert", "fsdp"),
            P("expert", "fsdp"),
            P("expert", None, None),
            P("expert", None),
            P("expert", None),
            P("expert", "fsdp", None),
            P("expert", "fsdp", None),
            P("expert", "fsdp", None),
        ),
        out_specs=(
            P("expert", "fsdp"),
            P("expert", "fsdp", None),
            P("expert", "fsdp", None),
            P("expert", "fsdp", None),
            P("expert", "fsdp"),
        ),
        check_vma=False,
    )
```

time: 52.1 us -> 43 us (0.83)
  local copies, waits for them, and re-layouts: 6.99 us -> 0.03 us
  waiting for transfers between devices: 18 us -> 16.6 us
  other arithmetic: 1.37 us -> 0.08 us
  Pallas kernels: 10.1 us -> 10.7 us
    unnamed x24 -> x4, local copies, waits for them, and re-layouts: 6.37 us -> 0.01 us
    ppermute x2, waiting for transfers between devices: 1.86 us -> 0.12 us  [to_expert(): return (x[0], lax.ppermute(x[1], 'expert', [(0, 1), (1, 0)])[None])]
    add x2 -> x1, other arithmetic: 1.1 us -> 0.03 us  [local(): chunks[0] + swap(chunks[1], 2) + swap(chunks[2], 4) + swap(chunks[3], 6)]
    pallas_call x1, Pallas kernels: 1.05 us -> 1.93 us  [local(): pl.pallas_call(gather_kernel, out_shape=(jax.ShapeDtypeStruct((experts, 2...]
    dynamic_slice x1 -> x0, local copies, waits for them, and re-layouts: 0.58 us -> none  [local(): prob_grad = lax.dynamic_slice_in_dim(prob_row, me * share, share, axis=1)]
    pallas_call x4 -> x7, Pallas kernels: 7.16 us -> 6.9 us  [the longest x1 3.37 us: local(): pl.pallas_call(functools.partial(weight_grad_kernel, rows // 2), out_shap...]
  transfers between devices with their start and end apart: 11 -> 11, of which waited for: 10 -> 10; matrix products, arithmetic and copies ran while one was open for 1% -> 0% of each run, Pallas kernels for 10% -> 14%
where the time goes in v2:
time: 43 us; the launch traced here: 42.8 us
  waiting for transfers between devices  16.6 us (39%)
  starting transfers between devices  14.6 us (34%)
  Pallas kernels  10.7 us (25%)
  between operations  0.75 us (2%)
    ppermute x9, waiting for transfers between devices, swap(): return lax.ppermute(x, 'fsdp', [(i, i ^ mask) for i in range(fsdp)])  16.5 us
    ppermute x9, starting transfers between devices, swap(): return lax.ppermute(x, 'fsdp', [(i, i ^ mask) for i in range(fsdp)])  10 us
    ppermute x2, starting transfers between devices, to_expert(): return (x[0], lax.ppermute(x[1], 'expert', [(0, 1), (1, 0)])[None])  4.56 us
    pallas_call x1, Pallas kernels, local(): pl.pallas_call(functools.partial(weight_grad_kernel, rows // 2), out_shap...  3.37 us
    pallas_call x1, Pallas kernels, local(): pl.pallas_call(gather_kernel, out_shape=(jax.ShapeDtypeStruct((experts, 2...  1.93 us
    pallas_call x1, Pallas kernels, local(): pl.pallas_call(load_kernel, out_shape=(jax.ShapeDtypeStruct((features, hi...  1.82 us
    pallas_call x1, Pallas kernels, local(): pl.pallas_call(token_grad_kernel, out_shape=jax.ShapeDtypeStruct((feature...  1.19 us
  transfers between devices with their start and end apart: 11, of which 10 were waited for; matrix products, arithmetic and copies ran while one was open for 0% of the time, Pallas kernels for 14%

profile of v2, /device:TPU:0, one launch (start us, length us, event | category | flops | bytes accessed | tf_op | source)
XLA Modules:
  0.0 42.8 jit_solution(13072880683271992816)
XLA Ops:
  0.6 1.9 %gather_rows.1 = (bf16[2,2,24,320]{3,2,1,0:T(8,128)(2,1)S(1)}, bf16[48,1024]{1,0:T(8,128)(2,1)S(1)}) custom-call(s32[2,24]{1,0:T(2,128)} %bitcast.30, bf16[320,1024]{1,0:T(8,128)(2,1)} %bitcast.28, bf16[320,1024]{1,0:T(8,128)(2,1)} %bitcast.29), custom_call_target="tpu_custom_call" | custom-call | tf_op jit(solution)/shard_map/gather_rows/pallas_call | solution.py:228
  2.6 3.0 %collective-permute-start = (bf16[2,24,320]{2,1,0:T(8,128)(2,1)S(1)}, bf16[2,24,320]{2,1,0:T(8,128)(2,1)S(1)}, u32[]{:S(2)}, u32[]{:S(2)}) collective-permute-start(bf16[2,24,320]{2,1,0:T(8,128)(2,1)S(1)} %get-tuple-element.37), channel_id=1, source_target_pairs={{0,1},{1,0},{2,3},{3,2},{4,5},{5,4},{6,7},{7,6},{8,9},{9,8},{10,11... | collective-permute-start | bytes 92168 | tf_op jit(solution)/shard_map/ppermute | solution.py:224
  5.6 1.8 %load_weights.1 = (bf16[320,1536]{1,0:T(8,128)(2,1)S(1)}, bf16[320,1536]{1,0:T(8,128)(2,1)S(1)}, bf16[320,1536]{1,0:T(8,128)(2,1)S(1)}) custom-call(bf16[2,24,320]{2,1,0:T(8,128)(2,1)S(1)} %get-tuple-element.38.after.own, bf16[1,320,1536]{2,1,0:T(8,128)(2,1)} %w_gate.1, bf16[1,320,1536]{2,1,0:T(8,128)(2,1)} %w_up.1, bf16[1,320,1536]{2,1,0:T(8,128)(2,1)} %w_down.1), custom_call_target="tpu_custom_call" | custom-call | bytes 2949120 | tf_op jit(solution)/shard_map/load_weights/pallas_call | solution.py:247
  7.4 0.1 collective-permute-done
  7.5 0.4 partial_sums.3
  7.9 0.0 copy-start
  7.9 0.0 copy-start.1
  7.9 0.1 collective-permute-start.1
  8.0 0.4 partial_sums.2
  8.4 1.4 %collective-permute-done.1.arrived = f32[4,72,384]{2,1,0:T(8,128)S(1)} collective-permute-done((f32[4,72,384]{2,1,0:T(8,128)S(1)}, f32[4,72,384]{2,1,0:T(8,128)S(1)}, u32[]{:S(2)}, u32[]{:S(2)}) %collective-permute-start.1) | collective-permute-done | bytes 442400 | tf_op jit(solution)/shard_map/ppermute | solution.py:220
  9.8 0.1 add.16
  9.9 2.1 %collective-permute-start.2 = (f32[72,384]{1,0:T(8,128)S(1)}, f32[72,384]{1,0:T(8,128)S(1)}, u32[]{:S(2)}, u32[]{:S(2)}) collective-permute-start(f32[72,384]{1,0:T(8,128)S(1)} %get-tuple-element.27), channel_id=1, source_target_pairs={{0,4},{2,6},{4,0},{6,2},{8,12},{10,14},{12,8},{14,10},{16,20},{18,... | collective-permute-start | bytes 331784 | tf_op jit(solution)/shard_map/ppermute | solution.py:220
  12.0 1.6 %collective-permute-start.3 = (f32[72,384]{1,0:T(8,128)S(1)}, f32[72,384]{1,0:T(8,128)S(1)}, u32[]{:S(2)}, u32[]{:S(2)}) collective-permute-start(f32[72,384]{1,0:T(8,128)S(1)} %get-tuple-element.28), channel_id=1, source_target_pairs={{0,8},{2,10},{4,12},{6,14},{8,0},{10,2},{12,4},{14,6},{16,24},{18,... | collective-permute-start | bytes 331784 | tf_op jit(solution)/shard_map/ppermute | solution.py:220
  13.5 0.0 collective-permute-start.4
  13.5 1.8 %collective-permute-done.2 = f32[72,384]{1,0:T(8,128)S(1)} collective-permute-done((f32[72,384]{1,0:T(8,128)S(1)}, f32[72,384]{1,0:T(8,128)S(1)}, u32[]{:S(2)}, u32[]{:S(2)}) %collective-permute-start.2) | collective-permute-done | bytes 110624 | tf_op jit(solution)/shard_map/ppermute | solution.py:220
  15.3 2.6 %collective-permute-done.3 = f32[72,384]{1,0:T(8,128)S(1)} collective-permute-done((f32[72,384]{1,0:T(8,128)S(1)}, f32[72,384]{1,0:T(8,128)S(1)}, u32[]{:S(2)}, u32[]{:S(2)}) %collective-permute-start.3) | collective-permute-done | bytes 110624 | tf_op jit(solution)/shard_map/ppermute | solution.py:220
  17.9 1.3 %collective-permute-done.4 = f32[72,384]{1,0:T(8,128)S(1)} collective-permute-done((f32[72,384]{1,0:T(8,128)S(1)}, f32[72,384]{1,0:T(8,128)S(1)}, u32[]{:S(2)}, u32[]{:S(2)}) %collective-permute-start.4) | collective-permute-done | bytes 110624 | tf_op jit(solution)/shard_map/ppermute | solution.py:220
  19.2 2.7 %collective-permute-start.5 = (f32[72,384]{1,0:T(8,128)S(1)}, f32[72,384]{1,0:T(8,128)S(1)}, u32[]{:S(2)}, u32[]{:S(2)}) collective-permute-start(f32[72,384]{1,0:T(8,128)S(1)} %add_add_fusion.sums), channel_id=1, source_target_pairs={{0,16},{2,18},{4,20},{6,22},{8,24},{10,26},{12,28},{14,30},{16,0},... | collective-permute-start | bytes 331784 | tf_op jit(solution)/shard_map/ppermute | solution.py:220
  21.9 4.4 %collective-permute-done.5.recv = f32[72,384]{1,0:T(8,128)S(1)} collective-permute-done((f32[72,384]{1,0:T(8,128)S(1)}, f32[72,384]{1,0:T(8,128)S(1)}, u32[]{:S(2)}, u32[]{:S(2)}) %collective-permute-start.5) | collective-permute-done | bytes 110624 | tf_op jit(solution)/shard_map/ppermute | solution.py:220
  26.2 0.0 copy-done
  26.2 0.0 copy-done.1
  26.3 0.7 %hidden.1.near0 = bf16[96,384]{1,0:T(8,128)(2,1)S(1)} custom-call(s32[2]{0:T(128)S(1)} %bitcast.26, f32[1,48]{1,0:T(1,128)S(1)} %copy-done.1, f32[72,384]{1,0:T(8,128)S(1)} %add_add_fusion.sums, f32[72,384]{1,0:T(8,128)S(1)} %collective-permute-done.5.recv), custom_call_target="tpu_custom_call" | custom-call | tf_op jit(solution)/shard_map/hidden/pallas_call | solution.py:290
  26.9 1.9 %collective-permute-start.8 = (bf16[96,384]{1,0:T(8,128)(2,1)S(1)}, bf16[96,384]{1,0:T(8,128)(2,1)S(1)}, u32[]{:S(2)}, u32[]{:S(2)}) collective-permute-start(bf16[96,384]{1,0:T(8,128)(2,1)S(1)} %hidden.1.near0), channel_id=1, source_target_pairs={{0,12},{2,14},{4,8},{6,10},{8,4},{10,6},{12,0},{14,2},{16,28},{18,... | collective-permute-start | bytes 221192 | tf_op jit(solution)/shard_map/ppermute | solution.py:220
  28.8 1.4 %collective-permute-start.7 = (bf16[96,384]{1,0:T(8,128)(2,1)S(1)}, bf16[96,384]{1,0:T(8,128)(2,1)S(1)}, u32[]{:S(2)}, u32[]{:S(2)}) collective-permute-start(bf16[96,384]{1,0:T(8,128)(2,1)S(1)} %hidden.1.near0), channel_id=1, source_target_pairs={{0,8},{2,10},{4,12},{6,14},{8,0},{10,2},{12,4},{14,6},{16,24},{18,... | collective-permute-start | bytes 221192 | tf_op jit(solution)/shard_map/ppermute | solution.py:220
  30.1 0.3 collective-permute-start.6
  30.5 1.8 %collective-permute-done.8.near3 = bf16[96,384]{1,0:T(8,128)(2,1)S(1)} collective-permute-done((bf16[96,384]{1,0:T(8,128)(2,1)S(1)}, bf16[96,384]{1,0:T(8,128)(2,1)S(1)}, u32[]{:S(2)}, u32[]{:S(2)}) %collective-permute-start.8) | collective-permute-done | bytes 73760 | tf_op jit(solution)/shard_map/ppermute | solution.py:220
  32.2 1.0 %collective-permute-done.7.near2 = bf16[96,384]{1,0:T(8,128)(2,1)S(1)} collective-permute-done((bf16[96,384]{1,0:T(8,128)(2,1)S(1)}, bf16[96,384]{1,0:T(8,128)(2,1)S(1)}, u32[]{:S(2)}, u32[]{:S(2)}) %collective-permute-start.7) | collective-permute-done | bytes 73760 | tf_op jit(solution)/shard_map/ppermute | solution.py:220
  33.3 1.2 %collective-permute-done.6.near1 = bf16[96,384]{1,0:T(8,128)(2,1)S(1)} collective-permute-done((bf16[96,384]{1,0:T(8,128)(2,1)S(1)}, bf16[96,384]{1,0:T(8,128)(2,1)S(1)}, u32[]{:S(2)}, u32[]{:S(2)}) %collective-permute-start.6) | collective-permute-done | bytes 73760 | tf_op jit(solution)/shard_map/ppermute | solution.py:220
  34.5 0.1 collective-permute-start.9
  34.6 0.4 %near_slot.1.before = f32[64,320]{1,0:T(8,128)S(1)} custom-call(bf16[96,384]{1,0:T(8,128)(2,1)S(1)} %hidden.1.near0, bf16[96,384]{1,0:T(8,128)(2,1)S(1)} %collective-permute-done.6.near1, bf16[96,384]{1,0:T(8,128)(2,1)S(1)} %collective-permute-done.7.near2, bf16[96,384]{1,0:T(8,128)(2,1)S(1)} %collective-permute-done.8.near3, ...), custom_call_target="tpu_custom_call" | custom-call | flops 47185920 | bytes 983040 | tf_op jit(solution)/shard_map/near_slot/pallas_call | solution.py:301
  35.1 1.1 %collective-permute-done.9.far = bf16[4,96,384]{2,1,0:T(8,128)(2,1)S(1)} collective-permute-done((bf16[4,96,384]{2,1,0:T(8,128)(2,1)S(1)}, bf16[4,96,384]{2,1,0:T(8,128)(2,1)S(1)}, u32[]{:S(2)}, u32[]{:S(2)}) %collective-permute-start.9) | collective-permute-done | bytes 294944 | tf_op jit(solution)/shard_map/ppermute | solution.py:220
  36.2 0.4 %slot_grad.1 = bf16[2,24,320]{2,1,0:T(8,128)(2,1)S(1)} custom-call(f32[64,320]{1,0:T(8,128)S(1)} %near_slot.1.before, bf16[4,96,384]{2,1,0:T(8,128)(2,1)S(1)} %collective-permute-done.9.far, bf16[320,1536]{1,0:T(8,128)(2,1)S(1)} %get-tuple-element.22.w_gate, bf16[320,1536]{1,0:T(8,128)(2,1)S(1)} %get-tuple-element.23.w_up), custom_call_target="tpu_custom_call" | custom-call | tf_op jit(solution)/shard_map/slot_grad/pallas_call | solution.py:312
  36.6 1.6 %collective-permute-start.10 = (bf16[24,320]{1,0:T(8,128)(2,1)S(1)}, bf16[24,320]{1,0:T(8,128)(2,1)S(1)}, u32[]{:S(2)}, u32[]{:S(2)}) collective-permute-start(bf16[24,320]{1,0:T(8,128)(2,1)S(1)} %get-tuple-element.39), channel_id=1, source_target_pairs={{0,1},{1,0},{2,3},{3,2},{4,5},{5,4},{6,7},{7,6},{8,9},{9,8},{10,11... | collective-permute-start | bytes 46088 | tf_op jit(solution)/shard_map/ppermute | solution.py:224
  38.2 3.4 %weight_grads.1 = (f32[1,320,1536]{2,1,0:T(8,128)}, f32[1,320,1536]{2,1,0:T(8,128)}, f32[1,320,1536]{2,1,0:T(8,128)}, f32[1,3]{1,0:T(1,128)}) custom-call(bf16[96,384]{1,0:T(8,128)(2,1)S(1)} %hidden.1.near0, bf16[96,384]{1,0:T(8,128)(2,1)S(1)} %collective-permute-done.6.near1, bf16[96,384]{1,0:T(8,128)(2,1)S(1)} %collective-permute-done.7.near2, ...), custom_call_target="tpu_custom_call" | custom-call | flops 141557760 | bytes 5898240 | tf_op jit(solution)/shard_map/weight_grads/pallas_call | solution.py:322
  41.6 0.0 collective-permute-done.10
  41.6 1.2 %token_grad.1 = bf16[320,1024]{1,0:T(8,128)(2,1)} custom-call(bf16[24,320]{1,0:T(8,128)(2,1)S(1)} %get-tuple-element.40.own, bf16[1,24,320]{2,1,0:T(8,128)(2,1)S(1)} %bitcast.25, bf16[48,1024]{1,0:T(8,128)(2,1)S(1)} %get-tuple-element.30.onehot), custom_call_target="tpu_custom_call" | custom-call | tf_op jit(solution)/shard_map/token_grad/pallas_call | solution.py:335
  (4 shorter events, 0.1 us)
Async XLA Ops:
  2.6 4.9 %collective-permute-start = (bf16[2,24,320]{2,1,0:T(8,128)(2,1)S(1)}, bf16[2,24,320]{2,1,0:T(8,128)(2,1)S(1)}, u32[]{:S(2)}, u32[]{:S(2)}) collective-permute-start(bf16[2,24,320]{2,1,0:T(8,128)(2,1)S(1)} %get-tuple-element.37), channel_id=1, source_target_pairs={{0,1},{1,0},{2,3},{3,2},{4,5},{5,4},{6,7},{7,6},{8,9},{9,8},{10,11... | collective-permute-start | bytes 92168 | tf_op jit(solution)/shard_map/ppermute | solution.py:224
  7.9 18.3 %copy-start = (s32[1,2]{1,0:T(1,128)S(1)}, s32[1,2]{1,0:T(1,128)}, u32[]{:S(2)}) copy-start(s32[1,2]{1,0:T(1,128)} %param.11) | copy-start | bytes 28
  7.9 18.3 %copy-start.1 = (f32[1,48]{1,0:T(1,128)S(1)}, f32[1,48]{1,0:T(1,128)}, u32[]{:S(2)}) copy-start(f32[1,48]{1,0:T(1,128)} %prob.1) | copy-start | bytes 580
  7.9 1.9 %collective-permute-start.1 = (f32[4,72,384]{2,1,0:T(8,128)S(1)}, f32[4,72,384]{2,1,0:T(8,128)S(1)}, u32[]{:S(2)}, u32[]{:S(2)}) collective-permute-start(f32[4,72,384]{2,1,0:T(8,128)S(1)} %partial_sums.3), channel_id=1, source_target_pairs={{0,2},{2,0},{4,6},{6,4},{8,10},{10,8},{12,14},{14,12},{16,18},{18,... | collective-permute-start | bytes 1327112 | tf_op jit(solution)/shard_map/ppermute | solution.py:220
  9.9 5.5 %collective-permute-start.2 = (f32[72,384]{1,0:T(8,128)S(1)}, f32[72,384]{1,0:T(8,128)S(1)}, u32[]{:S(2)}, u32[]{:S(2)}) collective-permute-start(f32[72,384]{1,0:T(8,128)S(1)} %get-tuple-element.27), channel_id=1, source_target_pairs={{0,4},{2,6},{4,0},{6,2},{8,12},{10,14},{12,8},{14,10},{16,20},{18,... | collective-permute-start | bytes 331784 | tf_op jit(solution)/shard_map/ppermute | solution.py:220
  12.0 5.9 %collective-permute-start.3 = (f32[72,384]{1,0:T(8,128)S(1)}, f32[72,384]{1,0:T(8,128)S(1)}, u32[]{:S(2)}, u32[]{:S(2)}) collective-permute-start(f32[72,384]{1,0:T(8,128)S(1)} %get-tuple-element.28), channel_id=1, source_target_pairs={{0,8},{2,10},{4,12},{6,14},{8,0},{10,2},{12,4},{14,6},{16,24},{18,... | collective-permute-start | bytes 331784 | tf_op jit(solution)/shard_map/ppermute | solution.py:220
  13.5 5.6 %collective-permute-start.4 = (f32[72,384]{1,0:T(8,128)S(1)}, f32[72,384]{1,0:T(8,128)S(1)}, u32[]{:S(2)}, u32[]{:S(2)}) collective-permute-start(f32[72,384]{1,0:T(8,128)S(1)} %get-tuple-element.29), channel_id=1, source_target_pairs={{0,12},{2,14},{4,8},{6,10},{8,4},{10,6},{12,0},{14,2},{16,28},{18,... | collective-permute-start | bytes 331784 | tf_op jit(solution)/shard_map/ppermute | solution.py:220
  19.2 7.0 %collective-permute-start.5 = (f32[72,384]{1,0:T(8,128)S(1)}, f32[72,384]{1,0:T(8,128)S(1)}, u32[]{:S(2)}, u32[]{:S(2)}) collective-permute-start(f32[72,384]{1,0:T(8,128)S(1)} %add_add_fusion.sums), channel_id=1, source_target_pairs={{0,16},{2,18},{4,20},{6,22},{8,24},{10,26},{12,28},{14,30},{16,0},... | collective-permute-start | bytes 331784 | tf_op jit(solution)/shard_map/ppermute | solution.py:220
  26.9 5.3 %collective-permute-start.8 = (bf16[96,384]{1,0:T(8,128)(2,1)S(1)}, bf16[96,384]{1,0:T(8,128)(2,1)S(1)}, u32[]{:S(2)}, u32[]{:S(2)}) collective-permute-start(bf16[96,384]{1,0:T(8,128)(2,1)S(1)} %hidden.1.near0), channel_id=1, source_target_pairs={{0,12},{2,14},{4,8},{6,10},{8,4},{10,6},{12,0},{14,2},{16,28},{18,... | collective-permute-start | bytes 221192 | tf_op jit(solution)/shard_map/ppermute | solution.py:220
  28.8 4.5 %collective-permute-start.7 = (bf16[96,384]{1,0:T(8,128)(2,1)S(1)}, bf16[96,384]{1,0:T(8,128)(2,1)S(1)}, u32[]{:S(2)}, u32[]{:S(2)}) collective-permute-start(bf16[96,384]{1,0:T(8,128)(2,1)S(1)} %hidden.1.near0), channel_id=1, source_target_pairs={{0,8},{2,10},{4,12},{6,14},{8,0},{10,2},{12,4},{14,6},{16,24},{18,... | collective-permute-start | bytes 221192 | tf_op jit(solution)/shard_map/ppermute | solution.py:220
  30.1 4.4 %collective-permute-start.6 = (bf16[96,384]{1,0:T(8,128)(2,1)S(1)}, bf16[96,384]{1,0:T(8,128)(2,1)S(1)}, u32[]{:S(2)}, u32[]{:S(2)}) collective-permute-start(bf16[96,384]{1,0:T(8,128)(2,1)S(1)} %hidden.1.near0), channel_id=1, source_target_pairs={{0,4},{2,6},{4,0},{6,2},{8,12},{10,14},{12,8},{14,10},{16,20},{18,... | collective-permute-start | bytes 221192 | tf_op jit(solution)/shard_map/ppermute | solution.py:220
  34.5 1.6 %collective-permute-start.9 = (bf16[4,96,384]{2,1,0:T(8,128)(2,1)S(1)}, bf16[4,96,384]{2,1,0:T(8,128)(2,1)S(1)}, u32[]{:S(2)}, u32[]{:S(2)}) collective-permute-start(bf16[4,96,384]{2,1,0:T(8,128)(2,1)S(1)} %pad_maximum_fusion), channel_id=1, source_target_pairs={{0,2},{2,0},{4,6},{6,4},{8,10},{10,8},{12,14},{14,12},{16,18},{18,... | collective-permute-start | bytes 884744 | tf_op jit(solution)/shard_map/ppermute | solution.py:220
  36.6 4.9 %collective-permute-start.10 = (bf16[24,320]{1,0:T(8,128)(2,1)S(1)}, bf16[24,320]{1,0:T(8,128)(2,1)S(1)}, u32[]{:S(2)}, u32[]{:S(2)}) collective-permute-start(bf16[24,320]{1,0:T(8,128)(2,1)S(1)} %get-tuple-element.39), channel_id=1, source_target_pairs={{0,1},{1,0},{2,3},{3,2},{4,5},{5,4},{6,7},{7,6},{8,9},{9,8},{10,11... | collective-permute-start | bytes 46088 | tf_op jit(solution)/shard_map/ppermute | solution.py:224

commit v3 on v2

v3 whole, which is shorter than its diff:
```python
import functools

import jax
import jax.numpy as jnp
from jax import lax
from jax.experimental import pallas as pl
from jax.experimental.pallas import tpu as pltpu
from jax.sharding import PartitionSpec as P

BF16 = jnp.bfloat16
F32 = jnp.float32
F16 = jnp.float16
VMEM = pl.BlockSpec(memory_space=pltpu.VMEM)
HBM = pl.BlockSpec(memory_space=pltpu.HBM)
SMEM = pl.BlockSpec(memory_space=pltpu.SMEM)
PARAMS = pltpu.CompilerParams(vmem_limit_bytes=40 * 2**20)

def in_hbm(x):
    return pltpu.with_memory_space_constraint(x, pltpu.HBM)


def dot(a, b, contract):
    return lax.dot_general(a, b, ((contract[0:1], contract[1:2]), ((), ())), preferred_element_type=F32)


def place(side, jy, width):
    me = lax.axis_index("fsdp")
    half = (me & 1) ^ side
    return pl.multiple_of((half * 2 + (((me >> 1) & 1) ^ jy)) * width, 128)


def row_part():
    return (lax.axis_index("fsdp") >> 2) & 1


def first_expert(experts):
    return lax.axis_index("expert") if experts == 2 else 0


def gather_kernel(slot_rows_hbm, tokens_hbm, grads_hbm, rows_out, onehot_out, slot_rows, tokens_t, grads_t, onehot_f, sems):
    copies = [
        pltpu.make_async_copy(source, to, sems.at[i])
        for i, (source, to) in enumerate(((slot_rows_hbm, slot_rows), (tokens_hbm, tokens_t), (grads_hbm, grads_t)))
    ]
    for copy in copies:
        copy.start()
    experts, slots = slot_rows.shape
    count = tokens_t.shape[1]
    first = first_expert(experts)
    lane = lax.broadcasted_iota(jnp.int32, (8, count), 1)
    sub = lax.broadcasted_iota(jnp.int32, (8, count), 0)
    copies[0].wait()
    for j in range(experts):
        expert = lax.rem(first + j, experts)
        for base in range(0, slots, 8):
            picked = jnp.zeros((8, count), jnp.int32)
            for r in range(8):
                picked = jnp.where(sub == r, slot_rows[expert, base + r], picked)
            onehot_f[pl.ds(j * slots + base, 8), :] = (picked == lane).astype(F32)
    onehot = onehot_f[...].astype(BF16)
    onehot_out[...] = onehot
    for kind, source in enumerate((tokens_t, grads_t)):
        copies[1 + kind].wait()
        rows = dot(onehot, source[...], (1, 1))
        for j in range(experts):
            rows_out[j, kind] = rows[j * slots : (j + 1) * slots].astype(BF16)


def load_kernel(after, w_gate, w_up, w_down, gate_out, up_out, down_out, sems):
    del after
    copies = [
        pltpu.make_async_copy(w.at[0], to, sems.at[i])
        for i, (w, to) in enumerate(((w_gate, gate_out), (w_up, up_out), (w_down, down_out)))
    ]
    for copy in copies:
        copy.start()
    for copy in copies:
        copy.wait()


def stacked_rows(own, recv, kind):
    blocks = [own[kind]] + [recv[j, kind] for j in range(recv.shape[0])]
    return jnp.concatenate([block.astype(F32) for block in blocks], axis=0)


def partial_kernel(side, own, recv, w_gate, w_up, w_down, out):
    tok, grad = stacked_rows(own, recv, 0).astype(BF16), stacked_rows(own, recv, 1).astype(BF16)
    chunk_rows, width = out.shape[1] // 3, out.shape[2]
    for jy in range(2):
        at = pl.ds(place(side, jy, width), width)
        for q, (x, w) in enumerate(((tok, w_gate), (tok, w_up), (grad, w_down))):
            sums = dot(x, w[:, at], (1, 0))
            for part in range(2):
                chunk = (row_part() ^ part) * 2 + jy
                out[chunk, pl.ds(q * chunk_rows, chunk_rows), :] = sums[part * chunk_rows : (part + 1) * chunk_rows]


def rows_kernel(counts, own, recv, prob, tok_t, grad_t, scale_out, live_out, diagonal_out):
    part0 = row_part()
    rows, lanes = diagonal_out.shape
    for to, x in ((tok_t, stacked_rows(own, recv, 0)), (grad_t, stacked_rows(own, recv, 1))):
        low, high = x[:rows], x[rows:]
        near, far = jnp.where(part0 == 0, low, high), jnp.where(part0 == 0, high, low)
        to[...] = jnp.concatenate([near, far], axis=0).T.astype(BF16)
    experts = counts.shape[0]
    slots = 2 * rows // experts
    first = first_expert(experts)
    row = lax.broadcasted_iota(jnp.int32, (rows, lanes), 0) + part0 * rows
    lane = lax.broadcasted_iota(jnp.int32, (rows, lanes), 1)
    slot, home, live_count = row, row, row
    for j in range(experts):
        source = lax.rem(first + j, experts)
        inside = (row >= j * slots) & (row < (j + 1) * slots)
        slot = jnp.where(inside, row - j * slots, slot)
        home = jnp.where(inside, source * slots + row - j * slots, home)
        live_count = jnp.where(inside, counts[source], live_count)
    live = (slot < live_count).astype(F32)
    diagonal = lane == home
    probs = jnp.concatenate([prob[...], jnp.zeros((1, lanes - 2 * rows), F32)], axis=1)
    row_prob = jnp.sum(jnp.where(diagonal, probs, 0.0), axis=1, keepdims=True)
    scale_out[...] = row_prob * live[:, :128]
    live_out[...] = live[:, :128]
    diagonal_out[...] = diagonal.astype(F32)


def add_kernel(kept, arrived, first, power_out, *outs):
    rows = first.shape[0] // 3
    width = first.shape[1]
    chunks = [kept[j] + arrived[j] for j in range(4)]
    first[...] = chunks[0]
    powers = []
    for q in range(3):
        most = functools.reduce(jnp.maximum, [jnp.abs(x[q * rows : (q + 1) * rows]) for x in chunks])
        most = jnp.max(jnp.max(most, axis=0, keepdims=True), axis=1, keepdims=True)
        most = jnp.maximum(jnp.broadcast_to(most, (1, width)), 1e-30)
        powers.append(jnp.ceil(jnp.log2(most)) - 14.0)
    power_out[...] = jnp.concatenate(powers + [jnp.zeros((5, width), F32)], axis=0)
    for x, out in zip(chunks[1:], outs):
        for q in range(3):
            out[pl.ds(q * rows, rows), :] = x[q * rows : (q + 1) * rows] * jnp.exp2(-powers[q])
        out[pl.ds(3 * rows, 8), :] = power_out[...]


def scaled(x, power):
    rows = x.shape[0] // 3
    return (x.reshape(3, rows, -1) * jnp.exp2(power[:3])[:, None]).reshape(x.shape)


def coded(x, power):
    return jnp.concatenate([scaled(x, -power), power], axis=0)


def decoded(x):
    x = x.astype(F32)
    return scaled(x[:-8], x[-8:]), x[-8:]


def hidden_kernel(scale, live, diagonal, sums, recv, out):
    rows = sums.shape[0] // 3
    width = sums.shape[1]
    total = sums[...] + recv[...]
    gate, up, down = total[:rows], total[rows : 2 * rows], total[2 * rows :]
    row_scale = jnp.concatenate([scale[...]] * (width // 128), axis=1)
    sigmoid = jax.nn.sigmoid(gate)
    silu = gate * sigmoid
    hidden = (silu * up).astype(BF16).astype(F32)
    hidden_grad = down * row_scale
    gate_act_grad = hidden_grad * up * sigmoid * (1.0 + gate * (1.0 - sigmoid))
    prob_grad = live[:, :1] * jnp.sum(hidden * down, axis=1, keepdims=True)
    prob_row = jnp.sum(diagonal[...] * prob_grad, axis=0, keepdims=True)
    high = prob_row.astype(BF16).astype(F32)
    tail = jnp.concatenate([high, prob_row - high, jnp.zeros((6, prob_row.shape[1]), F32)], axis=0)
    tail = jnp.concatenate([tail, jnp.zeros((8, width - prob_row.shape[1]), F32)], axis=1)
    out[...] = jnp.concatenate([hidden * row_scale, gate_act_grad, hidden_grad * silu, tail], axis=0).astype(BF16)


def parts(a, b):
    a, b = a[...].astype(F32), b[...].astype(F32)
    rows = (a.shape[0] - 8) // 3
    both = [jnp.concatenate([a[q * rows : (q + 1) * rows], b[q * rows : (q + 1) * rows]], axis=0) for q in range(3)]
    return [x.astype(BF16) for x in both]


def slot_part(a, b, w_gate, w_up, column):
    _, gate_act_grad, up_act_grad = parts(a, b)
    at = pl.ds(column, a.shape[1])
    return dot(gate_act_grad, w_gate[:, at], (1, 1)) + dot(up_act_grad, w_up[:, at], (1, 1))


def weight_grad_copies(pieces, tok_t, grad_t, outs, held, sems):
    copies = []
    for a, b, column in pieces:
        down, gate, up = parts(a, b)
        for x, y, out in ((tok_t, gate, outs[0]), (tok_t, up, outs[1]), (grad_t, down, outs[2])):
            n = len(copies)
            held[n] = dot(x[...], y, (1, 0))
            copies.append(pltpu.make_async_copy(held.at[n], out.at[0, :, pl.ds(column, a.shape[1])], sems.at[n]))
            copies[n].start()
    return copies


def near_kernel(near0, near1, near2, near3, w_gate, w_up, tok_t, grad_t, out, gate_grad, up_grad, down_grad, held, sems):
    width = near0.shape[1]
    pieces = [(near0, near2, place(0, 0, width))]
    copies = weight_grad_copies(pieces, tok_t, grad_t, (gate_grad, up_grad, down_grad), held, sems)
    out[...] = slot_part(near0, near2, w_gate, w_up, place(0, 0, width)) + slot_part(
        near1, near3, w_gate, w_up, place(0, 1, width)
    )
    for copy in copies:
        copy.wait()


def slot_kernel(before, far, w_gate, w_up, out):
    width = far.shape[2]
    experts, slots, _ = out.shape
    total = before[...]
    for jy in range(2):
        total += slot_part(far.at[jy], far.at[2 + jy], w_gate, w_up, place(1, jy, width))
    for part in range(2):
        for j in range(experts // 2):
            start = (part * (experts // 2) + j) * slots
            out[(row_part() ^ part) * (experts // 2) + j] = total[start : start + slots].astype(BF16)


def weight_grad_kernel(near0, near1, near2, near3, far, tok_t, grad_t, *refs):
    gate_grad, up_grad, down_grad, prob_out, held, sems = refs[3:]
    width = far.shape[2]
    pieces = [(near1, near3, place(0, 1, width))]
    pieces += [(far.at[jy], far.at[2 + jy], place(1, jy, width)) for jy in range(2)]
    copies = weight_grad_copies(pieces, tok_t, grad_t, (gate_grad, up_grad, down_grad), held, sems)
    tail = jnp.zeros((8, width), F32)
    for chunk in (near0, near1, near2, near3, far.at[0], far.at[1], far.at[2], far.at[3]):
        tail += chunk[...].astype(F32)[-8:]
    prob = jnp.broadcast_to(tail[0:1] + tail[1:2], (8, width))
    share = prob_out.shape[1]
    shift = lax.rem(width - lax.axis_index("fsdp") * share, width)
    prob_out[...] = pltpu.roll(prob, shift, 1)[:1, :share]
    for copy in copies:
        copy.wait()


def token_grad_kernel(own, recv, onehot, out, held, sems):
    blocks = [own[...]] + [recv[j] for j in range(recv.shape[0])]
    slot_grad = jnp.concatenate([block.astype(F32) for block in blocks], axis=0).T.astype(BF16)
    count, _, width = held.shape
    copies = []
    for i in range(count):
        held[i] = dot(slot_grad, onehot[:, i * width : (i + 1) * width], (1, 0)).astype(BF16)
        copies.append(pltpu.make_async_copy(held.at[i], out.at[:, pl.ds(i * width, width)], sems.at[i]))
        copies[i].start()
    for copy in copies:
        copy.wait()


def local(tokens, out_grad, slot_rows, expert_counts, route_prob, w_gate, w_up, w_down):
    fsdp, experts = lax.axis_size("fsdp"), lax.axis_size("expert")
    steps = fsdp.bit_length() - 1
    token_count, features = tokens.shape
    _, _, slots = slot_rows.shape
    rows = experts * slots
    hidden = w_gate.shape[2]
    half, quarter = hidden // 2, hidden // 4
    def swap(x, *bits):
        mask = sum(1 << b for b in bits)
        return lax.ppermute(x, "fsdp", [(i, i ^ mask) for i in range(fsdp)])

    def to_expert(x):
        if experts == 2:
            return x[0], lax.ppermute(x[1], "expert", [(0, 1), (1, 0)])[None]
        moved = lax.all_to_all(x, "expert", split_axis=0, concat_axis=0, tiled=True)
        return moved[0], moved[1:]

    rows_out, onehot = pl.pallas_call(
        gather_kernel,
        out_shape=(
            jax.ShapeDtypeStruct((experts, 2, slots, features), BF16),
            jax.ShapeDtypeStruct((rows, token_count), BF16),
        ),
        in_specs=[HBM] * 3,
        out_specs=(VMEM, VMEM),
        scratch_shapes=[
            pltpu.SMEM((experts, slots), jnp.int32),
            pltpu.VMEM((features, token_count), BF16),
            pltpu.VMEM((features, token_count), BF16),
            pltpu.VMEM((rows, token_count), F32),
            pltpu.SemaphoreType.DMA((3,)),
        ],
        compiler_params=PARAMS,
        name="gather_rows",
    )(*(in_hbm(x) for x in (slot_rows[0], tokens.T, out_grad.T)))
    own, recv = to_expert(rows_out)
    weights = pl.pallas_call(
        load_kernel,
        out_shape=(jax.ShapeDtypeStruct((features, hidden), BF16),) * 3,
        in_specs=[VMEM] + [HBM] * 3,
        out_specs=(VMEM,) * 3,
        scratch_shapes=[pltpu.SemaphoreType.DMA((3,))],
        compiler_params=PARAMS,
        cost_estimate=pl.CostEstimate(flops=0, bytes_accessed=6 * features * hidden, transcendentals=0),
        name="load_weights",
    )(own, *(in_hbm(w) for w in (w_gate, w_up, w_down)))

    def partial(side):
        return pl.pallas_call(
            functools.partial(partial_kernel, side),
            out_shape=jax.ShapeDtypeStruct((4, 3 * rows // 2, quarter), F32),
            in_specs=[VMEM] * 5,
            out_specs=VMEM,
            compiler_params=PARAMS,
            cost_estimate=pl.CostEstimate(
                flops=6 * rows * features * half, bytes_accessed=3 * features * half * 2, transcendentals=0
            ),
            name="partial_sums",
        )(own, recv, *weights)

    arrived = swap(partial(1), 0)
    kept = partial(0)
    turned_shape = jax.ShapeDtypeStruct((features, rows), BF16)
    fact_shape = jax.ShapeDtypeStruct((rows // 2, 128), F32)
    diagonal_shape = jax.ShapeDtypeStruct((rows // 2, (rows + 127) // 128 * 128), F32)
    tok_t, grad_t, scale, live, diagonal = pl.pallas_call(
        rows_kernel,
        out_shape=(turned_shape, turned_shape, fact_shape, fact_shape, diagonal_shape),
        in_specs=[SMEM] + [VMEM] * 3,
        out_specs=(VMEM,) * 5,
        compiler_params=PARAMS,
        cost_estimate=pl.CostEstimate(flops=0, bytes_accessed=8 * features * rows, transcendentals=0),
        name="row_facts",
    )(expert_counts[0], own, recv, route_prob)
    coded_shape = jax.ShapeDtypeStruct((3 * rows // 2 + 8, quarter), F32)
    total, power, *sent = pl.pallas_call(
        add_kernel,
        out_shape=(
            jax.ShapeDtypeStruct((3 * rows // 2, quarter), F32),
            jax.ShapeDtypeStruct((8, quarter), F32),
        )
        + (coded_shape,) * 3,
        in_specs=[VMEM] * 2,
        out_specs=(VMEM,) * 5,
        compiler_params=PARAMS,
        name="add",
    )(kept, arrived)
    arrived = [swap(x.astype(F16), *bits) for x, bits in zip(sent, ((1,), (2,), (1, 2)))]
    for x in arrived:
        chunk, its_power = decoded(x)
        total, power = total + chunk, jnp.maximum(power, its_power)
    power += 2.0
    for b in range(3, steps):
        arrived, its_power = decoded(swap(coded(total, power).astype(F16), b))
        if b < steps - 1:
            total, power = total + arrived, jnp.maximum(power, its_power) + 1.0
    acts = pl.pallas_call(
        hidden_kernel,
        out_shape=jax.ShapeDtypeStruct((3 * rows // 2 + 8, quarter), BF16),
        in_specs=[VMEM] * 5,
        out_specs=VMEM,
        compiler_params=PARAMS,
        name="hidden",
    )(scale, live, diagonal, total, arrived)
    near = [acts, swap(acts, 1), swap(acts, 2), swap(acts, 1, 2)]
    far = swap(jnp.stack(near), 0)

    grad_shape = jax.ShapeDtypeStruct((1, features, hidden), F32)

    def held(count):
        return [pltpu.VMEM((count, features, quarter), F32), pltpu.SemaphoreType.DMA((count,))]

    near_slot, *grads = pl.pallas_call(
        near_kernel,
        out_shape=(jax.ShapeDtypeStruct((rows, features), F32),) + (grad_shape,) * 3,
        in_specs=[VMEM] * 8,
        out_specs=(VMEM,) + (HBM,) * 3,
        scratch_shapes=held(3),
        compiler_params=PARAMS,
        cost_estimate=pl.CostEstimate(
            flops=4 * rows * features * hidden, bytes_accessed=3 * features * hidden, transcendentals=0
        ),
        name="near_piece",
    )(*near, weights[0], weights[1], tok_t, grad_t)
    slot_grad = pl.pallas_call(
        slot_kernel,
        out_shape=jax.ShapeDtypeStruct((experts, slots, features), BF16),
        in_specs=[VMEM] * 4,
        out_specs=VMEM,
        compiler_params=PARAMS,
        name="slot_grad",
    )(near_slot, far, weights[0], weights[1])
    slot_own, slot_recv = to_expert(slot_grad)
    gate_grad, up_grad, down_grad, prob_grad = pl.pallas_call(
        weight_grad_kernel,
        out_shape=(grad_shape,) * 3 + (jax.ShapeDtypeStruct((1, rows // fsdp), F32),),
        in_specs=[VMEM] * 7 + [HBM] * 3,
        out_specs=(HBM,) * 3 + (VMEM,),
        scratch_shapes=held(9),
        input_output_aliases={7 + i: i for i in range(3)},
        compiler_params=PARAMS,
        cost_estimate=pl.CostEstimate(
            flops=4 * rows * features * hidden, bytes_accessed=9 * features * hidden, transcendentals=0
        ),
        name="weight_grads",
    )(*near, far, tok_t, grad_t, *grads)

    token_grad = pl.pallas_call(
        token_grad_kernel,
        out_shape=jax.ShapeDtypeStruct((features, token_count), BF16),
        in_specs=[VMEM] * 3,
        out_specs=HBM,
        scratch_shapes=[pltpu.VMEM((4, features, token_count // 4), BF16), pltpu.SemaphoreType.DMA((4,))],
        compiler_params=PARAMS,
        name="token_grad",
    )(slot_own, slot_recv, onehot).T
    return (token_grad, gate_grad, up_grad, down_grad, prob_grad)


def solution(mesh):
    return jax.shard_map(
        local,
        mesh=mesh,
        in_specs=(
            P("expert", "fsdp"),
            P("expert", "fsdp"),
            P("expert", None, None),
            P("expert", None),
            P("expert", None),
            P("expert", "fsdp", None),
            P("expert", "fsdp", None),
            P("expert", "fsdp", None),
        ),
        out_specs=(
            P("expert", "fsdp"),
            P("expert", "fsdp", None),
            P("expert", "fsdp", None),
            P("expert", "fsdp", None),
            P("expert", "fsdp"),
        ),
        check_vma=False,
    )
```

time: 43 us -> 37.5 us (0.87)
  waiting for transfers between devices: 16.6 us -> 10.3 us
  Pallas kernels: 10.7 us -> 11.4 us
    ppermute x9, waiting for transfers between devices: 16.5 us -> 10.1 us  [swap(): return lax.ppermute(x, 'fsdp', [(i, i ^ mask) for i in range(fsdp)])]
    pallas_call x6 -> x7, Pallas kernels: 5.31 us -> 6.06 us  [the longest x1 2.86 us: local(): pl.pallas_call(weight_grad_kernel, out_shape=(grad_shape,) * 3 + (jax.Sha...]
  transfers between devices with their start and end apart: 11 -> 11, of which waited for: 10 -> 10; matrix products, arithmetic and copies ran while one was open for 0% -> 0% of each run, Pallas kernels for 14% -> 19%
where the time goes in v3:
time: 37.5 us; the launch traced here: 37.3 us
  starting transfers between devices  14.6 us (39%)
  Pallas kernels  11.4 us (30%)
  waiting for transfers between devices  10.3 us (27%)
  between operations  0.84 us (2%)
    ppermute x9, waiting for transfers between devices, swap(): return lax.ppermute(x, 'fsdp', [(i, i ^ mask) for i in range(fsdp)])  10.1 us
    ppermute x9, starting transfers between devices, swap(): return lax.ppermute(x, 'fsdp', [(i, i ^ mask) for i in range(fsdp)])  10.1 us
    ppermute x2, starting transfers between devices, to_expert(): return (x[0], lax.ppermute(x[1], 'expert', [(0, 1), (1, 0)])[None])  4.46 us
    pallas_call x1, Pallas kernels, local(): pl.pallas_call(weight_grad_kernel, out_shape=(grad_shape,) * 3 + (jax.Sha...  2.86 us
    pallas_call x1, Pallas kernels, local(): pl.pallas_call(gather_kernel, out_shape=(jax.ShapeDtypeStruct((experts, 2...  1.93 us
    pallas_call x1, Pallas kernels, local(): pl.pallas_call(load_kernel, out_shape=(jax.ShapeDtypeStruct((features, hi...  1.82 us
    pallas_call x1, Pallas kernels, local(): pl.pallas_call(near_kernel, out_shape=(jax.ShapeDtypeStruct((rows, featur...  1.37 us
    pallas_call x1, Pallas kernels, local(): pl.pallas_call(token_grad_kernel, out_shape=jax.ShapeDtypeStruct((feature...  1.16 us
  transfers between devices with their start and end apart: 11, of which 10 were waited for; matrix products, arithmetic and copies ran while one was open for 0% of the time, Pallas kernels for 19%

profile of v3, /device:TPU:0, one launch (start us, length us, event | category | flops | bytes accessed | tf_op | source)
XLA Modules:
  0.0 37.3 jit_solution(559953629907590028)
XLA Ops:
  0.6 1.9 %gather_rows.1 = (bf16[2,2,24,320]{3,2,1,0:T(8,128)(2,1)S(1)}, bf16[48,1024]{1,0:T(8,128)(2,1)S(1)}) custom-call(s32[2,24]{1,0:T(2,128)} %bitcast.46, bf16[320,1024]{1,0:T(8,128)(2,1)} %bitcast.44, bf16[320,1024]{1,0:T(8,128)(2,1)} %bitcast.45), custom_call_target="tpu_custom_call" | custom-call | tf_op jit(solution)/shard_map/gather_rows/pallas_call | solution.py:273
  2.6 3.0 %collective-permute-start = (bf16[2,24,320]{2,1,0:T(8,128)(2,1)S(1)}, bf16[2,24,320]{2,1,0:T(8,128)(2,1)S(1)}, u32[]{:S(2)}, u32[]{:S(2)}) collective-permute-start(bf16[2,24,320]{2,1,0:T(8,128)(2,1)S(1)} %get-tuple-element.55), channel_id=1, source_target_pairs={{0,1},{1,0},{2,3},{3,2},{4,5},{5,4},{6,7},{7,6},{8,9},{9,8},{10,11... | collective-permute-start | bytes 92168 | tf_op jit(solution)/shard_map/ppermute | solution.py:269
  5.6 1.8 %load_weights.1 = (bf16[320,1536]{1,0:T(8,128)(2,1)S(1)}, bf16[320,1536]{1,0:T(8,128)(2,1)S(1)}, bf16[320,1536]{1,0:T(8,128)(2,1)S(1)}) custom-call(bf16[2,24,320]{2,1,0:T(8,128)(2,1)S(1)} %get-tuple-element.56.own.after, bf16[1,320,1536]{2,1,0:T(8,128)(2,1)} %w_gate.1, bf16[1,320,1536]{2,1,0:T(8,128)(2,1)} %w_up.1, bf16[1,320,1536]{2,1,0:T(8,128)(2,1)} %w_down.1), custom_call_target="tpu_custom_call" | custom-call | bytes 2949120 | tf_op jit(solution)/shard_map/load_weights/pallas_call | solution.py:292
  7.4 0.1 collective-permute-done
  7.5 0.4 %partial_sums.3 = f32[4,72,384]{2,1,0:T(8,128)S(1)} custom-call(bf16[2,24,320]{2,1,0:T(8,128)(2,1)S(1)} %get-tuple-element.56.own.after, bf16[1,2,24,320]{3,2,1,0:T(8,128)(2,1)S(1)} %bitcast.38, bf16[320,1536]{1,0:T(8,128)(2,1)S(1)} %get-tuple-element.32.w_gate, bf16[320,1536]{1,0:T(8,128)(2,1)S(1)} %get-tuple-element.33.w_up, ...), custom_call_target="tpu_custom_call" | custom-call | flops 70778880 | bytes 1474560 | tf_op jit(solution)/shard_map/partial_sums/pallas_call | solution.py:304
  7.9 0.1 collective-permute-start.1
  8.0 0.4 %partial_sums.2.kept = f32[4,72,384]{2,1,0:T(8,128)S(1)} custom-call(bf16[2,24,320]{2,1,0:T(8,128)(2,1)S(1)} %get-tuple-element.56.own.after, bf16[1,2,24,320]{3,2,1,0:T(8,128)(2,1)S(1)} %bitcast.39, bf16[320,1536]{1,0:T(8,128)(2,1)S(1)} %get-tuple-element.32.w_gate, bf16[320,1536]{1,0:T(8,128)(2,1)S(1)} %get-tuple-element.33.w_up, ...), custom_call_target="tpu_custom_call" | custom-call | flops 70778880 | bytes 1474560 | tf_op jit(solution)/shard_map/partial_sums/pallas_call | solution.py:304
  8.4 0.0 copy-start
  8.4 0.0 copy-start.1
  8.4 1.4 %collective-permute-done.1.arrived = f32[4,72,384]{2,1,0:T(8,128)S(1)} collective-permute-done((f32[4,72,384]{2,1,0:T(8,128)S(1)}, f32[4,72,384]{2,1,0:T(8,128)S(1)}, u32[]{:S(2)}, u32[]{:S(2)}) %collective-permute-start.1) | collective-permute-done | bytes 442400 | tf_op jit(solution)/shard_map/ppermute | solution.py:265
  9.8 0.2 add.35
  10.0 3.1 %collective-permute-start.4 = (f16[80,384]{1,0:T(8,128)(2,1)S(1)}, f16[80,384]{1,0:T(8,128)(2,1)S(1)}, u32[]{:S(2)}, u32[]{:S(2)}) collective-permute-start(f16[80,384]{1,0:T(8,128)(2,1)S(1)} %convert_element_type.26), channel_id=1, source_target_pairs={{0,12},{2,14},{4,8},{6,10},{8,4},{10,6},{12,0},{14,2},{16,28},{18,... | collective-permute-start | bytes 184328 | tf_op jit(solution)/shard_map/ppermute | solution.py:265
  13.1 0.5 %collective-permute-start.3 = (f16[80,384]{1,0:T(8,128)(2,1)S(1)}, f16[80,384]{1,0:T(8,128)(2,1)S(1)}, u32[]{:S(2)}, u32[]{:S(2)}) collective-permute-start(f16[80,384]{1,0:T(8,128)(2,1)S(1)} %convert_element_type.24), channel_id=1, source_target_pairs={{0,8},{2,10},{4,12},{6,14},{8,0},{10,2},{12,4},{14,6},{16,24},{18,... | collective-permute-start | bytes 184328 | tf_op jit(solution)/shard_map/ppermute | solution.py:265
  13.6 0.1 collective-permute-start.2
  13.8 1.6 %collective-permute-done.4 = f16[80,384]{1,0:T(8,128)(2,1)S(1)} collective-permute-done((f16[80,384]{1,0:T(8,128)(2,1)S(1)}, f16[80,384]{1,0:T(8,128)(2,1)S(1)}, u32[]{:S(2)}, u32[]{:S(2)}) %collective-permute-start.4) | collective-permute-done | bytes 61472 | tf_op jit(solution)/shard_map/ppermute | solution.py:265
  15.4 2.0 %collective-permute-done.3 = f16[80,384]{1,0:T(8,128)(2,1)S(1)} collective-permute-done((f16[80,384]{1,0:T(8,128)(2,1)S(1)}, f16[80,384]{1,0:T(8,128)(2,1)S(1)}, u32[]{:S(2)}, u32[]{:S(2)}) %collective-permute-start.3) | collective-permute-done | bytes 61472 | tf_op jit(solution)/shard_map/ppermute | solution.py:265
  17.4 0.4 %collective-permute-done.2 = f16[80,384]{1,0:T(8,128)(2,1)S(1)} collective-permute-done((f16[80,384]{1,0:T(8,128)(2,1)S(1)}, f16[80,384]{1,0:T(8,128)(2,1)S(1)}, u32[]{:S(2)}, u32[]{:S(2)}) %collective-permute-start.2) | collective-permute-done | bytes 61472 | tf_op jit(solution)/shard_map/ppermute | solution.py:265
  17.9 0.1 fusion.3
  18.0 2.7 %collective-permute-start.5 = (f16[80,384]{1,0:T(8,128)(2,1)S(1)}, f16[80,384]{1,0:T(8,128)(2,1)S(1)}, u32[]{:S(2)}, u32[]{:S(2)}) collective-permute-start(f16[80,384]{1,0:T(8,128)(2,1)S(1)} %pad_maximum_fusion.1), channel_id=1, source_target_pairs={{0,16},{2,18},{4,20},{6,22},{8,24},{10,26},{12,28},{14,30},{16,0},... | collective-permute-start | bytes 184328 | tf_op jit(solution)/shard_map/ppermute | solution.py:265
  20.7 0.0 copy-done
  20.7 0.0 copy-done.1
  20.7 0.7 %row_facts.1 = (bf16[320,48]{1,0:T(8,128)(2,1)S(1)}, bf16[320,48]{1,0:T(8,128)(2,1)S(1)}, f32[24,128]{1,0:T(8,128)S(1)}, f32[24,128]{1,0:T(8,128)S(1)}, f32[24,128]{1,0:T(8,128)S(1)}) custom-call(s32[2]{0:T(128)S(1)} %bitcast.42, bf16[2,24,320]{2,1,0:T(8,128)(2,1)S(1)} %get-tuple-element.56.own.after, bf16[1,2,24,320]{3,2,1,0:T(8,128)(2,1)S(1)} %bitcast.40, ...), custom_call_target="tpu_custom_call" | custom-call | bytes 122880 | tf_op jit(solution)/shard_map/row_facts/pallas_call | solution.py:321
  21.4 1.8 %collective-permute-done.5 = f16[80,384]{1,0:T(8,128)(2,1)S(1)} collective-permute-done((f16[80,384]{1,0:T(8,128)(2,1)S(1)}, f16[80,384]{1,0:T(8,128)(2,1)S(1)}, u32[]{:S(2)}, u32[]{:S(2)}) %collective-permute-start.5) | collective-permute-done | bytes 61472 | tf_op jit(solution)/shard_map/ppermute | solution.py:265
  23.2 0.2 hidden.1.near0
  23.4 1.6 %collective-permute-start.8 = (bf16[80,384]{1,0:T(8,128)(2,1)S(1)}, bf16[80,384]{1,0:T(8,128)(2,1)S(1)}, u32[]{:S(2)}, u32[]{:S(2)}) collective-permute-start(bf16[80,384]{1,0:T(8,128)(2,1)S(1)} %hidden.1.near0), channel_id=1, source_target_pairs={{0,12},{2,14},{4,8},{6,10},{8,4},{10,6},{12,0},{14,2},{16,28},{18,... | collective-permute-start | bytes 184328 | tf_op jit(solution)/shard_map/ppermute | solution.py:265
  25.0 0.6 %collective-permute-start.7 = (bf16[80,384]{1,0:T(8,128)(2,1)S(1)}, bf16[80,384]{1,0:T(8,128)(2,1)S(1)}, u32[]{:S(2)}, u32[]{:S(2)}) collective-permute-start(bf16[80,384]{1,0:T(8,128)(2,1)S(1)} %hidden.1.near0), channel_id=1, source_target_pairs={{0,8},{2,10},{4,12},{6,14},{8,0},{10,2},{12,4},{14,6},{16,24},{18,... | collective-permute-start | bytes 184328 | tf_op jit(solution)/shard_map/ppermute | solution.py:265
  25.6 1.4 %collective-permute-start.6 = (bf16[80,384]{1,0:T(8,128)(2,1)S(1)}, bf16[80,384]{1,0:T(8,128)(2,1)S(1)}, u32[]{:S(2)}, u32[]{:S(2)}) collective-permute-start(bf16[80,384]{1,0:T(8,128)(2,1)S(1)} %hidden.1.near0), channel_id=1, source_target_pairs={{0,4},{2,6},{4,0},{6,2},{8,12},{10,14},{12,8},{14,10},{16,20},{18,... | collective-permute-start | bytes 184328 | tf_op jit(solution)/shard_map/ppermute | solution.py:265
  27.0 1.6 %collective-permute-done.8.near3 = bf16[80,384]{1,0:T(8,128)(2,1)S(1)} collective-permute-done((bf16[80,384]{1,0:T(8,128)(2,1)S(1)}, bf16[80,384]{1,0:T(8,128)(2,1)S(1)}, u32[]{:S(2)}, u32[]{:S(2)}) %collective-permute-start.8) | collective-permute-done | bytes 61472 | tf_op jit(solution)/shard_map/ppermute | solution.py:265
  28.6 0.6 %collective-permute-done.7.near2 = bf16[80,384]{1,0:T(8,128)(2,1)S(1)} collective-permute-done((bf16[80,384]{1,0:T(8,128)(2,1)S(1)}, bf16[80,384]{1,0:T(8,128)(2,1)S(1)}, u32[]{:S(2)}, u32[]{:S(2)}) %collective-permute-start.7) | collective-permute-done | bytes 61472 | tf_op jit(solution)/shard_map/ppermute | solution.py:265
  29.2 0.6 %collective-permute-done.6.near1 = bf16[80,384]{1,0:T(8,128)(2,1)S(1)} collective-permute-done((bf16[80,384]{1,0:T(8,128)(2,1)S(1)}, bf16[80,384]{1,0:T(8,128)(2,1)S(1)}, u32[]{:S(2)}, u32[]{:S(2)}) %collective-permute-start.6) | collective-permute-done | bytes 61472 | tf_op jit(solution)/shard_map/ppermute | solution.py:265
  29.8 0.1 collective-permute-start.9
  29.9 1.4 %near_piece.1 = (f32[48,320]{1,0:T(8,128)S(1)}, f32[1,320,1536]{2,1,0:T(8,128)}, f32[1,320,1536]{2,1,0:T(8,128)}, f32[1,320,1536]{2,1,0:T(8,128)}) custom-call(bf16[80,384]{1,0:T(8,128)(2,1)S(1)} %hidden.1.near0, bf16[80,384]{1,0:T(8,128)(2,1)S(1)} %collective-permute-done.6.near1, bf16[80,384]{1,0:T(8,128)(2,1)S(1)} %collective-permute-done.7.near2, ...), custom_call_target="tpu_custom_call" | custom-call | flops 94371840 | bytes 1474560 | tf_op jit(solution)/shard_map/near_piece/pallas_call | solution.py:368
  31.3 0.1 collective-permute-done.9.far
  31.4 0.4 %slot_grad.1 = bf16[2,24,320]{2,1,0:T(8,128)(2,1)S(1)} custom-call(f32[48,320]{1,0:T(8,128)S(1)} %get-tuple-element.42.before, bf16[4,80,384]{2,1,0:T(8,128)(2,1)S(1)} %collective-permute-done.9.far, bf16[320,1536]{1,0:T(8,128)(2,1)S(1)} %get-tuple-element.32.w_gate, bf16[320,1536]{1,0:T(8,128)(2,1)S(1)} %get-tuple-element.33.w_up), custom_call_target="tpu_custom_call" | custom-call | tf_op jit(solution)/shard_map/slot_grad/pallas_call | solution.py:380
  31.9 1.5 %collective-permute-start.10 = (bf16[24,320]{1,0:T(8,128)(2,1)S(1)}, bf16[24,320]{1,0:T(8,128)(2,1)S(1)}, u32[]{:S(2)}, u32[]{:S(2)}) collective-permute-start(bf16[24,320]{1,0:T(8,128)(2,1)S(1)} %get-tuple-element.57), channel_id=1, source_target_pairs={{0,1},{1,0},{2,3},{3,2},{4,5},{5,4},{6,7},{7,6},{8,9},{9,8},{10,11... | collective-permute-start | bytes 46088 | tf_op jit(solution)/shard_map/ppermute | solution.py:269
  33.3 2.9 %weight_grads.1 = (f32[1,320,1536]{2,1,0:T(8,128)}, f32[1,320,1536]{2,1,0:T(8,128)}, f32[1,320,1536]{2,1,0:T(8,128)}, f32[1,3]{1,0:T(1,128)}) custom-call(bf16[80,384]{1,0:T(8,128)(2,1)S(1)} %hidden.1.near0, bf16[80,384]{1,0:T(8,128)(2,1)S(1)} %collective-permute-done.6.near1, ...), custom_call_target="tpu_custom_call", output_to_operand_aliasing={{0}: (7, {}), {1}: (8, {}), {2}: (9, {})} | custom-call | flops 94371840 | bytes 4423680 | tf_op jit(solution)/shard_map/weight_grads/pallas_call | solution.py:389
  36.2 0.0 collective-permute-done.10
  36.2 1.2 %token_grad.1 = bf16[320,1024]{1,0:T(8,128)(2,1)} custom-call(bf16[24,320]{1,0:T(8,128)(2,1)S(1)} %get-tuple-element.58.own, bf16[1,24,320]{2,1,0:T(8,128)(2,1)S(1)} %bitcast.41, bf16[48,1024]{1,0:T(8,128)(2,1)S(1)} %get-tuple-element.43.onehot), custom_call_target="tpu_custom_call" | custom-call | tf_op jit(solution)/shard_map/token_grad/pallas_call | solution.py:403
  (18 shorter events, 0.2 us)
Async XLA Ops:
  2.6 4.9 %collective-permute-start = (bf16[2,24,320]{2,1,0:T(8,128)(2,1)S(1)}, bf16[2,24,320]{2,1,0:T(8,128)(2,1)S(1)}, u32[]{:S(2)}, u32[]{:S(2)}) collective-permute-start(bf16[2,24,320]{2,1,0:T(8,128)(2,1)S(1)} %get-tuple-element.55), channel_id=1, source_target_pairs={{0,1},{1,0},{2,3},{3,2},{4,5},{5,4},{6,7},{7,6},{8,9},{9,8},{10,11... | collective-permute-start | bytes 92168 | tf_op jit(solution)/shard_map/ppermute | solution.py:269
  7.9 1.9 %collective-permute-start.1 = (f32[4,72,384]{2,1,0:T(8,128)S(1)}, f32[4,72,384]{2,1,0:T(8,128)S(1)}, u32[]{:S(2)}, u32[]{:S(2)}) collective-permute-start(f32[4,72,384]{2,1,0:T(8,128)S(1)} %partial_sums.3), channel_id=1, source_target_pairs={{0,2},{2,0},{4,6},{6,4},{8,10},{10,8},{12,14},{14,12},{16,18},{18,... | collective-permute-start | bytes 1327112 | tf_op jit(solution)/shard_map/ppermute | solution.py:265
  8.4 12.3 %copy-start = (s32[1,2]{1,0:T(1,128)S(1)}, s32[1,2]{1,0:T(1,128)}, u32[]{:S(2)}) copy-start(s32[1,2]{1,0:T(1,128)} %param.11) | copy-start | bytes 28
  8.4 12.3 %copy-start.1 = (f32[1,48]{1,0:T(1,128)S(1)}, f32[1,48]{1,0:T(1,128)}, u32[]{:S(2)}) copy-start(f32[1,48]{1,0:T(1,128)} %prob.1) | copy-start | bytes 580
  10.0 5.4 %collective-permute-start.4 = (f16[80,384]{1,0:T(8,128)(2,1)S(1)}, f16[80,384]{1,0:T(8,128)(2,1)S(1)}, u32[]{:S(2)}, u32[]{:S(2)}) collective-permute-start(f16[80,384]{1,0:T(8,128)(2,1)S(1)} %convert_element_type.26), channel_id=1, source_target_pairs={{0,12},{2,14},{4,8},{6,10},{8,4},{10,6},{12,0},{14,2},{16,28},{18,... | collective-permute-start | bytes 184328 | tf_op jit(solution)/shard_map/ppermute | solution.py:265
  13.1 4.3 %collective-permute-start.3 = (f16[80,384]{1,0:T(8,128)(2,1)S(1)}, f16[80,384]{1,0:T(8,128)(2,1)S(1)}, u32[]{:S(2)}, u32[]{:S(2)}) collective-permute-start(f16[80,384]{1,0:T(8,128)(2,1)S(1)} %convert_element_type.24), channel_id=1, source_target_pairs={{0,8},{2,10},{4,12},{6,14},{8,0},{10,2},{12,4},{14,6},{16,24},{18,... | collective-permute-start | bytes 184328 | tf_op jit(solution)/shard_map/ppermute | solution.py:265
  13.6 4.2 %collective-permute-start.2 = (f16[80,384]{1,0:T(8,128)(2,1)S(1)}, f16[80,384]{1,0:T(8,128)(2,1)S(1)}, u32[]{:S(2)}, u32[]{:S(2)}) collective-permute-start(f16[80,384]{1,0:T(8,128)(2,1)S(1)} %convert_element_type.22), channel_id=1, source_target_pairs={{0,4},{2,6},{4,0},{6,2},{8,12},{10,14},{12,8},{14,10},{16,20},{18,... | collective-permute-start | bytes 184328 | tf_op jit(solution)/shard_map/ppermute | solution.py:265
  18.0 5.2 %collective-permute-start.5 = (f16[80,384]{1,0:T(8,128)(2,1)S(1)}, f16[80,384]{1,0:T(8,128)(2,1)S(1)}, u32[]{:S(2)}, u32[]{:S(2)}) collective-permute-start(f16[80,384]{1,0:T(8,128)(2,1)S(1)} %pad_maximum_fusion.1), channel_id=1, source_target_pairs={{0,16},{2,18},{4,20},{6,22},{8,24},{10,26},{12,28},{14,30},{16,0},... | collective-permute-start | bytes 184328 | tf_op jit(solution)/shard_map/ppermute | solution.py:265
  23.4 5.2 %collective-permute-start.8 = (bf16[80,384]{1,0:T(8,128)(2,1)S(1)}, bf16[80,384]{1,0:T(8,128)(2,1)S(1)}, u32[]{:S(2)}, u32[]{:S(2)}) collective-permute-start(bf16[80,384]{1,0:T(8,128)(2,1)S(1)} %hidden.1.near0), channel_id=1, source_target_pairs={{0,12},{2,14},{4,8},{6,10},{8,4},{10,6},{12,0},{14,2},{16,28},{18,... | collective-permute-start | bytes 184328 | tf_op jit(solution)/shard_map/ppermute | solution.py:265
  25.0 4.2 %collective-permute-start.7 = (bf16[80,384]{1,0:T(8,128)(2,1)S(1)}, bf16[80,384]{1,0:T(8,128)(2,1)S(1)}, u32[]{:S(2)}, u32[]{:S(2)}) collective-permute-start(bf16[80,384]{1,0:T(8,128)(2,1)S(1)} %hidden.1.near0), channel_id=1, source_target_pairs={{0,8},{2,10},{4,12},{6,14},{8,0},{10,2},{12,4},{14,6},{16,24},{18,... | collective-permute-start | bytes 184328 | tf_op jit(solution)/shard_map/ppermute | solution.py:265
  25.6 4.2 %collective-permute-start.6 = (bf16[80,384]{1,0:T(8,128)(2,1)S(1)}, bf16[80,384]{1,0:T(8,128)(2,1)S(1)}, u32[]{:S(2)}, u32[]{:S(2)}) collective-permute-start(bf16[80,384]{1,0:T(8,128)(2,1)S(1)} %hidden.1.near0), channel_id=1, source_target_pairs={{0,4},{2,6},{4,0},{6,2},{8,12},{10,14},{12,8},{14,10},{16,20},{18,... | collective-permute-start | bytes 184328 | tf_op jit(solution)/shard_map/ppermute | solution.py:265
  29.8 1.6 %collective-permute-start.9 = (bf16[4,80,384]{2,1,0:T(8,128)(2,1)S(1)}, bf16[4,80,384]{2,1,0:T(8,128)(2,1)S(1)}, u32[]{:S(2)}, u32[]{:S(2)}) collective-permute-start(bf16[4,80,384]{2,1,0:T(8,128)(2,1)S(1)} %pad_maximum_fusion), channel_id=1, source_target_pairs={{0,2},{2,0},{4,6},{6,4},{8,10},{10,8},{12,14},{14,12},{16,18},{18,... | collective-permute-start | bytes 737288 | tf_op jit(solution)/shard_map/ppermute | solution.py:265
  31.9 4.3 %collective-permute-start.10 = (bf16[24,320]{1,0:T(8,128)(2,1)S(1)}, bf16[24,320]{1,0:T(8,128)(2,1)S(1)}, u32[]{:S(2)}, u32[]{:S(2)}) collective-permute-start(bf16[24,320]{1,0:T(8,128)(2,1)S(1)} %get-tuple-element.57), channel_id=1, source_target_pairs={{0,1},{1,0},{2,3},{3,2},{4,5},{5,4},{6,7},{7,6},{8,9},{9,8},{10,11... | collective-permute-start | bytes 46088 | tf_op jit(solution)/shard_map/ppermute | solution.py:269

commit v4 on v3

--- a/solution.py
+++ b/solution.py
@@ -29,6 +29,16 @@
     return pl.multiple_of((half * 2 + (((me >> 1) & 1) ^ jy)) * width, 128)
 
 
+def place_in_half(jy, width):
+    return pl.multiple_of((((lax.axis_index("fsdp") >> 1) & 1) ^ jy) * width, 128)
+
+
+def half_copies(side, weights, to, sems):
+    width = to.shape[2]
+    at = pl.ds(pl.multiple_of(((lax.axis_index("fsdp") & 1) ^ side) * width, 128), width)
+    return [pltpu.make_async_copy(w.at[0, :, at], to.at[i], sems.at[i]) for i, w in enumerate(weights)]
+
+
 def row_part():
     return (lax.axis_index("fsdp") >> 2) & 1
 
@@ -37,12 +47,14 @@
     return lax.axis_index("expert") if experts == 2 else 0
 
 
-def gather_kernel(slot_rows_hbm, tokens_hbm, grads_hbm, rows_out, onehot_out, slot_rows, tokens_t, grads_t, onehot_f, sems):
+def gather_kernel(slot_rows_hbm, tokens_hbm, grads_hbm, *refs):
+    weights, (rows_out, onehot_out, far_out, slot_rows, tokens_t, grads_t, onehot_f, sems, far_sems) = refs[:3], refs[3:]
     copies = [
         pltpu.make_async_copy(source, to, sems.at[i])
         for i, (source, to) in enumerate(((slot_rows_hbm, slot_rows), (tokens_hbm, tokens_t), (grads_hbm, grads_t)))
     ]
-    for copy in copies:
+    far_copies = half_copies(1, weights, far_out, far_sems)
+    for copy in copies + far_copies:
         copy.start()
     experts, slots = slot_rows.shape
     count = tokens_t.shape[1]
@@ -64,14 +76,13 @@
         rows = dot(onehot, source[...], (1, 1))
         for j in range(experts):
             rows_out[j, kind] = rows[j * slots : (j + 1) * slots].astype(BF16)
-
-
-def load_kernel(after, w_gate, w_up, w_down, gate_out, up_out, down_out, sems):
+    for copy in far_copies:
+        copy.wait()
+
+
+def load_kernel(after, w_gate, w_up, w_down, out, sems):
     del after
-    copies = [
-        pltpu.make_async_copy(w.at[0], to, sems.at[i])
-        for i, (w, to) in enumerate(((w_gate, gate_out), (w_up, up_out), (w_down, down_out)))
-    ]
+    copies = half_copies(0, (w_gate, w_up, w_down), out, sems)
     for copy in copies:
         copy.start()
     for copy in copies:
@@ -83,13 +94,16 @@
     return jnp.concatenate([block.astype(F32) for block in blocks], axis=0)
 
 
-def partial_kernel(side, own, recv, w_gate, w_up, w_down, out):
-    tok, grad = stacked_rows(own, recv, 0).astype(BF16), stacked_rows(own, recv, 1).astype(BF16)
+def partial_sums(own, recv, weights, width, jy, q):
+    rows = stacked_rows(own, recv, q // 2).astype(BF16)
+    return dot(rows, weights[q, :, pl.ds(place_in_half(jy, width), width)], (1, 0))
+
+
+def partial_kernel(own, recv, weights, out):
     chunk_rows, width = out.shape[1] // 3, out.shape[2]
     for jy in range(2):
-        at = pl.ds(place(side, jy, width), width)
-        for q, (x, w) in enumerate(((tok, w_gate), (tok, w_up), (grad, w_down))):
-            sums = dot(x, w[:, at], (1, 0))
+        for q in range(3):
+            sums = partial_sums(own, recv, weights, width, jy, q)
             for part in range(2):
                 chunk = (row_part() ^ part) * 2 + jy
                 out[chunk, pl.ds(q * chunk_rows, chunk_rows), :] = sums[part * chunk_rows : (part + 1) * chunk_rows]
@@ -123,10 +137,12 @@
     diagonal_out[...] = diagonal.astype(F32)
 
 
-def add_kernel(kept, arrived, first, power_out, *outs):
+def add_kernel(kept, own, recv, weights, first, power_out, *refs):
+    outs, summed = refs[:-1], refs[-1]
+    partial_kernel(own, recv, weights, summed)
     rows = first.shape[0] // 3
     width = first.shape[1]
-    chunks = [kept[j] + arrived[j] for j in range(4)]
+    chunks = [kept[j] + summed[j] for j in range(4)]
     first[...] = chunks[0]
     powers = []
     for q in range(3):
@@ -181,10 +197,10 @@
     return [x.astype(BF16) for x in both]
 
 
-def slot_part(a, b, w_gate, w_up, column):
+def slot_part(a, b, weights, jy):
     _, gate_act_grad, up_act_grad = parts(a, b)
-    at = pl.ds(column, a.shape[1])
-    return dot(gate_act_grad, w_gate[:, at], (1, 1)) + dot(up_act_grad, w_up[:, at], (1, 1))
+    at = pl.ds(place_in_half(jy, a.shape[1]), a.shape[1])
+    return dot(gate_act_grad, weights[0, :, at], (1, 1)) + dot(up_act_grad, weights[1, :, at], (1, 1))
 
 
 def weight_grad_copies(pieces, tok_t, grad_t, outs, held, sems):
@@ -199,23 +215,20 @@
     return copies
 
 
-def near_kernel(near0, near1, near2, near3, w_gate, w_up, tok_t, grad_t, out, gate_grad, up_grad, down_grad, held, sems):
+def near_kernel(near0, near1, near2, near3, weights, tok_t, grad_t, out, gate_grad, up_grad, down_grad, held, sems):
     width = near0.shape[1]
     pieces = [(near0, near2, place(0, 0, width))]
     copies = weight_grad_copies(pieces, tok_t, grad_t, (gate_grad, up_grad, down_grad), held, sems)
-    out[...] = slot_part(near0, near2, w_gate, w_up, place(0, 0, width)) + slot_part(
-        near1, near3, w_gate, w_up, place(0, 1, width)
-    )
+    out[...] = slot_part(near0, near2, weights, 0) + slot_part(near1, near3, weights, 1)
     for copy in copies:
         copy.wait()
 
 
-def slot_kernel(before, far, w_gate, w_up, out):
-    width = far.shape[2]
+def slot_kernel(before, far, weights, out):
     experts, slots, _ = out.shape
     total = before[...]
     for jy in range(2):
-        total += slot_part(far.at[jy], far.at[2 + jy], w_gate, w_up, place(1, jy, width))
+        total += slot_part(far.at[jy], far.at[2 + jy], weights, jy)
     for part in range(2):
         for j in range(experts // 2):
             start = (part * (experts // 2) + j) * slots
@@ -270,51 +283,56 @@
         moved = lax.all_to_all(x, "expert", split_axis=0, concat_axis=0, tiled=True)
         return moved[0], moved[1:]
 
-    rows_out, onehot = pl.pallas_call(
+    half_shape = jax.ShapeDtypeStruct((3, features, half), BF16)
+    rows_out, onehot, far_weights = pl.pallas_call(
         gather_kernel,
         out_shape=(
             jax.ShapeDtypeStruct((experts, 2, slots, features), BF16),
             jax.ShapeDtypeStruct((rows, token_count), BF16),
-        ),
-        in_specs=[HBM] * 3,
-        out_specs=(VMEM, VMEM),
+            half_shape,
+        ),
+        in_specs=[HBM] * 6,
+        out_specs=(VMEM,) * 3,
         scratch_shapes=[
             pltpu.SMEM((experts, slots), jnp.int32),
             pltpu.VMEM((features, token_count), BF16),
             pltpu.VMEM((features, token_count), BF16),
             pltpu.VMEM((rows, token_count), F32),
             pltpu.SemaphoreType.DMA((3,)),
+            pltpu.SemaphoreType.DMA((3,)),
         ],
         compiler_params=PARAMS,
         name="gather_rows",
-    )(*(in_hbm(x) for x in (slot_rows[0], tokens.T, out_grad.T)))
+    )(*(in_hbm(x) for x in (slot_rows[0], tokens.T, out_grad.T, w_gate, w_up, w_down)))
     own, recv = to_expert(rows_out)
-    weights = pl.pallas_call(
+    if experts == 2:
+        crossed = [(f * 2 + x, (f ^ 1) * 2 + 1 - x) for f in range(fsdp) for x in range(2)]
+        other_recv = lax.ppermute(rows_out[1], ("fsdp", "expert"), crossed)[None]
+    else:
+        other_recv = swap(recv, 0)
+    other_own = swap(own, 0)
+    other_weights = swap(far_weights, 0)
+    near_weights = pl.pallas_call(
         load_kernel,
-        out_shape=(jax.ShapeDtypeStruct((features, hidden), BF16),) * 3,
+        out_shape=half_shape,
         in_specs=[VMEM] + [HBM] * 3,
-        out_specs=(VMEM,) * 3,
+        out_specs=VMEM,
         scratch_shapes=[pltpu.SemaphoreType.DMA((3,))],
         compiler_params=PARAMS,
-        cost_estimate=pl.CostEstimate(flops=0, bytes_accessed=6 * features * hidden, transcendentals=0),
+        cost_estimate=pl.CostEstimate(flops=0, bytes_accessed=6 * features * half, transcendentals=0),
         name="load_weights",
     )(own, *(in_hbm(w) for w in (w_gate, w_up, w_down)))
-
-    def partial(side):
-        return pl.pallas_call(
-            functools.partial(partial_kernel, side),
-            out_shape=jax.ShapeDtypeStruct((4, 3 * rows // 2, quarter), F32),
-            in_specs=[VMEM] * 5,
-            out_specs=VMEM,
-            compiler_params=PARAMS,
-            cost_estimate=pl.CostEstimate(
-                flops=6 * rows * features * half, bytes_accessed=3 * features * half * 2, transcendentals=0
-            ),
-            name="partial_sums",
-        )(own, recv, *weights)
-
-    arrived = swap(partial(1), 0)
-    kept = partial(0)
+    kept = pl.pallas_call(
+        partial_kernel,
+        out_shape=jax.ShapeDtypeStruct((4, 3 * rows // 2, quarter), F32),
+        in_specs=[VMEM] * 3,
+        out_specs=VMEM,
+        compiler_params=PARAMS,
+        cost_estimate=pl.CostEstimate(
+            flops=6 * rows * features * half, bytes_accessed=6 * features * half, transcendentals=0
+        ),
+        name="partial_sums",
+    )(own, recv, near_weights)
     turned_shape = jax.ShapeDtypeStruct((features, rows), BF16)
     fact_shape = jax.ShapeDtypeStruct((rows // 2, 128), F32)
     diagonal_shape = jax.ShapeDtypeStruct((rows // 2, (rows + 127) // 128 * 128), F32)
@@ -335,11 +353,12 @@
             jax.ShapeDtypeStruct((8, quarter), F32),
         )
         + (coded_shape,) * 3,
-        in_specs=[VMEM] * 2,
+        in_specs=[VMEM] * 4,
         out_specs=(VMEM,) * 5,
-        compiler_params=PARAMS,
-        name="add",
-    )(kept, arrived)
+        scratch_shapes=[pltpu.VMEM(kept.shape, F32)],
+        compiler_params=PARAMS,
+        name="add_other_core",
+    )(kept, other_own, other_recv, other_weights)
     arrived = [swap(x.astype(F16), *bits) for x, bits in zip(sent, ((1,), (2,), (1, 2)))]
     for x in arrived:
         chunk, its_power = decoded(x)
@@ -368,7 +387,7 @@
     near_slot, *grads = pl.pallas_call(
         near_kernel,
         out_shape=(jax.ShapeDtypeStruct((rows, features), F32),) + (grad_shape,) * 3,
-        in_specs=[VMEM] * 8,
+        in_specs=[VMEM] * 7,
         out_specs=(VMEM,) + (HBM,) * 3,
         scratch_shapes=held(3),
         compiler_params=PARAMS,
@@ -376,15 +395,15 @@
             flops=4 * rows * features * hidden, bytes_accessed=3 * features * hidden, transcendentals=0
         ),
         name="near_piece",
-    )(*near, weights[0], weights[1], tok_t, grad_t)
+    )(*near, near_weights, tok_t, grad_t)
     slot_grad = pl.pallas_call(
         slot_kernel,
         out_shape=jax.ShapeDtypeStruct((experts, slots, features), BF16),
-        in_specs=[VMEM] * 4,
+        in_specs=[VMEM] * 3,
         out_specs=VMEM,
         compiler_params=PARAMS,
         name="slot_grad",
-    )(near_slot, far, weights[0], weights[1])
+    )(near_slot, far, far_weights)
     slot_own, slot_recv = to_expert(slot_grad)
     gate_grad, up_grad, down_grad, prob_grad = pl.pallas_call(
         weight_grad_kernel,

time: 37.5 us -> 36.5 us (0.973)
  Pallas kernels: 11.4 us -> 10.9 us
  waiting for transfers between devices: 10.3 us -> 9.88 us
    ppermute x9 -> x10, waiting for transfers between devices: 10.1 us -> 8.47 us  [swap(): return lax.ppermute(x, 'fsdp', [(i, i ^ mask) for i in range(fsdp)])]
    ppermute x0 -> x1, waiting for transfers between devices: none -> 0.87 us  [local(): other_recv = lax.ppermute(rows_out[1], ('fsdp', 'expert'), crossed)[None]]
    pallas_call x3 -> x2, Pallas kernels: 2.59 us -> 1.73 us  [the longest x1 1.35 us: local(): pl.pallas_call(load_kernel, out_shape=half_shape, in_specs=[VMEM] + [HBM]...]
    ppermute x2, starting transfers between devices: 4.46 us -> 3.79 us  [to_expert(): return (x[0], lax.ppermute(x[1], 'expert', [(0, 1), (1, 0)])[None])]
    ppermute x2, waiting for transfers between devices: 0.12 us -> 0.55 us  [to_expert(): return (x[0], lax.ppermute(x[1], 'expert', [(0, 1), (1, 0)])[None])]
    pallas_call x1, Pallas kernels: 0.17 us -> 0.57 us  [local(): pl.pallas_call(add_kernel, out_shape=(jax.ShapeDtypeStruct((3 * rows // 2...]
    ppermute x9 -> x10, starting transfers between devices: 10.1 us -> 10.5 us  [swap(): return lax.ppermute(x, 'fsdp', [(i, i ^ mask) for i in range(fsdp)])]
  transfers between devices with their start and end apart: 11 -> 13, of which waited for: 10 -> 10; matrix products, arithmetic and copies ran while one was open for 0% -> 0% of each run, Pallas kernels for 19% -> 18%
where the time goes in v4:
time: 36.5 us; the launch traced here: 36.4 us
  starting transfers between devices  14.4 us (39%)
  Pallas kernels  10.9 us (30%)
  waiting for transfers between devices  9.88 us (27%)
  between operations  0.83 us (2%)
    ppermute x10, starting transfers between devices, swap(): return lax.ppermute(x, 'fsdp', [(i, i ^ mask) for i in range(fsdp)])  10.5 us
    ppermute x10, waiting for transfers between devices, swap(): return lax.ppermute(x, 'fsdp', [(i, i ^ mask) for i in range(fsdp)])  8.47 us
    ppermute x2, starting transfers between devices, to_expert(): return (x[0], lax.ppermute(x[1], 'expert', [(0, 1), (1, 0)])[None])  3.79 us
    pallas_call x1, Pallas kernels, local(): pl.pallas_call(weight_grad_kernel, out_shape=(grad_shape,) * 3 + (jax.Sha...  2.86 us
    pallas_call x1, Pallas kernels, local(): pl.pallas_call(gather_kernel, out_shape=(jax.ShapeDtypeStruct((experts, 2...  1.96 us
    pallas_call x1, Pallas kernels, local(): pl.pallas_call(near_kernel, out_shape=(jax.ShapeDtypeStruct((rows, featur...  1.36 us
    pallas_call x1, Pallas kernels, local(): pl.pallas_call(load_kernel, out_shape=half_shape, in_specs=[VMEM] + [HBM]...  1.35 us
    pallas_call x1, Pallas kernels, local(): pl.pallas_call(token_grad_kernel, out_shape=jax.ShapeDtypeStruct((feature...  1.16 us
  transfers between devices with their start and end apart: 13, of which 10 were waited for; matrix products, arithmetic and copies ran while one was open for 0% of the time, Pallas kernels for 18%

profile of v4, /device:TPU:0, one launch (start us, length us, event | category | flops | bytes accessed | tf_op | source)
XLA Modules:
  0.0 36.4 jit_solution(13151367664568802959)
XLA Ops:
  0.6 2.0 %gather_rows.1 = (bf16[2,2,24,320]{3,2,1,0:T(8,128)(2,1)S(1)}, bf16[48,1024]{1,0:T(8,128)(2,1)S(1)}, bf16[3,320,768]{2,1,0:T(8,128)(2,1)S(1)}) custom-call(s32[2,24]{1,0:T(2,128)} %bitcast.47, bf16[320,1024]{1,0:T(8,128)(2,1)} %bitcast.44, bf16[320,1024]{1,0:T(8,128)(2,1)} %bitcast.45, bf16[1,320,1536]{2,1,0:T(8,128)(2,1)} %w_gate.1, ...), custom_call_target="tpu_custom_call" | custom-call | tf_op jit(solution)/shard_map/gather_rows/pallas_call | solution.py:287
  2.6 0.5 %collective-permute-start.3 = (bf16[3,320,768]{2,1,0:T(8,128)(2,1)S(1)}, bf16[3,320,768]{2,1,0:T(8,128)(2,1)S(1)}, u32[]{:S(2)}, u32[]{:S(2)}) collective-permute-start(bf16[3,320,768]{2,1,0:T(8,128)(2,1)S(1)} %get-tuple-element.30.weights), channel_id=1, source_target_pairs={{0,2},{2,0},{4,6},{6,4},{8,10},{10,8},{12,14},{14,12},{16,18},{18,... | collective-permute-start | bytes 4423688 | tf_op jit(solution)/shard_map/ppermute | solution.py:278
  3.1 2.6 %collective-permute-start = (bf16[2,24,320]{2,1,0:T(8,128)(2,1)S(1)}, bf16[2,24,320]{2,1,0:T(8,128)(2,1)S(1)}, u32[]{:S(2)}, u32[]{:S(2)}) collective-permute-start(bf16[2,24,320]{2,1,0:T(8,128)(2,1)S(1)} %get-tuple-element.51), channel_id=1, source_target_pairs={{0,1},{1,0},{2,3},{3,2},{4,5},{5,4},{6,7},{7,6},{8,9},{9,8},{10,11... | collective-permute-start | bytes 92168 | tf_op jit(solution)/shard_map/ppermute | solution.py:282
  5.7 0.2 collective-permute-start.2
  5.9 0.1 collective-permute-start.1
  5.9 1.4 %load_weights.1.weights = bf16[3,320,768]{2,1,0:T(8,128)(2,1)S(1)} custom-call(bf16[2,24,320]{2,1,0:T(8,128)(2,1)S(1)} %get-tuple-element.52.own.after, bf16[1,320,1536]{2,1,0:T(8,128)(2,1)} %w_gate.1, bf16[1,320,1536]{2,1,0:T(8,128)(2,1)} %w_up.1, bf16[1,320,1536]{2,1,0:T(8,128)(2,1)} %w_down.1), custom_call_target="tpu_custom_call" | custom-call | bytes 1474560 | tf_op jit(solution)/shard_map/load_weights/pallas_call | solution.py:315
  7.3 0.5 %collective-permute-done = bf16[2,24,320]{2,1,0:T(8,128)(2,1)S(1)} collective-permute-done((bf16[2,24,320]{2,1,0:T(8,128)(2,1)S(1)}, bf16[2,24,320]{2,1,0:T(8,128)(2,1)S(1)}, u32[]{:S(2)}, u32[]{:S(2)}) %collective-permute-start) | collective-permute-done | bytes 30752 | tf_op jit(solution)/shard_map/ppermute | solution.py:282
  7.8 0.4 %partial_sums.1.kept = f32[4,72,384]{2,1,0:T(8,128)S(1)} custom-call(bf16[2,24,320]{2,1,0:T(8,128)(2,1)S(1)} %get-tuple-element.52.own.after, bf16[1,2,24,320]{3,2,1,0:T(8,128)(2,1)S(1)} %bitcast.39, bf16[3,320,768]{2,1,0:T(8,128)(2,1)S(1)} %load_weights.1.weights), custom_call_target="tpu_custom_call" | custom-call | flops 70778880 | bytes 1474560 | tf_op jit(solution)/shard_map/partial_sums/pallas_call | solution.py:325
  8.2 0.9 %collective-permute-done.2 = bf16[2,24,320]{2,1,0:T(8,128)(2,1)S(1)} collective-permute-done((bf16[2,24,320]{2,1,0:T(8,128)(2,1)S(1)}, bf16[2,24,320]{2,1,0:T(8,128)(2,1)S(1)}, u32[]{:S(2)}, u32[]{:S(2)}) %collective-permute-start.2) | collective-permute-done | bytes 30752 | tf_op jit(solution)/shard_map/ppermute | solution.py:310
  9.1 0.0 collective-permute-done.1.own
  9.1 0.0 collective-permute-done.3.weights
  9.1 0.0 copy-start
  9.1 0.0 copy-start.1
  9.1 0.6 %add_other_core.1 = (f32[72,384]{1,0:T(8,128)S(1)}, f32[8,384]{1,0:T(8,128)S(1)}, f32[80,384]{1,0:T(8,128)S(1)}, f32[80,384]{1,0:T(8,128)S(1)}, f32[80,384]{1,0:T(8,128)S(1)}) custom-call(f32[4,72,384]{2,1,0:T(8,128)S(1)} %partial_sums.1.kept, bf16[2,24,320]{2,1,0:T(8,128)(2,1)S(1)} %collective-permute-done.1.own, bf16[1,2,24,320]{3,2,1,0:T(8,128)(2,1)S(1)} %bitcast.41, ...), custom_call_target="tpu_custom_call" | custom-call | tf_op jit(solution)/shard_map/add_other_core/pallas_call | solution.py:349
  9.7 2.6 %collective-permute-start.6 = (f16[80,384]{1,0:T(8,128)(2,1)S(1)}, f16[80,384]{1,0:T(8,128)(2,1)S(1)}, u32[]{:S(2)}, u32[]{:S(2)}) collective-permute-start(f16[80,384]{1,0:T(8,128)(2,1)S(1)} %convert_element_type.26), channel_id=1, source_target_pairs={{0,12},{2,14},{4,8},{6,10},{8,4},{10,6},{12,0},{14,2},{16,28},{18,... | collective-permute-start | bytes 184328 | tf_op jit(solution)/shard_map/ppermute | solution.py:278
  12.3 0.5 %collective-permute-start.5 = (f16[80,384]{1,0:T(8,128)(2,1)S(1)}, f16[80,384]{1,0:T(8,128)(2,1)S(1)}, u32[]{:S(2)}, u32[]{:S(2)}) collective-permute-start(f16[80,384]{1,0:T(8,128)(2,1)S(1)} %convert_element_type.24), channel_id=1, source_target_pairs={{0,8},{2,10},{4,12},{6,14},{8,0},{10,2},{12,4},{14,6},{16,24},{18,... | collective-permute-start | bytes 184328 | tf_op jit(solution)/shard_map/ppermute | solution.py:278
  12.9 0.5 %collective-permute-start.4 = (f16[80,384]{1,0:T(8,128)(2,1)S(1)}, f16[80,384]{1,0:T(8,128)(2,1)S(1)}, u32[]{:S(2)}, u32[]{:S(2)}) collective-permute-start(f16[80,384]{1,0:T(8,128)(2,1)S(1)} %convert_element_type.22), channel_id=1, source_target_pairs={{0,4},{2,6},{4,0},{6,2},{8,12},{10,14},{12,8},{14,10},{16,20},{18,... | collective-permute-start | bytes 184328 | tf_op jit(solution)/shard_map/ppermute | solution.py:278
  13.4 1.6 %collective-permute-done.6 = f16[80,384]{1,0:T(8,128)(2,1)S(1)} collective-permute-done((f16[80,384]{1,0:T(8,128)(2,1)S(1)}, f16[80,384]{1,0:T(8,128)(2,1)S(1)}, u32[]{:S(2)}, u32[]{:S(2)}) %collective-permute-start.6) | collective-permute-done | bytes 61472 | tf_op jit(solution)/shard_map/ppermute | solution.py:278
  15.0 1.6 %collective-permute-done.5 = f16[80,384]{1,0:T(8,128)(2,1)S(1)} collective-permute-done((f16[80,384]{1,0:T(8,128)(2,1)S(1)}, f16[80,384]{1,0:T(8,128)(2,1)S(1)}, u32[]{:S(2)}, u32[]{:S(2)}) %collective-permute-start.5) | collective-permute-done | bytes 61472 | tf_op jit(solution)/shard_map/ppermute | solution.py:278
  16.7 0.4 %collective-permute-done.4 = f16[80,384]{1,0:T(8,128)(2,1)S(1)} collective-permute-done((f16[80,384]{1,0:T(8,128)(2,1)S(1)}, f16[80,384]{1,0:T(8,128)(2,1)S(1)}, u32[]{:S(2)}, u32[]{:S(2)}) %collective-permute-start.4) | collective-permute-done | bytes 61472 | tf_op jit(solution)/shard_map/ppermute | solution.py:278
  17.1 0.1 fusion.3
  17.2 2.7 %collective-permute-start.7 = (f16[80,384]{1,0:T(8,128)(2,1)S(1)}, f16[80,384]{1,0:T(8,128)(2,1)S(1)}, u32[]{:S(2)}, u32[]{:S(2)}) collective-permute-start(f16[80,384]{1,0:T(8,128)(2,1)S(1)} %pad_maximum_fusion.1), channel_id=1, source_target_pairs={{0,16},{2,18},{4,20},{6,22},{8,24},{10,26},{12,28},{14,30},{16,0},... | collective-permute-start | bytes 184328 | tf_op jit(solution)/shard_map/ppermute | solution.py:278
  19.9 0.0 copy-done
  19.9 0.0 copy-done.1
  19.9 0.7 %row_facts.1 = (bf16[320,48]{1,0:T(8,128)(2,1)S(1)}, bf16[320,48]{1,0:T(8,128)(2,1)S(1)}, f32[24,128]{1,0:T(8,128)S(1)}, f32[24,128]{1,0:T(8,128)S(1)}, f32[24,128]{1,0:T(8,128)S(1)}) custom-call(s32[2]{0:T(128)S(1)} %bitcast.43, bf16[2,24,320]{2,1,0:T(8,128)(2,1)S(1)} %get-tuple-element.52.own.after, bf16[1,2,24,320]{3,2,1,0:T(8,128)(2,1)S(1)} %bitcast.40, ...), custom_call_target="tpu_custom_call" | custom-call | bytes 122880 | tf_op jit(solution)/shard_map/row_facts/pallas_call | solution.py:339
  20.6 1.8 %collective-permute-done.7 = f16[80,384]{1,0:T(8,128)(2,1)S(1)} collective-permute-done((f16[80,384]{1,0:T(8,128)(2,1)S(1)}, f16[80,384]{1,0:T(8,128)(2,1)S(1)}, u32[]{:S(2)}, u32[]{:S(2)}) %collective-permute-start.7) | collective-permute-done | bytes 61472 | tf_op jit(solution)/shard_map/ppermute | solution.py:278
  22.5 0.2 hidden.1.near0
  22.6 1.6 %collective-permute-start.10 = (bf16[80,384]{1,0:T(8,128)(2,1)S(1)}, bf16[80,384]{1,0:T(8,128)(2,1)S(1)}, u32[]{:S(2)}, u32[]{:S(2)}) collective-permute-start(bf16[80,384]{1,0:T(8,128)(2,1)S(1)} %hidden.1.near0), channel_id=1, source_target_pairs={{0,12},{2,14},{4,8},{6,10},{8,4},{10,6},{12,0},{14,2},{16,28},{18,... | collective-permute-start | bytes 184328 | tf_op jit(solution)/shard_map/ppermute | solution.py:278
  24.3 0.5 %collective-permute-start.9 = (bf16[80,384]{1,0:T(8,128)(2,1)S(1)}, bf16[80,384]{1,0:T(8,128)(2,1)S(1)}, u32[]{:S(2)}, u32[]{:S(2)}) collective-permute-start(bf16[80,384]{1,0:T(8,128)(2,1)S(1)} %hidden.1.near0), channel_id=1, source_target_pairs={{0,8},{2,10},{4,12},{6,14},{8,0},{10,2},{12,4},{14,6},{16,24},{18,... | collective-permute-start | bytes 184328 | tf_op jit(solution)/shard_map/ppermute | solution.py:278
  24.8 1.4 %collective-permute-start.8 = (bf16[80,384]{1,0:T(8,128)(2,1)S(1)}, bf16[80,384]{1,0:T(8,128)(2,1)S(1)}, u32[]{:S(2)}, u32[]{:S(2)}) collective-permute-start(bf16[80,384]{1,0:T(8,128)(2,1)S(1)} %hidden.1.near0), channel_id=1, source_target_pairs={{0,4},{2,6},{4,0},{6,2},{8,12},{10,14},{12,8},{14,10},{16,20},{18,... | collective-permute-start | bytes 184328 | tf_op jit(solution)/shard_map/ppermute | solution.py:278
  26.2 1.6 %collective-permute-done.10.near3 = bf16[80,384]{1,0:T(8,128)(2,1)S(1)} collective-permute-done((bf16[80,384]{1,0:T(8,128)(2,1)S(1)}, bf16[80,384]{1,0:T(8,128)(2,1)S(1)}, u32[]{:S(2)}, u32[]{:S(2)}) %collective-permute-start.10) | collective-permute-done | bytes 61472 | tf_op jit(solution)/shard_map/ppermute | solution.py:278
  27.8 0.7 %collective-permute-done.9.near2 = bf16[80,384]{1,0:T(8,128)(2,1)S(1)} collective-permute-done((bf16[80,384]{1,0:T(8,128)(2,1)S(1)}, bf16[80,384]{1,0:T(8,128)(2,1)S(1)}, u32[]{:S(2)}, u32[]{:S(2)}) %collective-permute-start.9) | collective-permute-done | bytes 61472 | tf_op jit(solution)/shard_map/ppermute | solution.py:278
  28.5 0.5 %collective-permute-done.8.near1 = bf16[80,384]{1,0:T(8,128)(2,1)S(1)} collective-permute-done((bf16[80,384]{1,0:T(8,128)(2,1)S(1)}, bf16[80,384]{1,0:T(8,128)(2,1)S(1)}, u32[]{:S(2)}, u32[]{:S(2)}) %collective-permute-start.8) | collective-permute-done | bytes 61472 | tf_op jit(solution)/shard_map/ppermute | solution.py:278
  29.1 0.1 collective-permute-start.11
  29.2 1.4 %near_piece.1 = (f32[48,320]{1,0:T(8,128)S(1)}, f32[1,320,1536]{2,1,0:T(8,128)}, f32[1,320,1536]{2,1,0:T(8,128)}, f32[1,320,1536]{2,1,0:T(8,128)}) custom-call(bf16[80,384]{1,0:T(8,128)(2,1)S(1)} %hidden.1.near0, bf16[80,384]{1,0:T(8,128)(2,1)S(1)} %collective-permute-done.8.near1, bf16[80,384]{1,0:T(8,128)(2,1)S(1)} %collective-permute-done.9.near2, ...), custom_call_target="tpu_custom_call" | custom-call | flops 94371840 | bytes 1474560 | tf_op jit(solution)/shard_map/near_piece/pallas_call | solution.py:387
  30.6 0.1 collective-permute-done.11.far
  30.7 0.4 %slot_grad.1 = bf16[2,24,320]{2,1,0:T(8,128)(2,1)S(1)} custom-call(f32[48,320]{1,0:T(8,128)S(1)} %get-tuple-element.38.before, bf16[4,80,384]{2,1,0:T(8,128)(2,1)S(1)} %collective-permute-done.11.far, bf16[3,320,768]{2,1,0:T(8,128)(2,1)S(1)} %get-tuple-element.30.weights), custom_call_target="tpu_custom_call" | custom-call | tf_op jit(solution)/shard_map/slot_grad/pallas_call | solution.py:399
  31.1 1.2 %collective-permute-start.12 = (bf16[24,320]{1,0:T(8,128)(2,1)S(1)}, bf16[24,320]{1,0:T(8,128)(2,1)S(1)}, u32[]{:S(2)}, u32[]{:S(2)}) collective-permute-start(bf16[24,320]{1,0:T(8,128)(2,1)S(1)} %get-tuple-element.53), channel_id=1, source_target_pairs={{0,1},{1,0},{2,3},{3,2},{4,5},{5,4},{6,7},{7,6},{8,9},{9,8},{10,11... | collective-permute-start | bytes 46088 | tf_op jit(solution)/shard_map/ppermute | solution.py:282
  32.3 2.9 %weight_grads.1 = (f32[1,320,1536]{2,1,0:T(8,128)}, f32[1,320,1536]{2,1,0:T(8,128)}, f32[1,320,1536]{2,1,0:T(8,128)}, f32[1,3]{1,0:T(1,128)}) custom-call(bf16[80,384]{1,0:T(8,128)(2,1)S(1)} %hidden.1.near0, bf16[80,384]{1,0:T(8,128)(2,1)S(1)} %collective-permute-done.8.near1, ...), custom_call_target="tpu_custom_call", output_to_operand_aliasing={{0}: (7, {}), {1}: (8, {}), {2}: (9, {})} | custom-call | flops 94371840 | bytes 4423680 | tf_op jit(solution)/shard_map/weight_grads/pallas_call | solution.py:408
  35.2 0.0 collective-permute-done.12
  35.2 1.2 %token_grad.1 = bf16[320,1024]{1,0:T(8,128)(2,1)} custom-call(bf16[24,320]{1,0:T(8,128)(2,1)S(1)} %get-tuple-element.54.own, bf16[1,24,320]{2,1,0:T(8,128)(2,1)S(1)} %bitcast.42, bf16[48,1024]{1,0:T(8,128)(2,1)S(1)} %get-tuple-element.39.onehot), custom_call_target="tpu_custom_call" | custom-call | tf_op jit(solution)/shard_map/token_grad/pallas_call | solution.py:422
  (18 shorter events, 0.2 us)
Async XLA Ops:
  2.6 6.5 %collective-permute-start.3 = (bf16[3,320,768]{2,1,0:T(8,128)(2,1)S(1)}, bf16[3,320,768]{2,1,0:T(8,128)(2,1)S(1)}, u32[]{:S(2)}, u32[]{:S(2)}) collective-permute-start(bf16[3,320,768]{2,1,0:T(8,128)(2,1)S(1)} %get-tuple-element.30.weights), channel_id=1, source_target_pairs={{0,2},{2,0},{4,6},{6,4},{8,10},{10,8},{12,14},{14,12},{16,18},{18,... | collective-permute-start | bytes 4423688 | tf_op jit(solution)/shard_map/ppermute | solution.py:278
  3.1 4.7 %collective-permute-start = (bf16[2,24,320]{2,1,0:T(8,128)(2,1)S(1)}, bf16[2,24,320]{2,1,0:T(8,128)(2,1)S(1)}, u32[]{:S(2)}, u32[]{:S(2)}) collective-permute-start(bf16[2,24,320]{2,1,0:T(8,128)(2,1)S(1)} %get-tuple-element.51), channel_id=1, source_target_pairs={{0,1},{1,0},{2,3},{3,2},{4,5},{5,4},{6,7},{7,6},{8,9},{9,8},{10,11... | collective-permute-start | bytes 92168 | tf_op jit(solution)/shard_map/ppermute | solution.py:282
  5.7 3.4 %collective-permute-start.2 = (bf16[2,24,320]{2,1,0:T(8,128)(2,1)S(1)}, bf16[2,24,320]{2,1,0:T(8,128)(2,1)S(1)}, u32[]{:S(2)}, u32[]{:S(2)}) collective-permute-start(bf16[2,24,320]{2,1,0:T(8,128)(2,1)S(1)} %get-tuple-element.51), channel_id=1, source_target_pairs={{0,3},{1,2},{2,1},{3,0},{4,7},{5,6},{6,5},{7,4},{8,11},{9,10},{10,... | collective-permute-start | bytes 92168 | tf_op jit(solution)/shard_map/ppermute | solution.py:310
  5.9 3.2 %collective-permute-start.1 = (bf16[2,24,320]{2,1,0:T(8,128)(2,1)S(1)}, bf16[2,24,320]{2,1,0:T(8,128)(2,1)S(1)}, u32[]{:S(2)}, u32[]{:S(2)}) collective-permute-start(bf16[2,24,320]{2,1,0:T(8,128)(2,1)S(1)} %get-tuple-element.52.own.after), channel_id=1, source_target_pairs={{0,2},{2,0},{4,6},{6,4},{8,10},{10,8},{12,14},{14,12},{16,18},{18,... | collective-permute-start | bytes 92168 | tf_op jit(solution)/shard_map/ppermute | solution.py:278
  9.1 10.8 %copy-start = (s32[1,2]{1,0:T(1,128)S(1)}, s32[1,2]{1,0:T(1,128)}, u32[]{:S(2)}) copy-start(s32[1,2]{1,0:T(1,128)} %param.11) | copy-start | bytes 28
  9.1 10.8 %copy-start.1 = (f32[1,48]{1,0:T(1,128)S(1)}, f32[1,48]{1,0:T(1,128)}, u32[]{:S(2)}) copy-start(f32[1,48]{1,0:T(1,128)} %prob.1) | copy-start | bytes 580
  9.7 5.3 %collective-permute-start.6 = (f16[80,384]{1,0:T(8,128)(2,1)S(1)}, f16[80,384]{1,0:T(8,128)(2,1)S(1)}, u32[]{:S(2)}, u32[]{:S(2)}) collective-permute-start(f16[80,384]{1,0:T(8,128)(2,1)S(1)} %convert_element_type.26), channel_id=1, source_target_pairs={{0,12},{2,14},{4,8},{6,10},{8,4},{10,6},{12,0},{14,2},{16,28},{18,... | collective-permute-start | bytes 184328 | tf_op jit(solution)/shard_map/ppermute | solution.py:278
  12.3 4.3 %collective-permute-start.5 = (f16[80,384]{1,0:T(8,128)(2,1)S(1)}, f16[80,384]{1,0:T(8,128)(2,1)S(1)}, u32[]{:S(2)}, u32[]{:S(2)}) collective-permute-start(f16[80,384]{1,0:T(8,128)(2,1)S(1)} %convert_element_type.24), channel_id=1, source_target_pairs={{0,8},{2,10},{4,12},{6,14},{8,0},{10,2},{12,4},{14,6},{16,24},{18,... | collective-permute-start | bytes 184328 | tf_op jit(solution)/shard_map/ppermute | solution.py:278
  12.9 4.2 %collective-permute-start.4 = (f16[80,384]{1,0:T(8,128)(2,1)S(1)}, f16[80,384]{1,0:T(8,128)(2,1)S(1)}, u32[]{:S(2)}, u32[]{:S(2)}) collective-permute-start(f16[80,384]{1,0:T(8,128)(2,1)S(1)} %convert_element_type.22), channel_id=1, source_target_pairs={{0,4},{2,6},{4,0},{6,2},{8,12},{10,14},{12,8},{14,10},{16,20},{18,... | collective-permute-start | bytes 184328 | tf_op jit(solution)/shard_map/ppermute | solution.py:278
  17.2 5.2 %collective-permute-start.7 = (f16[80,384]{1,0:T(8,128)(2,1)S(1)}, f16[80,384]{1,0:T(8,128)(2,1)S(1)}, u32[]{:S(2)}, u32[]{:S(2)}) collective-permute-start(f16[80,384]{1,0:T(8,128)(2,1)S(1)} %pad_maximum_fusion.1), channel_id=1, source_target_pairs={{0,16},{2,18},{4,20},{6,22},{8,24},{10,26},{12,28},{14,30},{16,0},... | collective-permute-start | bytes 184328 | tf_op jit(solution)/shard_map/ppermute | solution.py:278
  22.6 5.2 %collective-permute-start.10 = (bf16[80,384]{1,0:T(8,128)(2,1)S(1)}, bf16[80,384]{1,0:T(8,128)(2,1)S(1)}, u32[]{:S(2)}, u32[]{:S(2)}) collective-permute-start(bf16[80,384]{1,0:T(8,128)(2,1)S(1)} %hidden.1.near0), channel_id=1, source_target_pairs={{0,12},{2,14},{4,8},{6,10},{8,4},{10,6},{12,0},{14,2},{16,28},{18,... | collective-permute-start | bytes 184328 | tf_op jit(solution)/shard_map/ppermute | solution.py:278
  24.3 4.2 %collective-permute-start.9 = (bf16[80,384]{1,0:T(8,128)(2,1)S(1)}, bf16[80,384]{1,0:T(8,128)(2,1)S(1)}, u32[]{:S(2)}, u32[]{:S(2)}) collective-permute-start(bf16[80,384]{1,0:T(8,128)(2,1)S(1)} %hidden.1.near0), channel_id=1, source_target_pairs={{0,8},{2,10},{4,12},{6,14},{8,0},{10,2},{12,4},{14,6},{16,24},{18,... | collective-permute-start | bytes 184328 | tf_op jit(solution)/shard_map/ppermute | solution.py:278
  24.8 4.2 %collective-permute-start.8 = (bf16[80,384]{1,0:T(8,128)(2,1)S(1)}, bf16[80,384]{1,0:T(8,128)(2,1)S(1)}, u32[]{:S(2)}, u32[]{:S(2)}) collective-permute-start(bf16[80,384]{1,0:T(8,128)(2,1)S(1)} %hidden.1.near0), channel_id=1, source_target_pairs={{0,4},{2,6},{4,0},{6,2},{8,12},{10,14},{12,8},{14,10},{16,20},{18,... | collective-permute-start | bytes 184328 | tf_op jit(solution)/shard_map/ppermute | solution.py:278
  29.1 1.6 %collective-permute-start.11 = (bf16[4,80,384]{2,1,0:T(8,128)(2,1)S(1)}, bf16[4,80,384]{2,1,0:T(8,128)(2,1)S(1)}, u32[]{:S(2)}, u32[]{:S(2)}) collective-permute-start(bf16[4,80,384]{2,1,0:T(8,128)(2,1)S(1)} %pad_maximum_fusion), channel_id=1, source_target_pairs={{0,2},{2,0},{4,6},{6,4},{8,10},{10,8},{12,14},{14,12},{16,18},{18,... | collective-permute-start | bytes 737288 | tf_op jit(solution)/shard_map/ppermute | solution.py:278
  31.1 4.1 %collective-permute-start.12 = (bf16[24,320]{1,0:T(8,128)(2,1)S(1)}, bf16[24,320]{1,0:T(8,128)(2,1)S(1)}, u32[]{:S(2)}, u32[]{:S(2)}) collective-permute-start(bf16[24,320]{1,0:T(8,128)(2,1)S(1)} %get-tuple-element.53), channel_id=1, source_target_pairs={{0,1},{1,0},{2,3},{3,2},{4,5},{5,4},{6,7},{7,6},{8,9},{9,8},{10,11... | collective-permute-start | bytes 46088 | tf_op jit(solution)/shard_map/ppermute | solution.py:282

commit v5 on v4

--- a/solution.py
+++ b/solution.py
@@ -236,7 +236,7 @@
 
 
 def weight_grad_kernel(near0, near1, near2, near3, far, tok_t, grad_t, *refs):
-    gate_grad, up_grad, down_grad, prob_out, held, sems = refs[3:]
+    gate_grad, up_grad, down_grad, prob_out, held, sems, prob_held, prob_sem = refs[3:]
     width = far.shape[2]
     pieces = [(near1, near3, place(0, 1, width))]
     pieces += [(far.at[jy], far.at[2 + jy], place(1, jy, width)) for jy in range(2)]
@@ -247,7 +247,9 @@
     prob = jnp.broadcast_to(tail[0:1] + tail[1:2], (8, width))
     share = prob_out.shape[1]
     shift = lax.rem(width - lax.axis_index("fsdp") * share, width)
-    prob_out[...] = pltpu.roll(prob, shift, 1)[:1, :share]
+    prob_held[...] = pltpu.roll(prob, shift, 1)[:1, :share]
+    copies.append(pltpu.make_async_copy(prob_held, prob_out, prob_sem))
+    copies[-1].start()
     for copy in copies:
         copy.wait()
 
@@ -409,8 +411,8 @@
         weight_grad_kernel,
         out_shape=(grad_shape,) * 3 + (jax.ShapeDtypeStruct((1, rows // fsdp), F32),),
         in_specs=[VMEM] * 7 + [HBM] * 3,
-        out_specs=(HBM,) * 3 + (VMEM,),
-        scratch_shapes=held(9),
+        out_specs=(HBM,) * 4,
+        scratch_shapes=held(9) + [pltpu.VMEM((1, rows // fsdp), F32), pltpu.SemaphoreType.DMA],
         input_output_aliases={7 + i: i for i in range(3)},
         compiler_params=PARAMS,
         cost_estimate=pl.CostEstimate(

time: 36.5 us -> 36.3 us (level)
  Pallas kernels: 10.9 us -> 10.4 us
    pallas_call x1, Pallas kernels: 2.86 us -> 2.36 us  [local(): pl.pallas_call(weight_grad_kernel, out_shape=(grad_shape,) * 3 + (jax.Sha...]
  transfers between devices with their start and end apart: 13 -> 13, of which waited for: 10 -> 11; matrix products, arithmetic and copies ran while one was open for 0% -> 0% of each run, Pallas kernels for 18% -> 17%
where the time goes in v5:
time: 36.3 us; the launch traced here: 36.1 us
  starting transfers between devices  14.4 us (40%)
  Pallas kernels  10.4 us (29%)
  waiting for transfers between devices  10.1 us (28%)
  between operations  0.82 us (2%)
    ppermute x10, starting transfers between devices, swap(): return lax.ppermute(x, 'fsdp', [(i, i ^ mask) for i in range(fsdp)])  10.5 us
    ppermute x10, waiting for transfers between devices, swap(): return lax.ppermute(x, 'fsdp', [(i, i ^ mask) for i in range(fsdp)])  8.47 us
    ppermute x2, starting transfers between devices, to_expert(): return (x[0], lax.ppermute(x[1], 'expert', [(0, 1), (1, 0)])[None])  3.79 us
    pallas_call x1, Pallas kernels, local(): pl.pallas_call(weight_grad_kernel, out_shape=(grad_shape,) * 3 + (jax.Sha...  2.36 us
    pallas_call x1, Pallas kernels, local(): pl.pallas_call(gather_kernel, out_shape=(jax.ShapeDtypeStruct((experts, 2...  1.96 us
    pallas_call x1, Pallas kernels, local(): pl.pallas_call(near_kernel, out_shape=(jax.ShapeDtypeStruct((rows, featur...  1.36 us
    pallas_call x1, Pallas kernels, local(): pl.pallas_call(load_kernel, out_shape=half_shape, in_specs=[VMEM] + [HBM]...  1.35 us
    pallas_call x1, Pallas kernels, local(): pl.pallas_call(token_grad_kernel, out_shape=jax.ShapeDtypeStruct((feature...  1.15 us
  transfers between devices with their start and end apart: 13, of which 11 were waited for; matrix products, arithmetic and copies ran while one was open for 0% of the time, Pallas kernels for 17%

profile of v5, /device:TPU:0, one launch (start us, length us, event | category | flops | bytes accessed | tf_op | source)
XLA Modules:
  0.0 36.1 jit_solution(8161099045413151814)
XLA Ops:
  0.6 2.0 %gather_rows.1 = (bf16[2,2,24,320]{3,2,1,0:T(8,128)(2,1)S(1)}, bf16[48,1024]{1,0:T(8,128)(2,1)S(1)}, bf16[3,320,768]{2,1,0:T(8,128)(2,1)S(1)}) custom-call(s32[2,24]{1,0:T(2,128)} %bitcast.47, bf16[320,1024]{1,0:T(8,128)(2,1)} %bitcast.44, bf16[320,1024]{1,0:T(8,128)(2,1)} %bitcast.45, bf16[1,320,1536]{2,1,0:T(8,128)(2,1)} %w_gate.1, ...), custom_call_target="tpu_custom_call" | custom-call | tf_op jit(solution)/shard_map/gather_rows/pallas_call | solution.py:289
  2.6 0.5 %collective-permute-start.3 = (bf16[3,320,768]{2,1,0:T(8,128)(2,1)S(1)}, bf16[3,320,768]{2,1,0:T(8,128)(2,1)S(1)}, u32[]{:S(2)}, u32[]{:S(2)}) collective-permute-start(bf16[3,320,768]{2,1,0:T(8,128)(2,1)S(1)} %get-tuple-element.30.weights), channel_id=1, source_target_pairs={{0,2},{2,0},{4,6},{6,4},{8,10},{10,8},{12,14},{14,12},{16,18},{18,... | collective-permute-start | bytes 4423688 | tf_op jit(solution)/shard_map/ppermute | solution.py:280
  3.1 2.6 %collective-permute-start = (bf16[2,24,320]{2,1,0:T(8,128)(2,1)S(1)}, bf16[2,24,320]{2,1,0:T(8,128)(2,1)S(1)}, u32[]{:S(2)}, u32[]{:S(2)}) collective-permute-start(bf16[2,24,320]{2,1,0:T(8,128)(2,1)S(1)} %get-tuple-element.51), channel_id=1, source_target_pairs={{0,1},{1,0},{2,3},{3,2},{4,5},{5,4},{6,7},{7,6},{8,9},{9,8},{10,11... | collective-permute-start | bytes 92168 | tf_op jit(solution)/shard_map/ppermute | solution.py:284
  5.7 0.2 collective-permute-start.2
  5.9 0.1 collective-permute-start.1
  5.9 1.4 %load_weights.1.weights = bf16[3,320,768]{2,1,0:T(8,128)(2,1)S(1)} custom-call(bf16[2,24,320]{2,1,0:T(8,128)(2,1)S(1)} %get-tuple-element.52.own.after, bf16[1,320,1536]{2,1,0:T(8,128)(2,1)} %w_gate.1, bf16[1,320,1536]{2,1,0:T(8,128)(2,1)} %w_up.1, bf16[1,320,1536]{2,1,0:T(8,128)(2,1)} %w_down.1), custom_call_target="tpu_custom_call" | custom-call | bytes 1474560 | tf_op jit(solution)/shard_map/load_weights/pallas_call | solution.py:317
  7.3 0.5 %collective-permute-done = bf16[2,24,320]{2,1,0:T(8,128)(2,1)S(1)} collective-permute-done((bf16[2,24,320]{2,1,0:T(8,128)(2,1)S(1)}, bf16[2,24,320]{2,1,0:T(8,128)(2,1)S(1)}, u32[]{:S(2)}, u32[]{:S(2)}) %collective-permute-start) | collective-permute-done | bytes 30752 | tf_op jit(solution)/shard_map/ppermute | solution.py:284
  7.8 0.4 %partial_sums.1.kept = f32[4,72,384]{2,1,0:T(8,128)S(1)} custom-call(bf16[2,24,320]{2,1,0:T(8,128)(2,1)S(1)} %get-tuple-element.52.own.after, bf16[1,2,24,320]{3,2,1,0:T(8,128)(2,1)S(1)} %bitcast.39, bf16[3,320,768]{2,1,0:T(8,128)(2,1)S(1)} %load_weights.1.weights), custom_call_target="tpu_custom_call" | custom-call | flops 70778880 | bytes 1474560 | tf_op jit(solution)/shard_map/partial_sums/pallas_call | solution.py:327
  8.2 0.9 %collective-permute-done.2 = bf16[2,24,320]{2,1,0:T(8,128)(2,1)S(1)} collective-permute-done((bf16[2,24,320]{2,1,0:T(8,128)(2,1)S(1)}, bf16[2,24,320]{2,1,0:T(8,128)(2,1)S(1)}, u32[]{:S(2)}, u32[]{:S(2)}) %collective-permute-start.2) | collective-permute-done | bytes 30752 | tf_op jit(solution)/shard_map/ppermute | solution.py:312
  9.1 0.0 collective-permute-done.1.own
  9.1 0.0 collective-permute-done.3.weights
  9.1 0.0 copy-start
  9.1 0.0 copy-start.1
  9.1 0.6 %add_other_core.1 = (f32[72,384]{1,0:T(8,128)S(1)}, f32[8,384]{1,0:T(8,128)S(1)}, f32[80,384]{1,0:T(8,128)S(1)}, f32[80,384]{1,0:T(8,128)S(1)}, f32[80,384]{1,0:T(8,128)S(1)}) custom-call(f32[4,72,384]{2,1,0:T(8,128)S(1)} %partial_sums.1.kept, bf16[2,24,320]{2,1,0:T(8,128)(2,1)S(1)} %collective-permute-done.1.own, bf16[1,2,24,320]{3,2,1,0:T(8,128)(2,1)S(1)} %bitcast.41, ...), custom_call_target="tpu_custom_call" | custom-call | tf_op jit(solution)/shard_map/add_other_core/pallas_call | solution.py:351
  9.7 2.6 %collective-permute-start.6 = (f16[80,384]{1,0:T(8,128)(2,1)S(1)}, f16[80,384]{1,0:T(8,128)(2,1)S(1)}, u32[]{:S(2)}, u32[]{:S(2)}) collective-permute-start(f16[80,384]{1,0:T(8,128)(2,1)S(1)} %convert_element_type.26), channel_id=1, source_target_pairs={{0,12},{2,14},{4,8},{6,10},{8,4},{10,6},{12,0},{14,2},{16,28},{18,... | collective-permute-start | bytes 184328 | tf_op jit(solution)/shard_map/ppermute | solution.py:280
  12.3 0.5 %collective-permute-start.5 = (f16[80,384]{1,0:T(8,128)(2,1)S(1)}, f16[80,384]{1,0:T(8,128)(2,1)S(1)}, u32[]{:S(2)}, u32[]{:S(2)}) collective-permute-start(f16[80,384]{1,0:T(8,128)(2,1)S(1)} %convert_element_type.24), channel_id=1, source_target_pairs={{0,8},{2,10},{4,12},{6,14},{8,0},{10,2},{12,4},{14,6},{16,24},{18,... | collective-permute-start | bytes 184328 | tf_op jit(solution)/shard_map/ppermute | solution.py:280
  12.9 0.5 %collective-permute-start.4 = (f16[80,384]{1,0:T(8,128)(2,1)S(1)}, f16[80,384]{1,0:T(8,128)(2,1)S(1)}, u32[]{:S(2)}, u32[]{:S(2)}) collective-permute-start(f16[80,384]{1,0:T(8,128)(2,1)S(1)} %convert_element_type.22), channel_id=1, source_target_pairs={{0,4},{2,6},{4,0},{6,2},{8,12},{10,14},{12,8},{14,10},{16,20},{18,... | collective-permute-start | bytes 184328 | tf_op jit(solution)/shard_map/ppermute | solution.py:280
  13.4 1.6 %collective-permute-done.6 = f16[80,384]{1,0:T(8,128)(2,1)S(1)} collective-permute-done((f16[80,384]{1,0:T(8,128)(2,1)S(1)}, f16[80,384]{1,0:T(8,128)(2,1)S(1)}, u32[]{:S(2)}, u32[]{:S(2)}) %collective-permute-start.6) | collective-permute-done | bytes 61472 | tf_op jit(solution)/shard_map/ppermute | solution.py:280
  15.0 1.6 %collective-permute-done.5 = f16[80,384]{1,0:T(8,128)(2,1)S(1)} collective-permute-done((f16[80,384]{1,0:T(8,128)(2,1)S(1)}, f16[80,384]{1,0:T(8,128)(2,1)S(1)}, u32[]{:S(2)}, u32[]{:S(2)}) %collective-permute-start.5) | collective-permute-done | bytes 61472 | tf_op jit(solution)/shard_map/ppermute | solution.py:280
  16.7 0.4 %collective-permute-done.4 = f16[80,384]{1,0:T(8,128)(2,1)S(1)} collective-permute-done((f16[80,384]{1,0:T(8,128)(2,1)S(1)}, f16[80,384]{1,0:T(8,128)(2,1)S(1)}, u32[]{:S(2)}, u32[]{:S(2)}) %collective-permute-start.4) | collective-permute-done | bytes 61472 | tf_op jit(solution)/shard_map/ppermute | solution.py:280
  17.1 0.1 fusion.3
  17.2 2.7 %collective-permute-start.7 = (f16[80,384]{1,0:T(8,128)(2,1)S(1)}, f16[80,384]{1,0:T(8,128)(2,1)S(1)}, u32[]{:S(2)}, u32[]{:S(2)}) collective-permute-start(f16[80,384]{1,0:T(8,128)(2,1)S(1)} %pad_maximum_fusion.1), channel_id=1, source_target_pairs={{0,16},{2,18},{4,20},{6,22},{8,24},{10,26},{12,28},{14,30},{16,0},... | collective-permute-start | bytes 184328 | tf_op jit(solution)/shard_map/ppermute | solution.py:280
  19.9 0.0 copy-done
  19.9 0.0 copy-done.1
  19.9 0.7 %row_facts.1 = (bf16[320,48]{1,0:T(8,128)(2,1)S(1)}, bf16[320,48]{1,0:T(8,128)(2,1)S(1)}, f32[24,128]{1,0:T(8,128)S(1)}, f32[24,128]{1,0:T(8,128)S(1)}, f32[24,128]{1,0:T(8,128)S(1)}) custom-call(s32[2]{0:T(128)S(1)} %bitcast.43, bf16[2,24,320]{2,1,0:T(8,128)(2,1)S(1)} %get-tuple-element.52.own.after, bf16[1,2,24,320]{3,2,1,0:T(8,128)(2,1)S(1)} %bitcast.40, ...), custom_call_target="tpu_custom_call" | custom-call | bytes 122880 | tf_op jit(solution)/shard_map/row_facts/pallas_call | solution.py:341
  20.6 1.8 %collective-permute-done.7 = f16[80,384]{1,0:T(8,128)(2,1)S(1)} collective-permute-done((f16[80,384]{1,0:T(8,128)(2,1)S(1)}, f16[80,384]{1,0:T(8,128)(2,1)S(1)}, u32[]{:S(2)}, u32[]{:S(2)}) %collective-permute-start.7) | collective-permute-done | bytes 61472 | tf_op jit(solution)/shard_map/ppermute | solution.py:280
  22.5 0.2 hidden.1.near0
  22.6 1.6 %collective-permute-start.10 = (bf16[80,384]{1,0:T(8,128)(2,1)S(1)}, bf16[80,384]{1,0:T(8,128)(2,1)S(1)}, u32[]{:S(2)}, u32[]{:S(2)}) collective-permute-start(bf16[80,384]{1,0:T(8,128)(2,1)S(1)} %hidden.1.near0), channel_id=1, source_target_pairs={{0,12},{2,14},{4,8},{6,10},{8,4},{10,6},{12,0},{14,2},{16,28},{18,... | collective-permute-start | bytes 184328 | tf_op jit(solution)/shard_map/ppermute | solution.py:280
  24.3 0.5 %collective-permute-start.9 = (bf16[80,384]{1,0:T(8,128)(2,1)S(1)}, bf16[80,384]{1,0:T(8,128)(2,1)S(1)}, u32[]{:S(2)}, u32[]{:S(2)}) collective-permute-start(bf16[80,384]{1,0:T(8,128)(2,1)S(1)} %hidden.1.near0), channel_id=1, source_target_pairs={{0,8},{2,10},{4,12},{6,14},{8,0},{10,2},{12,4},{14,6},{16,24},{18,... | collective-permute-start | bytes 184328 | tf_op jit(solution)/shard_map/ppermute | solution.py:280
  24.8 1.4 %collective-permute-start.8 = (bf16[80,384]{1,0:T(8,128)(2,1)S(1)}, bf16[80,384]{1,0:T(8,128)(2,1)S(1)}, u32[]{:S(2)}, u32[]{:S(2)}) collective-permute-start(bf16[80,384]{1,0:T(8,128)(2,1)S(1)} %hidden.1.near0), channel_id=1, source_target_pairs={{0,4},{2,6},{4,0},{6,2},{8,12},{10,14},{12,8},{14,10},{16,20},{18,... | collective-permute-start | bytes 184328 | tf_op jit(solution)/shard_map/ppermute | solution.py:280
  26.2 1.6 %collective-permute-done.10.near3 = bf16[80,384]{1,0:T(8,128)(2,1)S(1)} collective-permute-done((bf16[80,384]{1,0:T(8,128)(2,1)S(1)}, bf16[80,384]{1,0:T(8,128)(2,1)S(1)}, u32[]{:S(2)}, u32[]{:S(2)}) %collective-permute-start.10) | collective-permute-done | bytes 61472 | tf_op jit(solution)/shard_map/ppermute | solution.py:280
  27.8 0.7 %collective-permute-done.9.near2 = bf16[80,384]{1,0:T(8,128)(2,1)S(1)} collective-permute-done((bf16[80,384]{1,0:T(8,128)(2,1)S(1)}, bf16[80,384]{1,0:T(8,128)(2,1)S(1)}, u32[]{:S(2)}, u32[]{:S(2)}) %collective-permute-start.9) | collective-permute-done | bytes 61472 | tf_op jit(solution)/shard_map/ppermute | solution.py:280
  28.5 0.5 %collective-permute-done.8.near1 = bf16[80,384]{1,0:T(8,128)(2,1)S(1)} collective-permute-done((bf16[80,384]{1,0:T(8,128)(2,1)S(1)}, bf16[80,384]{1,0:T(8,128)(2,1)S(1)}, u32[]{:S(2)}, u32[]{:S(2)}) %collective-permute-start.8) | collective-permute-done | bytes 61472 | tf_op jit(solution)/shard_map/ppermute | solution.py:280
  29.1 0.1 collective-permute-start.11
  29.2 1.4 %near_piece.1 = (f32[48,320]{1,0:T(8,128)S(1)}, f32[1,320,1536]{2,1,0:T(8,128)}, f32[1,320,1536]{2,1,0:T(8,128)}, f32[1,320,1536]{2,1,0:T(8,128)}) custom-call(bf16[80,384]{1,0:T(8,128)(2,1)S(1)} %hidden.1.near0, bf16[80,384]{1,0:T(8,128)(2,1)S(1)} %collective-permute-done.8.near1, bf16[80,384]{1,0:T(8,128)(2,1)S(1)} %collective-permute-done.9.near2, ...), custom_call_target="tpu_custom_call" | custom-call | flops 94371840 | bytes 1474560 | tf_op jit(solution)/shard_map/near_piece/pallas_call | solution.py:389
  30.6 0.1 collective-permute-done.11.far
  30.7 0.4 %slot_grad.1 = bf16[2,24,320]{2,1,0:T(8,128)(2,1)S(1)} custom-call(f32[48,320]{1,0:T(8,128)S(1)} %get-tuple-element.38.before, bf16[4,80,384]{2,1,0:T(8,128)(2,1)S(1)} %collective-permute-done.11.far, bf16[3,320,768]{2,1,0:T(8,128)(2,1)S(1)} %get-tuple-element.30.weights), custom_call_target="tpu_custom_call" | custom-call | tf_op jit(solution)/shard_map/slot_grad/pallas_call | solution.py:401
  31.1 1.2 %collective-permute-start.12 = (bf16[24,320]{1,0:T(8,128)(2,1)S(1)}, bf16[24,320]{1,0:T(8,128)(2,1)S(1)}, u32[]{:S(2)}, u32[]{:S(2)}) collective-permute-start(bf16[24,320]{1,0:T(8,128)(2,1)S(1)} %get-tuple-element.53), channel_id=1, source_target_pairs={{0,1},{1,0},{2,3},{3,2},{4,5},{5,4},{6,7},{7,6},{8,9},{9,8},{10,11... | collective-permute-start | bytes 46088 | tf_op jit(solution)/shard_map/ppermute | solution.py:284
  32.3 2.4 %weight_grads.1 = (f32[1,320,1536]{2,1,0:T(8,128)}, f32[1,320,1536]{2,1,0:T(8,128)}, f32[1,320,1536]{2,1,0:T(8,128)}, f32[1,3]{1,0:T(1,128)}) custom-call(bf16[80,384]{1,0:T(8,128)(2,1)S(1)} %hidden.1.near0, bf16[80,384]{1,0:T(8,128)(2,1)S(1)} %collective-permute-done.8.near1, ...), custom_call_target="tpu_custom_call", output_to_operand_aliasing={{0}: (7, {}), {1}: (8, {}), {2}: (9, {})} | custom-call | flops 94371840 | bytes 4423680 | tf_op jit(solution)/shard_map/weight_grads/pallas_call | solution.py:410
  34.7 0.3 collective-permute-done.12
  35.0 1.2 %token_grad.1 = bf16[320,1024]{1,0:T(8,128)(2,1)} custom-call(bf16[24,320]{1,0:T(8,128)(2,1)S(1)} %get-tuple-element.54.own, bf16[1,24,320]{2,1,0:T(8,128)(2,1)S(1)} %bitcast.42, bf16[48,1024]{1,0:T(8,128)(2,1)S(1)} %get-tuple-element.39.onehot), custom_call_target="tpu_custom_call" | custom-call | tf_op jit(solution)/shard_map/token_grad/pallas_call | solution.py:424
  (18 shorter events, 0.2 us)
Async XLA Ops:
  2.6 6.5 %collective-permute-start.3 = (bf16[3,320,768]{2,1,0:T(8,128)(2,1)S(1)}, bf16[3,320,768]{2,1,0:T(8,128)(2,1)S(1)}, u32[]{:S(2)}, u32[]{:S(2)}) collective-permute-start(bf16[3,320,768]{2,1,0:T(8,128)(2,1)S(1)} %get-tuple-element.30.weights), channel_id=1, source_target_pairs={{0,2},{2,0},{4,6},{6,4},{8,10},{10,8},{12,14},{14,12},{16,18},{18,... | collective-permute-start | bytes 4423688 | tf_op jit(solution)/shard_map/ppermute | solution.py:280
  3.1 4.7 %collective-permute-start = (bf16[2,24,320]{2,1,0:T(8,128)(2,1)S(1)}, bf16[2,24,320]{2,1,0:T(8,128)(2,1)S(1)}, u32[]{:S(2)}, u32[]{:S(2)}) collective-permute-start(bf16[2,24,320]{2,1,0:T(8,128)(2,1)S(1)} %get-tuple-element.51), channel_id=1, source_target_pairs={{0,1},{1,0},{2,3},{3,2},{4,5},{5,4},{6,7},{7,6},{8,9},{9,8},{10,11... | collective-permute-start | bytes 92168 | tf_op jit(solution)/shard_map/ppermute | solution.py:284
  5.7 3.4 %collective-permute-start.2 = (bf16[2,24,320]{2,1,0:T(8,128)(2,1)S(1)}, bf16[2,24,320]{2,1,0:T(8,128)(2,1)S(1)}, u32[]{:S(2)}, u32[]{:S(2)}) collective-permute-start(bf16[2,24,320]{2,1,0:T(8,128)(2,1)S(1)} %get-tuple-element.51), channel_id=1, source_target_pairs={{0,3},{1,2},{2,1},{3,0},{4,7},{5,6},{6,5},{7,4},{8,11},{9,10},{10,... | collective-permute-start | bytes 92168 | tf_op jit(solution)/shard_map/ppermute | solution.py:312
  5.9 3.2 %collective-permute-start.1 = (bf16[2,24,320]{2,1,0:T(8,128)(2,1)S(1)}, bf16[2,24,320]{2,1,0:T(8,128)(2,1)S(1)}, u32[]{:S(2)}, u32[]{:S(2)}) collective-permute-start(bf16[2,24,320]{2,1,0:T(8,128)(2,1)S(1)} %get-tuple-element.52.own.after), channel_id=1, source_target_pairs={{0,2},{2,0},{4,6},{6,4},{8,10},{10,8},{12,14},{14,12},{16,18},{18,... | collective-permute-start | bytes 92168 | tf_op jit(solution)/shard_map/ppermute | solution.py:280
  9.1 10.8 %copy-start = (s32[1,2]{1,0:T(1,128)S(1)}, s32[1,2]{1,0:T(1,128)}, u32[]{:S(2)}) copy-start(s32[1,2]{1,0:T(1,128)} %param.11) | copy-start | bytes 28
  9.1 10.8 %copy-start.1 = (f32[1,48]{1,0:T(1,128)S(1)}, f32[1,48]{1,0:T(1,128)}, u32[]{:S(2)}) copy-start(f32[1,48]{1,0:T(1,128)} %prob.1) | copy-start | bytes 580
  9.7 5.3 %collective-permute-start.6 = (f16[80,384]{1,0:T(8,128)(2,1)S(1)}, f16[80,384]{1,0:T(8,128)(2,1)S(1)}, u32[]{:S(2)}, u32[]{:S(2)}) collective-permute-start(f16[80,384]{1,0:T(8,128)(2,1)S(1)} %convert_element_type.26), channel_id=1, source_target_pairs={{0,12},{2,14},{4,8},{6,10},{8,4},{10,6},{12,0},{14,2},{16,28},{18,... | collective-permute-start | bytes 184328 | tf_op jit(solution)/shard_map/ppermute | solution.py:280
  12.3 4.3 %collective-permute-start.5 = (f16[80,384]{1,0:T(8,128)(2,1)S(1)}, f16[80,384]{1,0:T(8,128)(2,1)S(1)}, u32[]{:S(2)}, u32[]{:S(2)}) collective-permute-start(f16[80,384]{1,0:T(8,128)(2,1)S(1)} %convert_element_type.24), channel_id=1, source_target_pairs={{0,8},{2,10},{4,12},{6,14},{8,0},{10,2},{12,4},{14,6},{16,24},{18,... | collective-permute-start | bytes 184328 | tf_op jit(solution)/shard_map/ppermute | solution.py:280
  12.9 4.2 %collective-permute-start.4 = (f16[80,384]{1,0:T(8,128)(2,1)S(1)}, f16[80,384]{1,0:T(8,128)(2,1)S(1)}, u32[]{:S(2)}, u32[]{:S(2)}) collective-permute-start(f16[80,384]{1,0:T(8,128)(2,1)S(1)} %convert_element_type.22), channel_id=1, source_target_pairs={{0,4},{2,6},{4,0},{6,2},{8,12},{10,14},{12,8},{14,10},{16,20},{18,... | collective-permute-start | bytes 184328 | tf_op jit(solution)/shard_map/ppermute | solution.py:280
  17.2 5.2 %collective-permute-start.7 = (f16[80,384]{1,0:T(8,128)(2,1)S(1)}, f16[80,384]{1,0:T(8,128)(2,1)S(1)}, u32[]{:S(2)}, u32[]{:S(2)}) collective-permute-start(f16[80,384]{1,0:T(8,128)(2,1)S(1)} %pad_maximum_fusion.1), channel_id=1, source_target_pairs={{0,16},{2,18},{4,20},{6,22},{8,24},{10,26},{12,28},{14,30},{16,0},... | collective-permute-start | bytes 184328 | tf_op jit(solution)/shard_map/ppermute | solution.py:280
  22.6 5.2 %collective-permute-start.10 = (bf16[80,384]{1,0:T(8,128)(2,1)S(1)}, bf16[80,384]{1,0:T(8,128)(2,1)S(1)}, u32[]{:S(2)}, u32[]{:S(2)}) collective-permute-start(bf16[80,384]{1,0:T(8,128)(2,1)S(1)} %hidden.1.near0), channel_id=1, source_target_pairs={{0,12},{2,14},{4,8},{6,10},{8,4},{10,6},{12,0},{14,2},{16,28},{18,... | collective-permute-start | bytes 184328 | tf_op jit(solution)/shard_map/ppermute | solution.py:280
  24.3 4.2 %collective-permute-start.9 = (bf16[80,384]{1,0:T(8,128)(2,1)S(1)}, bf16[80,384]{1,0:T(8,128)(2,1)S(1)}, u32[]{:S(2)}, u32[]{:S(2)}) collective-permute-start(bf16[80,384]{1,0:T(8,128)(2,1)S(1)} %hidden.1.near0), channel_id=1, source_target_pairs={{0,8},{2,10},{4,12},{6,14},{8,0},{10,2},{12,4},{14,6},{16,24},{18,... | collective-permute-start | bytes 184328 | tf_op jit(solution)/shard_map/ppermute | solution.py:280
  24.8 4.2 %collective-permute-start.8 = (bf16[80,384]{1,0:T(8,128)(2,1)S(1)}, bf16[80,384]{1,0:T(8,128)(2,1)S(1)}, u32[]{:S(2)}, u32[]{:S(2)}) collective-permute-start(bf16[80,384]{1,0:T(8,128)(2,1)S(1)} %hidden.1.near0), channel_id=1, source_target_pairs={{0,4},{2,6},{4,0},{6,2},{8,12},{10,14},{12,8},{14,10},{16,20},{18,... | collective-permute-start | bytes 184328 | tf_op jit(solution)/shard_map/ppermute | solution.py:280
  29.1 1.6 %collective-permute-start.11 = (bf16[4,80,384]{2,1,0:T(8,128)(2,1)S(1)}, bf16[4,80,384]{2,1,0:T(8,128)(2,1)S(1)}, u32[]{:S(2)}, u32[]{:S(2)}) collective-permute-start(bf16[4,80,384]{2,1,0:T(8,128)(2,1)S(1)} %pad_maximum_fusion), channel_id=1, source_target_pairs={{0,2},{2,0},{4,6},{6,4},{8,10},{10,8},{12,14},{14,12},{16,18},{18,... | collective-permute-start | bytes 737288 | tf_op jit(solution)/shard_map/ppermute | solution.py:280
  31.1 3.9 %collective-permute-start.12 = (bf16[24,320]{1,0:T(8,128)(2,1)S(1)}, bf16[24,320]{1,0:T(8,128)(2,1)S(1)}, u32[]{:S(2)}, u32[]{:S(2)}) collective-permute-start(bf16[24,320]{1,0:T(8,128)(2,1)S(1)} %get-tuple-element.53), channel_id=1, source_target_pairs={{0,1},{1,0},{2,3},{3,2},{4,5},{5,4},{6,7},{7,6},{8,9},{9,8},{10,11... | collective-permute-start | bytes 46088 | tf_op jit(solution)/shard_map/ppermute | solution.py:284

commit v6 on v5

--- a/solution.py
+++ b/solution.py
@@ -257,11 +257,12 @@
 def token_grad_kernel(own, recv, onehot, out, held, sems):
     blocks = [own[...]] + [recv[j] for j in range(recv.shape[0])]
     slot_grad = jnp.concatenate([block.astype(F32) for block in blocks], axis=0).T.astype(BF16)
-    count, _, width = held.shape
     copies = []
-    for i in range(count):
-        held[i] = dot(slot_grad, onehot[:, i * width : (i + 1) * width], (1, 0)).astype(BF16)
-        copies.append(pltpu.make_async_copy(held.at[i], out.at[:, pl.ds(i * width, width)], sems.at[i]))
+    step = out.shape[0] // 5
+    for i in range(5):
+        rows = pl.ds(i * step, step)
+        held[rows, :] = dot(slot_grad[i * step : (i + 1) * step], onehot[...], (1, 0)).astype(BF16)
+        copies.append(pltpu.make_async_copy(held.at[rows], out.at[rows], sems.at[i]))
         copies[i].start()
     for copy in copies:
         copy.wait()
@@ -426,7 +427,7 @@
         out_shape=jax.ShapeDtypeStruct((features, token_count), BF16),
         in_specs=[VMEM] * 3,
         out_specs=HBM,
-        scratch_shapes=[pltpu.VMEM((4, features, token_count // 4), BF16), pltpu.SemaphoreType.DMA((4,))],
+        scratch_shapes=[pltpu.VMEM((features, token_count), BF16), pltpu.SemaphoreType.DMA((5,))],
         compiler_params=PARAMS,
         name="token_grad",
     )(slot_own, slot_recv, onehot).T

time: 36.3 us -> 36.3 us (level)
  no operation moved by 1% of the time
where the time goes in v6:
time: 36.3 us; the launch traced here: 36.1 us
  starting transfers between devices  14.4 us (40%)
  Pallas kernels  10.4 us (29%)
  waiting for transfers between devices  10.1 us (28%)
  between operations  0.82 us (2%)
    ppermute x10, starting transfers between devices, swap(): return lax.ppermute(x, 'fsdp', [(i, i ^ mask) for i in range(fsdp)])  10.5 us
    ppermute x10, waiting for transfers between devices, swap(): return lax.ppermute(x, 'fsdp', [(i, i ^ mask) for i in range(fsdp)])  8.47 us
    ppermute x2, starting transfers between devices, to_expert(): return (x[0], lax.ppermute(x[1], 'expert', [(0, 1), (1, 0)])[None])  3.79 us
    pallas_call x1, Pallas kernels, local(): pl.pallas_call(weight_grad_kernel, out_shape=(grad_shape,) * 3 + (jax.Sha...  2.36 us
    pallas_call x1, Pallas kernels, local(): pl.pallas_call(gather_kernel, out_shape=(jax.ShapeDtypeStruct((experts, 2...  1.96 us
    pallas_call x1, Pallas kernels, local(): pl.pallas_call(near_kernel, out_shape=(jax.ShapeDtypeStruct((rows, featur...  1.36 us
    pallas_call x1, Pallas kernels, local(): pl.pallas_call(load_kernel, out_shape=half_shape, in_specs=[VMEM] + [HBM]...  1.35 us
    pallas_call x1, Pallas kernels, local(): pl.pallas_call(token_grad_kernel, out_shape=jax.ShapeDtypeStruct((feature...  1.11 us
  transfers between devices with their start and end apart: 13, of which 11 were waited for; matrix products, arithmetic and copies ran while one was open for 0% of the time, Pallas kernels for 17%

profile of v6, /device:TPU:0, one launch (start us, length us, event | category | flops | bytes accessed | tf_op | source)
XLA Modules:
  0.0 36.1 jit_solution(111503035539523663)
XLA Ops:
  0.6 2.0 %gather_rows.1 = (bf16[2,2,24,320]{3,2,1,0:T(8,128)(2,1)S(1)}, bf16[48,1024]{1,0:T(8,128)(2,1)S(1)}, bf16[3,320,768]{2,1,0:T(8,128)(2,1)S(1)}) custom-call(s32[2,24]{1,0:T(2,128)} %bitcast.47, bf16[320,1024]{1,0:T(8,128)(2,1)} %bitcast.44, bf16[320,1024]{1,0:T(8,128)(2,1)} %bitcast.45, bf16[1,320,1536]{2,1,0:T(8,128)(2,1)} %w_gate.1, ...), custom_call_target="tpu_custom_call" | custom-call | tf_op jit(solution)/shard_map/gather_rows/pallas_call | solution.py:290
  2.6 0.5 %collective-permute-start.3 = (bf16[3,320,768]{2,1,0:T(8,128)(2,1)S(1)}, bf16[3,320,768]{2,1,0:T(8,128)(2,1)S(1)}, u32[]{:S(2)}, u32[]{:S(2)}) collective-permute-start(bf16[3,320,768]{2,1,0:T(8,128)(2,1)S(1)} %get-tuple-element.30.weights), channel_id=1, source_target_pairs={{0,2},{2,0},{4,6},{6,4},{8,10},{10,8},{12,14},{14,12},{16,18},{18,... | collective-permute-start | bytes 4423688 | tf_op jit(solution)/shard_map/ppermute | solution.py:281
  3.1 2.6 %collective-permute-start = (bf16[2,24,320]{2,1,0:T(8,128)(2,1)S(1)}, bf16[2,24,320]{2,1,0:T(8,128)(2,1)S(1)}, u32[]{:S(2)}, u32[]{:S(2)}) collective-permute-start(bf16[2,24,320]{2,1,0:T(8,128)(2,1)S(1)} %get-tuple-element.51), channel_id=1, source_target_pairs={{0,1},{1,0},{2,3},{3,2},{4,5},{5,4},{6,7},{7,6},{8,9},{9,8},{10,11... | collective-permute-start | bytes 92168 | tf_op jit(solution)/shard_map/ppermute | solution.py:285
  5.7 0.2 collective-permute-start.2
  5.9 0.1 collective-permute-start.1
  5.9 1.4 %load_weights.1.weights = bf16[3,320,768]{2,1,0:T(8,128)(2,1)S(1)} custom-call(bf16[2,24,320]{2,1,0:T(8,128)(2,1)S(1)} %get-tuple-element.52.own.after, bf16[1,320,1536]{2,1,0:T(8,128)(2,1)} %w_gate.1, bf16[1,320,1536]{2,1,0:T(8,128)(2,1)} %w_up.1, bf16[1,320,1536]{2,1,0:T(8,128)(2,1)} %w_down.1), custom_call_target="tpu_custom_call" | custom-call | bytes 1474560 | tf_op jit(solution)/shard_map/load_weights/pallas_call | solution.py:318
  7.3 0.5 %collective-permute-done = bf16[2,24,320]{2,1,0:T(8,128)(2,1)S(1)} collective-permute-done((bf16[2,24,320]{2,1,0:T(8,128)(2,1)S(1)}, bf16[2,24,320]{2,1,0:T(8,128)(2,1)S(1)}, u32[]{:S(2)}, u32[]{:S(2)}) %collective-permute-start) | collective-permute-done | bytes 30752 | tf_op jit(solution)/shard_map/ppermute | solution.py:285
  7.8 0.4 %partial_sums.1.kept = f32[4,72,384]{2,1,0:T(8,128)S(1)} custom-call(bf16[2,24,320]{2,1,0:T(8,128)(2,1)S(1)} %get-tuple-element.52.own.after, bf16[1,2,24,320]{3,2,1,0:T(8,128)(2,1)S(1)} %bitcast.39, bf16[3,320,768]{2,1,0:T(8,128)(2,1)S(1)} %load_weights.1.weights), custom_call_target="tpu_custom_call" | custom-call | flops 70778880 | bytes 1474560 | tf_op jit(solution)/shard_map/partial_sums/pallas_call | solution.py:328
  8.2 0.9 %collective-permute-done.2 = bf16[2,24,320]{2,1,0:T(8,128)(2,1)S(1)} collective-permute-done((bf16[2,24,320]{2,1,0:T(8,128)(2,1)S(1)}, bf16[2,24,320]{2,1,0:T(8,128)(2,1)S(1)}, u32[]{:S(2)}, u32[]{:S(2)}) %collective-permute-start.2) | collective-permute-done | bytes 30752 | tf_op jit(solution)/shard_map/ppermute | solution.py:313
  9.1 0.0 collective-permute-done.1.own
  9.1 0.0 collective-permute-done.3.weights
  9.1 0.0 copy-start
  9.1 0.0 copy-start.1
  9.1 0.6 %add_other_core.1 = (f32[72,384]{1,0:T(8,128)S(1)}, f32[8,384]{1,0:T(8,128)S(1)}, f32[80,384]{1,0:T(8,128)S(1)}, f32[80,384]{1,0:T(8,128)S(1)}, f32[80,384]{1,0:T(8,128)S(1)}) custom-call(f32[4,72,384]{2,1,0:T(8,128)S(1)} %partial_sums.1.kept, bf16[2,24,320]{2,1,0:T(8,128)(2,1)S(1)} %collective-permute-done.1.own, bf16[1,2,24,320]{3,2,1,0:T(8,128)(2,1)S(1)} %bitcast.41, ...), custom_call_target="tpu_custom_call" | custom-call | tf_op jit(solution)/shard_map/add_other_core/pallas_call | solution.py:352
  9.7 2.6 %collective-permute-start.6 = (f16[80,384]{1,0:T(8,128)(2,1)S(1)}, f16[80,384]{1,0:T(8,128)(2,1)S(1)}, u32[]{:S(2)}, u32[]{:S(2)}) collective-permute-start(f16[80,384]{1,0:T(8,128)(2,1)S(1)} %convert_element_type.26), channel_id=1, source_target_pairs={{0,12},{2,14},{4,8},{6,10},{8,4},{10,6},{12,0},{14,2},{16,28},{18,... | collective-permute-start | bytes 184328 | tf_op jit(solution)/shard_map/ppermute | solution.py:281
  12.3 0.5 %collective-permute-start.5 = (f16[80,384]{1,0:T(8,128)(2,1)S(1)}, f16[80,384]{1,0:T(8,128)(2,1)S(1)}, u32[]{:S(2)}, u32[]{:S(2)}) collective-permute-start(f16[80,384]{1,0:T(8,128)(2,1)S(1)} %convert_element_type.24), channel_id=1, source_target_pairs={{0,8},{2,10},{4,12},{6,14},{8,0},{10,2},{12,4},{14,6},{16,24},{18,... | collective-permute-start | bytes 184328 | tf_op jit(solution)/shard_map/ppermute | solution.py:281
  12.9 0.5 %collective-permute-start.4 = (f16[80,384]{1,0:T(8,128)(2,1)S(1)}, f16[80,384]{1,0:T(8,128)(2,1)S(1)}, u32[]{:S(2)}, u32[]{:S(2)}) collective-permute-start(f16[80,384]{1,0:T(8,128)(2,1)S(1)} %convert_element_type.22), channel_id=1, source_target_pairs={{0,4},{2,6},{4,0},{6,2},{8,12},{10,14},{12,8},{14,10},{16,20},{18,... | collective-permute-start | bytes 184328 | tf_op jit(solution)/shard_map/ppermute | solution.py:281
  13.4 1.6 %collective-permute-done.6 = f16[80,384]{1,0:T(8,128)(2,1)S(1)} collective-permute-done((f16[80,384]{1,0:T(8,128)(2,1)S(1)}, f16[80,384]{1,0:T(8,128)(2,1)S(1)}, u32[]{:S(2)}, u32[]{:S(2)}) %collective-permute-start.6) | collective-permute-done | bytes 61472 | tf_op jit(solution)/shard_map/ppermute | solution.py:281
  15.0 1.6 %collective-permute-done.5 = f16[80,384]{1,0:T(8,128)(2,1)S(1)} collective-permute-done((f16[80,384]{1,0:T(8,128)(2,1)S(1)}, f16[80,384]{1,0:T(8,128)(2,1)S(1)}, u32[]{:S(2)}, u32[]{:S(2)}) %collective-permute-start.5) | collective-permute-done | bytes 61472 | tf_op jit(solution)/shard_map/ppermute | solution.py:281
  16.7 0.4 %collective-permute-done.4 = f16[80,384]{1,0:T(8,128)(2,1)S(1)} collective-permute-done((f16[80,384]{1,0:T(8,128)(2,1)S(1)}, f16[80,384]{1,0:T(8,128)(2,1)S(1)}, u32[]{:S(2)}, u32[]{:S(2)}) %collective-permute-start.4) | collective-permute-done | bytes 61472 | tf_op jit(solution)/shard_map/ppermute | solution.py:281
  17.1 0.1 fusion.3
  17.2 2.7 %collective-permute-start.7 = (f16[80,384]{1,0:T(8,128)(2,1)S(1)}, f16[80,384]{1,0:T(8,128)(2,1)S(1)}, u32[]{:S(2)}, u32[]{:S(2)}) collective-permute-start(f16[80,384]{1,0:T(8,128)(2,1)S(1)} %pad_maximum_fusion.1), channel_id=1, source_target_pairs={{0,16},{2,18},{4,20},{6,22},{8,24},{10,26},{12,28},{14,30},{16,0},... | collective-permute-start | bytes 184328 | tf_op jit(solution)/shard_map/ppermute | solution.py:281
  19.9 0.0 copy-done
  19.9 0.0 copy-done.1
  19.9 0.7 %row_facts.1 = (bf16[320,48]{1,0:T(8,128)(2,1)S(1)}, bf16[320,48]{1,0:T(8,128)(2,1)S(1)}, f32[24,128]{1,0:T(8,128)S(1)}, f32[24,128]{1,0:T(8,128)S(1)}, f32[24,128]{1,0:T(8,128)S(1)}) custom-call(s32[2]{0:T(128)S(1)} %bitcast.43, bf16[2,24,320]{2,1,0:T(8,128)(2,1)S(1)} %get-tuple-element.52.own.after, bf16[1,2,24,320]{3,2,1,0:T(8,128)(2,1)S(1)} %bitcast.40, ...), custom_call_target="tpu_custom_call" | custom-call | bytes 122880 | tf_op jit(solution)/shard_map/row_facts/pallas_call | solution.py:342
  20.6 1.8 %collective-permute-done.7 = f16[80,384]{1,0:T(8,128)(2,1)S(1)} collective-permute-done((f16[80,384]{1,0:T(8,128)(2,1)S(1)}, f16[80,384]{1,0:T(8,128)(2,1)S(1)}, u32[]{:S(2)}, u32[]{:S(2)}) %collective-permute-start.7) | collective-permute-done | bytes 61472 | tf_op jit(solution)/shard_map/ppermute | solution.py:281
  22.5 0.2 hidden.1.near0
  22.6 1.6 %collective-permute-start.10 = (bf16[80,384]{1,0:T(8,128)(2,1)S(1)}, bf16[80,384]{1,0:T(8,128)(2,1)S(1)}, u32[]{:S(2)}, u32[]{:S(2)}) collective-permute-start(bf16[80,384]{1,0:T(8,128)(2,1)S(1)} %hidden.1.near0), channel_id=1, source_target_pairs={{0,12},{2,14},{4,8},{6,10},{8,4},{10,6},{12,0},{14,2},{16,28},{18,... | collective-permute-start | bytes 184328 | tf_op jit(solution)/shard_map/ppermute | solution.py:281
  24.3 0.5 %collective-permute-start.9 = (bf16[80,384]{1,0:T(8,128)(2,1)S(1)}, bf16[80,384]{1,0:T(8,128)(2,1)S(1)}, u32[]{:S(2)}, u32[]{:S(2)}) collective-permute-start(bf16[80,384]{1,0:T(8,128)(2,1)S(1)} %hidden.1.near0), channel_id=1, source_target_pairs={{0,8},{2,10},{4,12},{6,14},{8,0},{10,2},{12,4},{14,6},{16,24},{18,... | collective-permute-start | bytes 184328 | tf_op jit(solution)/shard_map/ppermute | solution.py:281
  24.8 1.4 %collective-permute-start.8 = (bf16[80,384]{1,0:T(8,128)(2,1)S(1)}, bf16[80,384]{1,0:T(8,128)(2,1)S(1)}, u32[]{:S(2)}, u32[]{:S(2)}) collective-permute-start(bf16[80,384]{1,0:T(8,128)(2,1)S(1)} %hidden.1.near0), channel_id=1, source_target_pairs={{0,4},{2,6},{4,0},{6,2},{8,12},{10,14},{12,8},{14,10},{16,20},{18,... | collective-permute-start | bytes 184328 | tf_op jit(solution)/shard_map/ppermute | solution.py:281
  26.2 1.6 %collective-permute-done.10.near3 = bf16[80,384]{1,0:T(8,128)(2,1)S(1)} collective-permute-done((bf16[80,384]{1,0:T(8,128)(2,1)S(1)}, bf16[80,384]{1,0:T(8,128)(2,1)S(1)}, u32[]{:S(2)}, u32[]{:S(2)}) %collective-permute-start.10) | collective-permute-done | bytes 61472 | tf_op jit(solution)/shard_map/ppermute | solution.py:281
  27.8 0.7 %collective-permute-done.9.near2 = bf16[80,384]{1,0:T(8,128)(2,1)S(1)} collective-permute-done((bf16[80,384]{1,0:T(8,128)(2,1)S(1)}, bf16[80,384]{1,0:T(8,128)(2,1)S(1)}, u32[]{:S(2)}, u32[]{:S(2)}) %collective-permute-start.9) | collective-permute-done | bytes 61472 | tf_op jit(solution)/shard_map/ppermute | solution.py:281
  28.5 0.5 %collective-permute-done.8.near1 = bf16[80,384]{1,0:T(8,128)(2,1)S(1)} collective-permute-done((bf16[80,384]{1,0:T(8,128)(2,1)S(1)}, bf16[80,384]{1,0:T(8,128)(2,1)S(1)}, u32[]{:S(2)}, u32[]{:S(2)}) %collective-permute-start.8) | collective-permute-done | bytes 61472 | tf_op jit(solution)/shard_map/ppermute | solution.py:281
  29.1 0.1 collective-permute-start.11
  29.2 1.4 %near_piece.1 = (f32[48,320]{1,0:T(8,128)S(1)}, f32[1,320,1536]{2,1,0:T(8,128)}, f32[1,320,1536]{2,1,0:T(8,128)}, f32[1,320,1536]{2,1,0:T(8,128)}) custom-call(bf16[80,384]{1,0:T(8,128)(2,1)S(1)} %hidden.1.near0, bf16[80,384]{1,0:T(8,128)(2,1)S(1)} %collective-permute-done.8.near1, bf16[80,384]{1,0:T(8,128)(2,1)S(1)} %collective-permute-done.9.near2, ...), custom_call_target="tpu_custom_call" | custom-call | flops 94371840 | bytes 1474560 | tf_op jit(solution)/shard_map/near_piece/pallas_call | solution.py:390
  30.6 0.1 collective-permute-done.11.far
  30.7 0.4 %slot_grad.1 = bf16[2,24,320]{2,1,0:T(8,128)(2,1)S(1)} custom-call(f32[48,320]{1,0:T(8,128)S(1)} %get-tuple-element.38.before, bf16[4,80,384]{2,1,0:T(8,128)(2,1)S(1)} %collective-permute-done.11.far, bf16[3,320,768]{2,1,0:T(8,128)(2,1)S(1)} %get-tuple-element.30.weights), custom_call_target="tpu_custom_call" | custom-call | tf_op jit(solution)/shard_map/slot_grad/pallas_call | solution.py:402
  31.1 1.2 %collective-permute-start.12 = (bf16[24,320]{1,0:T(8,128)(2,1)S(1)}, bf16[24,320]{1,0:T(8,128)(2,1)S(1)}, u32[]{:S(2)}, u32[]{:S(2)}) collective-permute-start(bf16[24,320]{1,0:T(8,128)(2,1)S(1)} %get-tuple-element.53), channel_id=1, source_target_pairs={{0,1},{1,0},{2,3},{3,2},{4,5},{5,4},{6,7},{7,6},{8,9},{9,8},{10,11... | collective-permute-start | bytes 46088 | tf_op jit(solution)/shard_map/ppermute | solution.py:285
  32.3 2.4 %weight_grads.1 = (f32[1,320,1536]{2,1,0:T(8,128)}, f32[1,320,1536]{2,1,0:T(8,128)}, f32[1,320,1536]{2,1,0:T(8,128)}, f32[1,3]{1,0:T(1,128)}) custom-call(bf16[80,384]{1,0:T(8,128)(2,1)S(1)} %hidden.1.near0, bf16[80,384]{1,0:T(8,128)(2,1)S(1)} %collective-permute-done.8.near1, ...), custom_call_target="tpu_custom_call", output_to_operand_aliasing={{0}: (7, {}), {1}: (8, {}), {2}: (9, {})} | custom-call | flops 94371840 | bytes 4423680 | tf_op jit(solution)/shard_map/weight_grads/pallas_call | solution.py:411
  34.7 0.3 collective-permute-done.12
  35.0 1.1 %token_grad.1 = bf16[320,1024]{1,0:T(8,128)(2,1)} custom-call(bf16[24,320]{1,0:T(8,128)(2,1)S(1)} %get-tuple-element.54.own, bf16[1,24,320]{2,1,0:T(8,128)(2,1)S(1)} %bitcast.42, bf16[48,1024]{1,0:T(8,128)(2,1)S(1)} %get-tuple-element.39.onehot), custom_call_target="tpu_custom_call" | custom-call | tf_op jit(solution)/shard_map/token_grad/pallas_call | solution.py:425
  (18 shorter events, 0.2 us)
Async XLA Ops:
  2.6 6.5 %collective-permute-start.3 = (bf16[3,320,768]{2,1,0:T(8,128)(2,1)S(1)}, bf16[3,320,768]{2,1,0:T(8,128)(2,1)S(1)}, u32[]{:S(2)}, u32[]{:S(2)}) collective-permute-start(bf16[3,320,768]{2,1,0:T(8,128)(2,1)S(1)} %get-tuple-element.30.weights), channel_id=1, source_target_pairs={{0,2},{2,0},{4,6},{6,4},{8,10},{10,8},{12,14},{14,12},{16,18},{18,... | collective-permute-start | bytes 4423688 | tf_op jit(solution)/shard_map/ppermute | solution.py:281
  3.1 4.7 %collective-permute-start = (bf16[2,24,320]{2,1,0:T(8,128)(2,1)S(1)}, bf16[2,24,320]{2,1,0:T(8,128)(2,1)S(1)}, u32[]{:S(2)}, u32[]{:S(2)}) collective-permute-start(bf16[2,24,320]{2,1,0:T(8,128)(2,1)S(1)} %get-tuple-element.51), channel_id=1, source_target_pairs={{0,1},{1,0},{2,3},{3,2},{4,5},{5,4},{6,7},{7,6},{8,9},{9,8},{10,11... | collective-permute-start | bytes 92168 | tf_op jit(solution)/shard_map/ppermute | solution.py:285
  5.7 3.4 %collective-permute-start.2 = (bf16[2,24,320]{2,1,0:T(8,128)(2,1)S(1)}, bf16[2,24,320]{2,1,0:T(8,128)(2,1)S(1)}, u32[]{:S(2)}, u32[]{:S(2)}) collective-permute-start(bf16[2,24,320]{2,1,0:T(8,128)(2,1)S(1)} %get-tuple-element.51), channel_id=1, source_target_pairs={{0,3},{1,2},{2,1},{3,0},{4,7},{5,6},{6,5},{7,4},{8,11},{9,10},{10,... | collective-permute-start | bytes 92168 | tf_op jit(solution)/shard_map/ppermute | solution.py:313
  5.9 3.2 %collective-permute-start.1 = (bf16[2,24,320]{2,1,0:T(8,128)(2,1)S(1)}, bf16[2,24,320]{2,1,0:T(8,128)(2,1)S(1)}, u32[]{:S(2)}, u32[]{:S(2)}) collective-permute-start(bf16[2,24,320]{2,1,0:T(8,128)(2,1)S(1)} %get-tuple-element.52.own.after), channel_id=1, source_target_pairs={{0,2},{2,0},{4,6},{6,4},{8,10},{10,8},{12,14},{14,12},{16,18},{18,... | collective-permute-start | bytes 92168 | tf_op jit(solution)/shard_map/ppermute | solution.py:281
  9.1 10.8 %copy-start = (s32[1,2]{1,0:T(1,128)S(1)}, s32[1,2]{1,0:T(1,128)}, u32[]{:S(2)}) copy-start(s32[1,2]{1,0:T(1,128)} %param.11) | copy-start | bytes 28
  9.1 10.8 %copy-start.1 = (f32[1,48]{1,0:T(1,128)S(1)}, f32[1,48]{1,0:T(1,128)}, u32[]{:S(2)}) copy-start(f32[1,48]{1,0:T(1,128)} %prob.1) | copy-start | bytes 580
  9.7 5.3 %collective-permute-start.6 = (f16[80,384]{1,0:T(8,128)(2,1)S(1)}, f16[80,384]{1,0:T(8,128)(2,1)S(1)}, u32[]{:S(2)}, u32[]{:S(2)}) collective-permute-start(f16[80,384]{1,0:T(8,128)(2,1)S(1)} %convert_element_type.26), channel_id=1, source_target_pairs={{0,12},{2,14},{4,8},{6,10},{8,4},{10,6},{12,0},{14,2},{16,28},{18,... | collective-permute-start | bytes 184328 | tf_op jit(solution)/shard_map/ppermute | solution.py:281
  12.3 4.3 %collective-permute-start.5 = (f16[80,384]{1,0:T(8,128)(2,1)S(1)}, f16[80,384]{1,0:T(8,128)(2,1)S(1)}, u32[]{:S(2)}, u32[]{:S(2)}) collective-permute-start(f16[80,384]{1,0:T(8,128)(2,1)S(1)} %convert_element_type.24), channel_id=1, source_target_pairs={{0,8},{2,10},{4,12},{6,14},{8,0},{10,2},{12,4},{14,6},{16,24},{18,... | collective-permute-start | bytes 184328 | tf_op jit(solution)/shard_map/ppermute | solution.py:281
  12.9 4.2 %collective-permute-start.4 = (f16[80,384]{1,0:T(8,128)(2,1)S(1)}, f16[80,384]{1,0:T(8,128)(2,1)S(1)}, u32[]{:S(2)}, u32[]{:S(2)}) collective-permute-start(f16[80,384]{1,0:T(8,128)(2,1)S(1)} %convert_element_type.22), channel_id=1, source_target_pairs={{0,4},{2,6},{4,0},{6,2},{8,12},{10,14},{12,8},{14,10},{16,20},{18,... | collective-permute-start | bytes 184328 | tf_op jit(solution)/shard_map/ppermute | solution.py:281
  17.2 5.2 %collective-permute-start.7 = (f16[80,384]{1,0:T(8,128)(2,1)S(1)}, f16[80,384]{1,0:T(8,128)(2,1)S(1)}, u32[]{:S(2)}, u32[]{:S(2)}) collective-permute-start(f16[80,384]{1,0:T(8,128)(2,1)S(1)} %pad_maximum_fusion.1), channel_id=1, source_target_pairs={{0,16},{2,18},{4,20},{6,22},{8,24},{10,26},{12,28},{14,30},{16,0},... | collective-permute-start | bytes 184328 | tf_op jit(solution)/shard_map/ppermute | solution.py:281
  22.6 5.2 %collective-permute-start.10 = (bf16[80,384]{1,0:T(8,128)(2,1)S(1)}, bf16[80,384]{1,0:T(8,128)(2,1)S(1)}, u32[]{:S(2)}, u32[]{:S(2)}) collective-permute-start(bf16[80,384]{1,0:T(8,128)(2,1)S(1)} %hidden.1.near0), channel_id=1, source_target_pairs={{0,12},{2,14},{4,8},{6,10},{8,4},{10,6},{12,0},{14,2},{16,28},{18,... | collective-permute-start | bytes 184328 | tf_op jit(solution)/shard_map/ppermute | solution.py:281
  24.3 4.2 %collective-permute-start.9 = (bf16[80,384]{1,0:T(8,128)(2,1)S(1)}, bf16[80,384]{1,0:T(8,128)(2,1)S(1)}, u32[]{:S(2)}, u32[]{:S(2)}) collective-permute-start(bf16[80,384]{1,0:T(8,128)(2,1)S(1)} %hidden.1.near0), channel_id=1, source_target_pairs={{0,8},{2,10},{4,12},{6,14},{8,0},{10,2},{12,4},{14,6},{16,24},{18,... | collective-permute-start | bytes 184328 | tf_op jit(solution)/shard_map/ppermute | solution.py:281
  24.8 4.2 %collective-permute-start.8 = (bf16[80,384]{1,0:T(8,128)(2,1)S(1)}, bf16[80,384]{1,0:T(8,128)(2,1)S(1)}, u32[]{:S(2)}, u32[]{:S(2)}) collective-permute-start(bf16[80,384]{1,0:T(8,128)(2,1)S(1)} %hidden.1.near0), channel_id=1, source_target_pairs={{0,4},{2,6},{4,0},{6,2},{8,12},{10,14},{12,8},{14,10},{16,20},{18,... | collective-permute-start | bytes 184328 | tf_op jit(solution)/shard_map/ppermute | solution.py:281
  29.1 1.6 %collective-permute-start.11 = (bf16[4,80,384]{2,1,0:T(8,128)(2,1)S(1)}, bf16[4,80,384]{2,1,0:T(8,128)(2,1)S(1)}, u32[]{:S(2)}, u32[]{:S(2)}) collective-permute-start(bf16[4,80,384]{2,1,0:T(8,128)(2,1)S(1)} %pad_maximum_fusion), channel_id=1, source_target_pairs={{0,2},{2,0},{4,6},{6,4},{8,10},{10,8},{12,14},{14,12},{16,18},{18,... | collective-permute-start | bytes 737288 | tf_op jit(solution)/shard_map/ppermute | solution.py:281
  31.1 3.9 %collective-permute-start.12 = (bf16[24,320]{1,0:T(8,128)(2,1)S(1)}, bf16[24,320]{1,0:T(8,128)(2,1)S(1)}, u32[]{:S(2)}, u32[]{:S(2)}) collective-permute-start(bf16[24,320]{1,0:T(8,128)(2,1)S(1)} %get-tuple-element.53), channel_id=1, source_target_pairs={{0,1},{1,0},{2,3},{3,2},{4,5},{5,4},{6,7},{7,6},{8,9},{9,8},{10,11... | collective-permute-start | bytes 46088 | tf_op jit(solution)/shard_map/ppermute | solution.py:285

commit v7 on v6

--- a/solution.py
+++ b/solution.py
@@ -147,8 +147,7 @@
     powers = []
     for q in range(3):
         most = functools.reduce(jnp.maximum, [jnp.abs(x[q * rows : (q + 1) * rows]) for x in chunks])
-        most = jnp.max(jnp.max(most, axis=0, keepdims=True), axis=1, keepdims=True)
-        most = jnp.maximum(jnp.broadcast_to(most, (1, width)), 1e-30)
+        most = jnp.maximum(jnp.max(most, axis=0, keepdims=True), 1e-30)
         powers.append(jnp.ceil(jnp.log2(most)) - 14.0)
     power_out[...] = jnp.concatenate(powers + [jnp.zeros((5, width), F32)], axis=0)
     for x, out in zip(chunks[1:], outs):

time: 36.3 us -> 36.1 us (level)
  no operation moved by 1% of the time
where the time goes in v7:
time: 36.1 us; the launch traced here: 36 us
  starting transfers between devices  14.5 us (40%)
  Pallas kernels  10.3 us (29%)
  waiting for transfers between devices  10.1 us (28%)
  between operations  0.82 us (2%)
    ppermute x10, starting transfers between devices, swap(): return lax.ppermute(x, 'fsdp', [(i, i ^ mask) for i in range(fsdp)])  10.5 us
    ppermute x10, waiting for transfers between devices, swap(): return lax.ppermute(x, 'fsdp', [(i, i ^ mask) for i in range(fsdp)])  8.46 us
    ppermute x2, starting transfers between devices, to_expert(): return (x[0], lax.ppermute(x[1], 'expert', [(0, 1), (1, 0)])[None])  3.82 us
    pallas_call x1, Pallas kernels, local(): pl.pallas_call(weight_grad_kernel, out_shape=(grad_shape,) * 3 + (jax.Sha...  2.37 us
    pallas_call x1, Pallas kernels, local(): pl.pallas_call(gather_kernel, out_shape=(jax.ShapeDtypeStruct((experts, 2...  1.96 us
    pallas_call x1, Pallas kernels, local(): pl.pallas_call(near_kernel, out_shape=(jax.ShapeDtypeStruct((rows, featur...  1.37 us
    pallas_call x1, Pallas kernels, local(): pl.pallas_call(load_kernel, out_shape=half_shape, in_specs=[VMEM] + [HBM]...  1.35 us
    pallas_call x1, Pallas kernels, local(): pl.pallas_call(token_grad_kernel, out_shape=jax.ShapeDtypeStruct((feature...  1.11 us
  transfers between devices with their start and end apart: 13, of which 11 were waited for; matrix products, arithmetic and copies ran while one was open for 0% of the time, Pallas kernels for 17%

profile of v7, /device:TPU:0, one launch (start us, length us, event | category | flops | bytes accessed | tf_op | source)
XLA Modules:
  0.0 36.0 jit_solution(13876467861930134711)
XLA Ops:
  0.6 2.0 %gather_rows.1 = (bf16[2,2,24,320]{3,2,1,0:T(8,128)(2,1)S(1)}, bf16[48,1024]{1,0:T(8,128)(2,1)S(1)}, bf16[3,320,768]{2,1,0:T(8,128)(2,1)S(1)}) custom-call(s32[2,24]{1,0:T(2,128)} %bitcast.47, bf16[320,1024]{1,0:T(8,128)(2,1)} %bitcast.44, bf16[320,1024]{1,0:T(8,128)(2,1)} %bitcast.45, bf16[1,320,1536]{2,1,0:T(8,128)(2,1)} %w_gate.1, ...), custom_call_target="tpu_custom_call" | custom-call | tf_op jit(solution)/shard_map/gather_rows/pallas_call | solution.py:289
  2.6 0.5 %collective-permute-start.3 = (bf16[3,320,768]{2,1,0:T(8,128)(2,1)S(1)}, bf16[3,320,768]{2,1,0:T(8,128)(2,1)S(1)}, u32[]{:S(2)}, u32[]{:S(2)}) collective-permute-start(bf16[3,320,768]{2,1,0:T(8,128)(2,1)S(1)} %get-tuple-element.30.weights), channel_id=1, source_target_pairs={{0,2},{2,0},{4,6},{6,4},{8,10},{10,8},{12,14},{14,12},{16,18},{18,... | collective-permute-start | bytes 4423688 | tf_op jit(solution)/shard_map/ppermute | solution.py:280
  3.1 2.6 %collective-permute-start = (bf16[2,24,320]{2,1,0:T(8,128)(2,1)S(1)}, bf16[2,24,320]{2,1,0:T(8,128)(2,1)S(1)}, u32[]{:S(2)}, u32[]{:S(2)}) collective-permute-start(bf16[2,24,320]{2,1,0:T(8,128)(2,1)S(1)} %get-tuple-element.51), channel_id=1, source_target_pairs={{0,1},{1,0},{2,3},{3,2},{4,5},{5,4},{6,7},{7,6},{8,9},{9,8},{10,11... | collective-permute-start | bytes 92168 | tf_op jit(solution)/shard_map/ppermute | solution.py:284
  5.7 0.2 collective-permute-start.2
  5.9 0.1 collective-permute-start.1
  5.9 1.4 %load_weights.1.weights = bf16[3,320,768]{2,1,0:T(8,128)(2,1)S(1)} custom-call(bf16[2,24,320]{2,1,0:T(8,128)(2,1)S(1)} %get-tuple-element.52.own.after, bf16[1,320,1536]{2,1,0:T(8,128)(2,1)} %w_gate.1, bf16[1,320,1536]{2,1,0:T(8,128)(2,1)} %w_up.1, bf16[1,320,1536]{2,1,0:T(8,128)(2,1)} %w_down.1), custom_call_target="tpu_custom_call" | custom-call | bytes 1474560 | tf_op jit(solution)/shard_map/load_weights/pallas_call | solution.py:317
  7.3 0.5 %collective-permute-done = bf16[2,24,320]{2,1,0:T(8,128)(2,1)S(1)} collective-permute-done((bf16[2,24,320]{2,1,0:T(8,128)(2,1)S(1)}, bf16[2,24,320]{2,1,0:T(8,128)(2,1)S(1)}, u32[]{:S(2)}, u32[]{:S(2)}) %collective-permute-start) | collective-permute-done | bytes 30752 | tf_op jit(solution)/shard_map/ppermute | solution.py:284
  7.8 0.4 %partial_sums.1.kept = f32[4,72,384]{2,1,0:T(8,128)S(1)} custom-call(bf16[2,24,320]{2,1,0:T(8,128)(2,1)S(1)} %get-tuple-element.52.own.after, bf16[1,2,24,320]{3,2,1,0:T(8,128)(2,1)S(1)} %bitcast.39, bf16[3,320,768]{2,1,0:T(8,128)(2,1)S(1)} %load_weights.1.weights), custom_call_target="tpu_custom_call" | custom-call | flops 70778880 | bytes 1474560 | tf_op jit(solution)/shard_map/partial_sums/pallas_call | solution.py:327
  8.2 0.9 %collective-permute-done.2 = bf16[2,24,320]{2,1,0:T(8,128)(2,1)S(1)} collective-permute-done((bf16[2,24,320]{2,1,0:T(8,128)(2,1)S(1)}, bf16[2,24,320]{2,1,0:T(8,128)(2,1)S(1)}, u32[]{:S(2)}, u32[]{:S(2)}) %collective-permute-start.2) | collective-permute-done | bytes 30752 | tf_op jit(solution)/shard_map/ppermute | solution.py:312
  9.1 0.0 collective-permute-done.1.own
  9.1 0.0 collective-permute-done.3.weights
  9.1 0.0 copy-start
  9.1 0.0 copy-start.1
  9.1 0.5 %add_other_core.1 = (f32[72,384]{1,0:T(8,128)S(1)}, f32[8,384]{1,0:T(8,128)S(1)}, f32[80,384]{1,0:T(8,128)S(1)}, f32[80,384]{1,0:T(8,128)S(1)}, f32[80,384]{1,0:T(8,128)S(1)}) custom-call(f32[4,72,384]{2,1,0:T(8,128)S(1)} %partial_sums.1.kept, bf16[2,24,320]{2,1,0:T(8,128)(2,1)S(1)} %collective-permute-done.1.own, bf16[1,2,24,320]{3,2,1,0:T(8,128)(2,1)S(1)} %bitcast.41, ...), custom_call_target="tpu_custom_call" | custom-call | tf_op jit(solution)/shard_map/add_other_core/pallas_call | solution.py:351
  9.6 2.6 %collective-permute-start.6 = (f16[80,384]{1,0:T(8,128)(2,1)S(1)}, f16[80,384]{1,0:T(8,128)(2,1)S(1)}, u32[]{:S(2)}, u32[]{:S(2)}) collective-permute-start(f16[80,384]{1,0:T(8,128)(2,1)S(1)} %convert_element_type.26), channel_id=1, source_target_pairs={{0,12},{2,14},{4,8},{6,10},{8,4},{10,6},{12,0},{14,2},{16,28},{18,... | collective-permute-start | bytes 184328 | tf_op jit(solution)/shard_map/ppermute | solution.py:280
  12.2 0.5 %collective-permute-start.5 = (f16[80,384]{1,0:T(8,128)(2,1)S(1)}, f16[80,384]{1,0:T(8,128)(2,1)S(1)}, u32[]{:S(2)}, u32[]{:S(2)}) collective-permute-start(f16[80,384]{1,0:T(8,128)(2,1)S(1)} %convert_element_type.24), channel_id=1, source_target_pairs={{0,8},{2,10},{4,12},{6,14},{8,0},{10,2},{12,4},{14,6},{16,24},{18,... | collective-permute-start | bytes 184328 | tf_op jit(solution)/shard_map/ppermute | solution.py:280
  12.8 0.5 %collective-permute-start.4 = (f16[80,384]{1,0:T(8,128)(2,1)S(1)}, f16[80,384]{1,0:T(8,128)(2,1)S(1)}, u32[]{:S(2)}, u32[]{:S(2)}) collective-permute-start(f16[80,384]{1,0:T(8,128)(2,1)S(1)} %convert_element_type.22), channel_id=1, source_target_pairs={{0,4},{2,6},{4,0},{6,2},{8,12},{10,14},{12,8},{14,10},{16,20},{18,... | collective-permute-start | bytes 184328 | tf_op jit(solution)/shard_map/ppermute | solution.py:280
  13.3 1.6 %collective-permute-done.6 = f16[80,384]{1,0:T(8,128)(2,1)S(1)} collective-permute-done((f16[80,384]{1,0:T(8,128)(2,1)S(1)}, f16[80,384]{1,0:T(8,128)(2,1)S(1)}, u32[]{:S(2)}, u32[]{:S(2)}) %collective-permute-start.6) | collective-permute-done | bytes 61472 | tf_op jit(solution)/shard_map/ppermute | solution.py:280
  14.9 1.6 %collective-permute-done.5 = f16[80,384]{1,0:T(8,128)(2,1)S(1)} collective-permute-done((f16[80,384]{1,0:T(8,128)(2,1)S(1)}, f16[80,384]{1,0:T(8,128)(2,1)S(1)}, u32[]{:S(2)}, u32[]{:S(2)}) %collective-permute-start.5) | collective-permute-done | bytes 61472 | tf_op jit(solution)/shard_map/ppermute | solution.py:280
  16.6 0.4 %collective-permute-done.4 = f16[80,384]{1,0:T(8,128)(2,1)S(1)} collective-permute-done((f16[80,384]{1,0:T(8,128)(2,1)S(1)}, f16[80,384]{1,0:T(8,128)(2,1)S(1)}, u32[]{:S(2)}, u32[]{:S(2)}) %collective-permute-start.4) | collective-permute-done | bytes 61472 | tf_op jit(solution)/shard_map/ppermute | solution.py:280
  17.0 0.1 fusion.3
  17.1 2.7 %collective-permute-start.7 = (f16[80,384]{1,0:T(8,128)(2,1)S(1)}, f16[80,384]{1,0:T(8,128)(2,1)S(1)}, u32[]{:S(2)}, u32[]{:S(2)}) collective-permute-start(f16[80,384]{1,0:T(8,128)(2,1)S(1)} %pad_maximum_fusion.1), channel_id=1, source_target_pairs={{0,16},{2,18},{4,20},{6,22},{8,24},{10,26},{12,28},{14,30},{16,0},... | collective-permute-start | bytes 184328 | tf_op jit(solution)/shard_map/ppermute | solution.py:280
  19.8 0.0 copy-done
  19.8 0.0 copy-done.1
  19.8 0.7 %row_facts.1 = (bf16[320,48]{1,0:T(8,128)(2,1)S(1)}, bf16[320,48]{1,0:T(8,128)(2,1)S(1)}, f32[24,128]{1,0:T(8,128)S(1)}, f32[24,128]{1,0:T(8,128)S(1)}, f32[24,128]{1,0:T(8,128)S(1)}) custom-call(s32[2]{0:T(128)S(1)} %bitcast.43, bf16[2,24,320]{2,1,0:T(8,128)(2,1)S(1)} %get-tuple-element.52.own.after, bf16[1,2,24,320]{3,2,1,0:T(8,128)(2,1)S(1)} %bitcast.40, ...), custom_call_target="tpu_custom_call" | custom-call | bytes 122880 | tf_op jit(solution)/shard_map/row_facts/pallas_call | solution.py:341
  20.5 1.8 %collective-permute-done.7 = f16[80,384]{1,0:T(8,128)(2,1)S(1)} collective-permute-done((f16[80,384]{1,0:T(8,128)(2,1)S(1)}, f16[80,384]{1,0:T(8,128)(2,1)S(1)}, u32[]{:S(2)}, u32[]{:S(2)}) %collective-permute-start.7) | collective-permute-done | bytes 61472 | tf_op jit(solution)/shard_map/ppermute | solution.py:280
  22.4 0.2 hidden.1.near0
  22.6 1.6 %collective-permute-start.10 = (bf16[80,384]{1,0:T(8,128)(2,1)S(1)}, bf16[80,384]{1,0:T(8,128)(2,1)S(1)}, u32[]{:S(2)}, u32[]{:S(2)}) collective-permute-start(bf16[80,384]{1,0:T(8,128)(2,1)S(1)} %hidden.1.near0), channel_id=1, source_target_pairs={{0,12},{2,14},{4,8},{6,10},{8,4},{10,6},{12,0},{14,2},{16,28},{18,... | collective-permute-start | bytes 184328 | tf_op jit(solution)/shard_map/ppermute | solution.py:280
  24.2 0.5 %collective-permute-start.9 = (bf16[80,384]{1,0:T(8,128)(2,1)S(1)}, bf16[80,384]{1,0:T(8,128)(2,1)S(1)}, u32[]{:S(2)}, u32[]{:S(2)}) collective-permute-start(bf16[80,384]{1,0:T(8,128)(2,1)S(1)} %hidden.1.near0), channel_id=1, source_target_pairs={{0,8},{2,10},{4,12},{6,14},{8,0},{10,2},{12,4},{14,6},{16,24},{18,... | collective-permute-start | bytes 184328 | tf_op jit(solution)/shard_map/ppermute | solution.py:280
  24.7 1.4 %collective-permute-start.8 = (bf16[80,384]{1,0:T(8,128)(2,1)S(1)}, bf16[80,384]{1,0:T(8,128)(2,1)S(1)}, u32[]{:S(2)}, u32[]{:S(2)}) collective-permute-start(bf16[80,384]{1,0:T(8,128)(2,1)S(1)} %hidden.1.near0), channel_id=1, source_target_pairs={{0,4},{2,6},{4,0},{6,2},{8,12},{10,14},{12,8},{14,10},{16,20},{18,... | collective-permute-start | bytes 184328 | tf_op jit(solution)/shard_map/ppermute | solution.py:280
  26.1 1.6 %collective-permute-done.10.near3 = bf16[80,384]{1,0:T(8,128)(2,1)S(1)} collective-permute-done((bf16[80,384]{1,0:T(8,128)(2,1)S(1)}, bf16[80,384]{1,0:T(8,128)(2,1)S(1)}, u32[]{:S(2)}, u32[]{:S(2)}) %collective-permute-start.10) | collective-permute-done | bytes 61472 | tf_op jit(solution)/shard_map/ppermute | solution.py:280
  27.8 0.7 %collective-permute-done.9.near2 = bf16[80,384]{1,0:T(8,128)(2,1)S(1)} collective-permute-done((bf16[80,384]{1,0:T(8,128)(2,1)S(1)}, bf16[80,384]{1,0:T(8,128)(2,1)S(1)}, u32[]{:S(2)}, u32[]{:S(2)}) %collective-permute-start.9) | collective-permute-done | bytes 61472 | tf_op jit(solution)/shard_map/ppermute | solution.py:280
  28.4 0.5 %collective-permute-done.8.near1 = bf16[80,384]{1,0:T(8,128)(2,1)S(1)} collective-permute-done((bf16[80,384]{1,0:T(8,128)(2,1)S(1)}, bf16[80,384]{1,0:T(8,128)(2,1)S(1)}, u32[]{:S(2)}, u32[]{:S(2)}) %collective-permute-start.8) | collective-permute-done | bytes 61472 | tf_op jit(solution)/shard_map/ppermute | solution.py:280
  29.0 0.1 collective-permute-start.11
  29.1 1.4 %near_piece.1 = (f32[48,320]{1,0:T(8,128)S(1)}, f32[1,320,1536]{2,1,0:T(8,128)}, f32[1,320,1536]{2,1,0:T(8,128)}, f32[1,320,1536]{2,1,0:T(8,128)}) custom-call(bf16[80,384]{1,0:T(8,128)(2,1)S(1)} %hidden.1.near0, bf16[80,384]{1,0:T(8,128)(2,1)S(1)} %collective-permute-done.8.near1, bf16[80,384]{1,0:T(8,128)(2,1)S(1)} %collective-permute-done.9.near2, ...), custom_call_target="tpu_custom_call" | custom-call | flops 94371840 | bytes 1474560 | tf_op jit(solution)/shard_map/near_piece/pallas_call | solution.py:389
  30.5 0.1 collective-permute-done.11.far
  30.6 0.4 %slot_grad.1 = bf16[2,24,320]{2,1,0:T(8,128)(2,1)S(1)} custom-call(f32[48,320]{1,0:T(8,128)S(1)} %get-tuple-element.38.before, bf16[4,80,384]{2,1,0:T(8,128)(2,1)S(1)} %collective-permute-done.11.far, bf16[3,320,768]{2,1,0:T(8,128)(2,1)S(1)} %get-tuple-element.30.weights), custom_call_target="tpu_custom_call" | custom-call | tf_op jit(solution)/shard_map/slot_grad/pallas_call | solution.py:401
  31.0 1.2 %collective-permute-start.12 = (bf16[24,320]{1,0:T(8,128)(2,1)S(1)}, bf16[24,320]{1,0:T(8,128)(2,1)S(1)}, u32[]{:S(2)}, u32[]{:S(2)}) collective-permute-start(bf16[24,320]{1,0:T(8,128)(2,1)S(1)} %get-tuple-element.53), channel_id=1, source_target_pairs={{0,1},{1,0},{2,3},{3,2},{4,5},{5,4},{6,7},{7,6},{8,9},{9,8},{10,11... | collective-permute-start | bytes 46088 | tf_op jit(solution)/shard_map/ppermute | solution.py:284
  32.3 2.4 %weight_grads.1 = (f32[1,320,1536]{2,1,0:T(8,128)}, f32[1,320,1536]{2,1,0:T(8,128)}, f32[1,320,1536]{2,1,0:T(8,128)}, f32[1,3]{1,0:T(1,128)}) custom-call(bf16[80,384]{1,0:T(8,128)(2,1)S(1)} %hidden.1.near0, bf16[80,384]{1,0:T(8,128)(2,1)S(1)} %collective-permute-done.8.near1, ...), custom_call_target="tpu_custom_call", output_to_operand_aliasing={{0}: (7, {}), {1}: (8, {}), {2}: (9, {})} | custom-call | flops 94371840 | bytes 4423680 | tf_op jit(solution)/shard_map/weight_grads/pallas_call | solution.py:410
  34.7 0.2 collective-permute-done.12
  34.9 1.1 %token_grad.1 = bf16[320,1024]{1,0:T(8,128)(2,1)} custom-call(bf16[24,320]{1,0:T(8,128)(2,1)S(1)} %get-tuple-element.54.own, bf16[1,24,320]{2,1,0:T(8,128)(2,1)S(1)} %bitcast.42, bf16[48,1024]{1,0:T(8,128)(2,1)S(1)} %get-tuple-element.39.onehot), custom_call_target="tpu_custom_call" | custom-call | tf_op jit(solution)/shard_map/token_grad/pallas_call | solution.py:424
  (18 shorter events, 0.2 us)
Async XLA Ops:
  2.6 6.5 %collective-permute-start.3 = (bf16[3,320,768]{2,1,0:T(8,128)(2,1)S(1)}, bf16[3,320,768]{2,1,0:T(8,128)(2,1)S(1)}, u32[]{:S(2)}, u32[]{:S(2)}) collective-permute-start(bf16[3,320,768]{2,1,0:T(8,128)(2,1)S(1)} %get-tuple-element.30.weights), channel_id=1, source_target_pairs={{0,2},{2,0},{4,6},{6,4},{8,10},{10,8},{12,14},{14,12},{16,18},{18,... | collective-permute-start | bytes 4423688 | tf_op jit(solution)/shard_map/ppermute | solution.py:280
  3.1 4.7 %collective-permute-start = (bf16[2,24,320]{2,1,0:T(8,128)(2,1)S(1)}, bf16[2,24,320]{2,1,0:T(8,128)(2,1)S(1)}, u32[]{:S(2)}, u32[]{:S(2)}) collective-permute-start(bf16[2,24,320]{2,1,0:T(8,128)(2,1)S(1)} %get-tuple-element.51), channel_id=1, source_target_pairs={{0,1},{1,0},{2,3},{3,2},{4,5},{5,4},{6,7},{7,6},{8,9},{9,8},{10,11... | collective-permute-start | bytes 92168 | tf_op jit(solution)/shard_map/ppermute | solution.py:284
  5.7 3.4 %collective-permute-start.2 = (bf16[2,24,320]{2,1,0:T(8,128)(2,1)S(1)}, bf16[2,24,320]{2,1,0:T(8,128)(2,1)S(1)}, u32[]{:S(2)}, u32[]{:S(2)}) collective-permute-start(bf16[2,24,320]{2,1,0:T(8,128)(2,1)S(1)} %get-tuple-element.51), channel_id=1, source_target_pairs={{0,3},{1,2},{2,1},{3,0},{4,7},{5,6},{6,5},{7,4},{8,11},{9,10},{10,... | collective-permute-start | bytes 92168 | tf_op jit(solution)/shard_map/ppermute | solution.py:312
  5.9 3.2 %collective-permute-start.1 = (bf16[2,24,320]{2,1,0:T(8,128)(2,1)S(1)}, bf16[2,24,320]{2,1,0:T(8,128)(2,1)S(1)}, u32[]{:S(2)}, u32[]{:S(2)}) collective-permute-start(bf16[2,24,320]{2,1,0:T(8,128)(2,1)S(1)} %get-tuple-element.52.own.after), channel_id=1, source_target_pairs={{0,2},{2,0},{4,6},{6,4},{8,10},{10,8},{12,14},{14,12},{16,18},{18,... | collective-permute-start | bytes 92168 | tf_op jit(solution)/shard_map/ppermute | solution.py:280
  9.1 10.7 %copy-start = (s32[1,2]{1,0:T(1,128)S(1)}, s32[1,2]{1,0:T(1,128)}, u32[]{:S(2)}) copy-start(s32[1,2]{1,0:T(1,128)} %param.11) | copy-start | bytes 28
  9.1 10.7 %copy-start.1 = (f32[1,48]{1,0:T(1,128)S(1)}, f32[1,48]{1,0:T(1,128)}, u32[]{:S(2)}) copy-start(f32[1,48]{1,0:T(1,128)} %prob.1) | copy-start | bytes 580
  9.6 5.3 %collective-permute-start.6 = (f16[80,384]{1,0:T(8,128)(2,1)S(1)}, f16[80,384]{1,0:T(8,128)(2,1)S(1)}, u32[]{:S(2)}, u32[]{:S(2)}) collective-permute-start(f16[80,384]{1,0:T(8,128)(2,1)S(1)} %convert_element_type.26), channel_id=1, source_target_pairs={{0,12},{2,14},{4,8},{6,10},{8,4},{10,6},{12,0},{14,2},{16,28},{18,... | collective-permute-start | bytes 184328 | tf_op jit(solution)/shard_map/ppermute | solution.py:280
  12.2 4.3 %collective-permute-start.5 = (f16[80,384]{1,0:T(8,128)(2,1)S(1)}, f16[80,384]{1,0:T(8,128)(2,1)S(1)}, u32[]{:S(2)}, u32[]{:S(2)}) collective-permute-start(f16[80,384]{1,0:T(8,128)(2,1)S(1)} %convert_element_type.24), channel_id=1, source_target_pairs={{0,8},{2,10},{4,12},{6,14},{8,0},{10,2},{12,4},{14,6},{16,24},{18,... | collective-permute-start | bytes 184328 | tf_op jit(solution)/shard_map/ppermute | solution.py:280
  12.8 4.2 %collective-permute-start.4 = (f16[80,384]{1,0:T(8,128)(2,1)S(1)}, f16[80,384]{1,0:T(8,128)(2,1)S(1)}, u32[]{:S(2)}, u32[]{:S(2)}) collective-permute-start(f16[80,384]{1,0:T(8,128)(2,1)S(1)} %convert_element_type.22), channel_id=1, source_target_pairs={{0,4},{2,6},{4,0},{6,2},{8,12},{10,14},{12,8},{14,10},{16,20},{18,... | collective-permute-start | bytes 184328 | tf_op jit(solution)/shard_map/ppermute | solution.py:280
  17.1 5.2 %collective-permute-start.7 = (f16[80,384]{1,0:T(8,128)(2,1)S(1)}, f16[80,384]{1,0:T(8,128)(2,1)S(1)}, u32[]{:S(2)}, u32[]{:S(2)}) collective-permute-start(f16[80,384]{1,0:T(8,128)(2,1)S(1)} %pad_maximum_fusion.1), channel_id=1, source_target_pairs={{0,16},{2,18},{4,20},{6,22},{8,24},{10,26},{12,28},{14,30},{16,0},... | collective-permute-start | bytes 184328 | tf_op jit(solution)/shard_map/ppermute | solution.py:280
  22.6 5.2 %collective-permute-start.10 = (bf16[80,384]{1,0:T(8,128)(2,1)S(1)}, bf16[80,384]{1,0:T(8,128)(2,1)S(1)}, u32[]{:S(2)}, u32[]{:S(2)}) collective-permute-start(bf16[80,384]{1,0:T(8,128)(2,1)S(1)} %hidden.1.near0), channel_id=1, source_target_pairs={{0,12},{2,14},{4,8},{6,10},{8,4},{10,6},{12,0},{14,2},{16,28},{18,... | collective-permute-start | bytes 184328 | tf_op jit(solution)/shard_map/ppermute | solution.py:280
  24.2 4.2 %collective-permute-start.9 = (bf16[80,384]{1,0:T(8,128)(2,1)S(1)}, bf16[80,384]{1,0:T(8,128)(2,1)S(1)}, u32[]{:S(2)}, u32[]{:S(2)}) collective-permute-start(bf16[80,384]{1,0:T(8,128)(2,1)S(1)} %hidden.1.near0), channel_id=1, source_target_pairs={{0,8},{2,10},{4,12},{6,14},{8,0},{10,2},{12,4},{14,6},{16,24},{18,... | collective-permute-start | bytes 184328 | tf_op jit(solution)/shard_map/ppermute | solution.py:280
  24.7 4.2 %collective-permute-start.8 = (bf16[80,384]{1,0:T(8,128)(2,1)S(1)}, bf16[80,384]{1,0:T(8,128)(2,1)S(1)}, u32[]{:S(2)}, u32[]{:S(2)}) collective-permute-start(bf16[80,384]{1,0:T(8,128)(2,1)S(1)} %hidden.1.near0), channel_id=1, source_target_pairs={{0,4},{2,6},{4,0},{6,2},{8,12},{10,14},{12,8},{14,10},{16,20},{18,... | collective-permute-start | bytes 184328 | tf_op jit(solution)/shard_map/ppermute | solution.py:280
  29.0 1.6 %collective-permute-start.11 = (bf16[4,80,384]{2,1,0:T(8,128)(2,1)S(1)}, bf16[4,80,384]{2,1,0:T(8,128)(2,1)S(1)}, u32[]{:S(2)}, u32[]{:S(2)}) collective-permute-start(bf16[4,80,384]{2,1,0:T(8,128)(2,1)S(1)} %pad_maximum_fusion), channel_id=1, source_target_pairs={{0,2},{2,0},{4,6},{6,4},{8,10},{10,8},{12,14},{14,12},{16,18},{18,... | collective-permute-start | bytes 737288 | tf_op jit(solution)/shard_map/ppermute | solution.py:280
  31.0 3.8 %collective-permute-start.12 = (bf16[24,320]{1,0:T(8,128)(2,1)S(1)}, bf16[24,320]{1,0:T(8,128)(2,1)S(1)}, u32[]{:S(2)}, u32[]{:S(2)}) collective-permute-start(bf16[24,320]{1,0:T(8,128)(2,1)S(1)} %get-tuple-element.53), channel_id=1, source_target_pairs={{0,1},{1,0},{2,3},{3,2},{4,5},{5,4},{6,7},{7,6},{8,9},{9,8},{10,11... | collective-permute-start | bytes 46088 | tf_op jit(solution)/shard_map/ppermute | solution.py:284

commit v8 on v7

--- a/solution.py
+++ b/solution.py
@@ -173,8 +173,12 @@
 def hidden_kernel(scale, live, diagonal, sums, recv, out):
     rows = sums.shape[0] // 3
     width = sums.shape[1]
-    total = sums[...] + recv[...]
-    gate, up, down = total[:rows], total[rows : 2 * rows], total[2 * rows :]
+    powers = [recv[pl.ds(3 * rows + q, 1), :] for q in range(3)]
+    total = [
+        sums[pl.ds(q * rows, rows), :] + recv[pl.ds(q * rows, rows), :] * jnp.exp2(power)
+        for q, power in enumerate(powers)
+    ]
+    gate, up, down = total
     row_scale = jnp.concatenate([scale[...]] * (width // 128), axis=1)
     sigmoid = jax.nn.sigmoid(gate)
     silu = gate * sigmoid
@@ -367,9 +371,10 @@
         total, power = total + chunk, jnp.maximum(power, its_power)
     power += 2.0
     for b in range(3, steps):
-        arrived, its_power = decoded(swap(coded(total, power).astype(F16), b))
+        arrived = swap(coded(total, power).astype(F16), b)
         if b < steps - 1:
-            total, power = total + arrived, jnp.maximum(power, its_power) + 1.0
+            chunk, its_power = decoded(arrived)
+            total, power = total + chunk, jnp.maximum(power, its_power) + 1.0
     acts = pl.pallas_call(
         hidden_kernel,
         out_shape=jax.ShapeDtypeStruct((3 * rows // 2 + 8, quarter), BF16),
@@ -377,7 +382,7 @@
         out_specs=VMEM,
         compiler_params=PARAMS,
         name="hidden",
-    )(scale, live, diagonal, total, arrived)
+    )(scale, live, diagonal, total, arrived.astype(F32))
     near = [acts, swap(acts, 1), swap(acts, 2), swap(acts, 1, 2)]
     far = swap(jnp.stack(near), 0)
 

time: 36.1 us -> 36.1 us (level)
  no operation moved by 1% of the time
where the time goes in v8:
time: 36.1 us; the launch traced here: 36 us
  starting transfers between devices  14.4 us (40%)
  Pallas kernels  10.3 us (29%)
  waiting for transfers between devices  10.1 us (28%)
  between operations  0.81 us (2%)
    ppermute x10, starting transfers between devices, swap(): return lax.ppermute(x, 'fsdp', [(i, i ^ mask) for i in range(fsdp)])  10.5 us
    ppermute x10, waiting for transfers between devices, swap(): return lax.ppermute(x, 'fsdp', [(i, i ^ mask) for i in range(fsdp)])  8.47 us
    ppermute x2, starting transfers between devices, to_expert(): return (x[0], lax.ppermute(x[1], 'expert', [(0, 1), (1, 0)])[None])  3.79 us
    pallas_call x1, Pallas kernels, local(): pl.pallas_call(weight_grad_kernel, out_shape=(grad_shape,) * 3 + (jax.Sha...  2.36 us
    pallas_call x1, Pallas kernels, local(): pl.pallas_call(gather_kernel, out_shape=(jax.ShapeDtypeStruct((experts, 2...  1.96 us
    pallas_call x1, Pallas kernels, local(): pl.pallas_call(near_kernel, out_shape=(jax.ShapeDtypeStruct((rows, featur...  1.36 us
    pallas_call x1, Pallas kernels, local(): pl.pallas_call(load_kernel, out_shape=half_shape, in_specs=[VMEM] + [HBM]...  1.35 us
    pallas_call x1, Pallas kernels, local(): pl.pallas_call(token_grad_kernel, out_shape=jax.ShapeDtypeStruct((feature...  1.11 us
  transfers between devices with their start and end apart: 13, of which 11 were waited for; matrix products, arithmetic and copies ran while one was open for 0% of the time, Pallas kernels for 17%

profile of v8, /device:TPU:0, one launch (start us, length us, event | category | flops | bytes accessed | tf_op | source)
XLA Modules:
  0.0 36.0 jit_solution(2301639049431581122)
XLA Ops:
  0.6 2.0 %gather_rows.1 = (bf16[2,2,24,320]{3,2,1,0:T(8,128)(2,1)S(1)}, bf16[48,1024]{1,0:T(8,128)(2,1)S(1)}, bf16[3,320,768]{2,1,0:T(8,128)(2,1)S(1)}) custom-call(s32[2,24]{1,0:T(2,128)} %bitcast.45, bf16[320,1024]{1,0:T(8,128)(2,1)} %bitcast.42, bf16[320,1024]{1,0:T(8,128)(2,1)} %bitcast.43, bf16[1,320,1536]{2,1,0:T(8,128)(2,1)} %w_gate.1, ...), custom_call_target="tpu_custom_call" | custom-call | tf_op jit(solution)/shard_map/gather_rows/pallas_call | solution.py:293
  2.6 0.5 %collective-permute-start.3 = (bf16[3,320,768]{2,1,0:T(8,128)(2,1)S(1)}, bf16[3,320,768]{2,1,0:T(8,128)(2,1)S(1)}, u32[]{:S(2)}, u32[]{:S(2)}) collective-permute-start(bf16[3,320,768]{2,1,0:T(8,128)(2,1)S(1)} %get-tuple-element.30.weights), channel_id=1, source_target_pairs={{0,2},{2,0},{4,6},{6,4},{8,10},{10,8},{12,14},{14,12},{16,18},{18,... | collective-permute-start | bytes 4423688 | tf_op jit(solution)/shard_map/ppermute | solution.py:284
  3.1 2.6 %collective-permute-start = (bf16[2,24,320]{2,1,0:T(8,128)(2,1)S(1)}, bf16[2,24,320]{2,1,0:T(8,128)(2,1)S(1)}, u32[]{:S(2)}, u32[]{:S(2)}) collective-permute-start(bf16[2,24,320]{2,1,0:T(8,128)(2,1)S(1)} %get-tuple-element.51), channel_id=1, source_target_pairs={{0,1},{1,0},{2,3},{3,2},{4,5},{5,4},{6,7},{7,6},{8,9},{9,8},{10,11... | collective-permute-start | bytes 92168 | tf_op jit(solution)/shard_map/ppermute | solution.py:288
  5.7 0.2 collective-permute-start.2
  5.9 0.1 collective-permute-start.1
  5.9 1.4 %load_weights.1.weights = bf16[3,320,768]{2,1,0:T(8,128)(2,1)S(1)} custom-call(bf16[2,24,320]{2,1,0:T(8,128)(2,1)S(1)} %get-tuple-element.52.own.after, bf16[1,320,1536]{2,1,0:T(8,128)(2,1)} %w_gate.1, bf16[1,320,1536]{2,1,0:T(8,128)(2,1)} %w_up.1, bf16[1,320,1536]{2,1,0:T(8,128)(2,1)} %w_down.1), custom_call_target="tpu_custom_call" | custom-call | bytes 1474560 | tf_op jit(solution)/shard_map/load_weights/pallas_call | solution.py:321
  7.3 0.5 %collective-permute-done = bf16[2,24,320]{2,1,0:T(8,128)(2,1)S(1)} collective-permute-done((bf16[2,24,320]{2,1,0:T(8,128)(2,1)S(1)}, bf16[2,24,320]{2,1,0:T(8,128)(2,1)S(1)}, u32[]{:S(2)}, u32[]{:S(2)}) %collective-permute-start) | collective-permute-done | bytes 30752 | tf_op jit(solution)/shard_map/ppermute | solution.py:288
  7.8 0.4 %partial_sums.1.kept = f32[4,72,384]{2,1,0:T(8,128)S(1)} custom-call(bf16[2,24,320]{2,1,0:T(8,128)(2,1)S(1)} %get-tuple-element.52.own.after, bf16[1,2,24,320]{3,2,1,0:T(8,128)(2,1)S(1)} %bitcast.37, bf16[3,320,768]{2,1,0:T(8,128)(2,1)S(1)} %load_weights.1.weights), custom_call_target="tpu_custom_call" | custom-call | flops 70778880 | bytes 1474560 | tf_op jit(solution)/shard_map/partial_sums/pallas_call | solution.py:331
  8.2 0.9 %collective-permute-done.2 = bf16[2,24,320]{2,1,0:T(8,128)(2,1)S(1)} collective-permute-done((bf16[2,24,320]{2,1,0:T(8,128)(2,1)S(1)}, bf16[2,24,320]{2,1,0:T(8,128)(2,1)S(1)}, u32[]{:S(2)}, u32[]{:S(2)}) %collective-permute-start.2) | collective-permute-done | bytes 30752 | tf_op jit(solution)/shard_map/ppermute | solution.py:316
  9.1 0.0 collective-permute-done.1.own
  9.1 0.0 collective-permute-done.3.weights
  9.1 0.0 copy-start
  9.1 0.0 copy-start.1
  9.1 0.5 %add_other_core.1 = (f32[72,384]{1,0:T(8,128)S(1)}, f32[8,384]{1,0:T(8,128)S(1)}, f32[80,384]{1,0:T(8,128)S(1)}, f32[80,384]{1,0:T(8,128)S(1)}, f32[80,384]{1,0:T(8,128)S(1)}) custom-call(f32[4,72,384]{2,1,0:T(8,128)S(1)} %partial_sums.1.kept, bf16[2,24,320]{2,1,0:T(8,128)(2,1)S(1)} %collective-permute-done.1.own, bf16[1,2,24,320]{3,2,1,0:T(8,128)(2,1)S(1)} %bitcast.39, ...), custom_call_target="tpu_custom_call" | custom-call | tf_op jit(solution)/shard_map/add_other_core/pallas_call | solution.py:355
  9.6 2.6 %collective-permute-start.6 = (f16[80,384]{1,0:T(8,128)(2,1)S(1)}, f16[80,384]{1,0:T(8,128)(2,1)S(1)}, u32[]{:S(2)}, u32[]{:S(2)}) collective-permute-start(f16[80,384]{1,0:T(8,128)(2,1)S(1)} %convert_element_type.26), channel_id=1, source_target_pairs={{0,12},{2,14},{4,8},{6,10},{8,4},{10,6},{12,0},{14,2},{16,28},{18,... | collective-permute-start | bytes 184328 | tf_op jit(solution)/shard_map/ppermute | solution.py:284
  12.2 0.5 %collective-permute-start.5 = (f16[80,384]{1,0:T(8,128)(2,1)S(1)}, f16[80,384]{1,0:T(8,128)(2,1)S(1)}, u32[]{:S(2)}, u32[]{:S(2)}) collective-permute-start(f16[80,384]{1,0:T(8,128)(2,1)S(1)} %convert_element_type.24), channel_id=1, source_target_pairs={{0,8},{2,10},{4,12},{6,14},{8,0},{10,2},{12,4},{14,6},{16,24},{18,... | collective-permute-start | bytes 184328 | tf_op jit(solution)/shard_map/ppermute | solution.py:284
  12.8 0.5 %collective-permute-start.4 = (f16[80,384]{1,0:T(8,128)(2,1)S(1)}, f16[80,384]{1,0:T(8,128)(2,1)S(1)}, u32[]{:S(2)}, u32[]{:S(2)}) collective-permute-start(f16[80,384]{1,0:T(8,128)(2,1)S(1)} %convert_element_type.22), channel_id=1, source_target_pairs={{0,4},{2,6},{4,0},{6,2},{8,12},{10,14},{12,8},{14,10},{16,20},{18,... | collective-permute-start | bytes 184328 | tf_op jit(solution)/shard_map/ppermute | solution.py:284
  13.3 1.6 %collective-permute-done.6 = f16[80,384]{1,0:T(8,128)(2,1)S(1)} collective-permute-done((f16[80,384]{1,0:T(8,128)(2,1)S(1)}, f16[80,384]{1,0:T(8,128)(2,1)S(1)}, u32[]{:S(2)}, u32[]{:S(2)}) %collective-permute-start.6) | collective-permute-done | bytes 61472 | tf_op jit(solution)/shard_map/ppermute | solution.py:284
  14.9 1.6 %collective-permute-done.5 = f16[80,384]{1,0:T(8,128)(2,1)S(1)} collective-permute-done((f16[80,384]{1,0:T(8,128)(2,1)S(1)}, f16[80,384]{1,0:T(8,128)(2,1)S(1)}, u32[]{:S(2)}, u32[]{:S(2)}) %collective-permute-start.5) | collective-permute-done | bytes 61472 | tf_op jit(solution)/shard_map/ppermute | solution.py:284
  16.6 0.4 %collective-permute-done.4 = f16[80,384]{1,0:T(8,128)(2,1)S(1)} collective-permute-done((f16[80,384]{1,0:T(8,128)(2,1)S(1)}, f16[80,384]{1,0:T(8,128)(2,1)S(1)}, u32[]{:S(2)}, u32[]{:S(2)}) %collective-permute-start.4) | collective-permute-done | bytes 61472 | tf_op jit(solution)/shard_map/ppermute | solution.py:284
  17.0 0.1 fusion.3
  17.1 2.7 %collective-permute-start.7 = (f16[80,384]{1,0:T(8,128)(2,1)S(1)}, f16[80,384]{1,0:T(8,128)(2,1)S(1)}, u32[]{:S(2)}, u32[]{:S(2)}) collective-permute-start(f16[80,384]{1,0:T(8,128)(2,1)S(1)} %pad_maximum_fusion.1), channel_id=1, source_target_pairs={{0,16},{2,18},{4,20},{6,22},{8,24},{10,26},{12,28},{14,30},{16,0},... | collective-permute-start | bytes 184328 | tf_op jit(solution)/shard_map/ppermute | solution.py:284
  19.8 0.0 copy-done
  19.8 0.0 copy-done.1
  19.8 0.7 %row_facts.1 = (bf16[320,48]{1,0:T(8,128)(2,1)S(1)}, bf16[320,48]{1,0:T(8,128)(2,1)S(1)}, f32[24,128]{1,0:T(8,128)S(1)}, f32[24,128]{1,0:T(8,128)S(1)}, f32[24,128]{1,0:T(8,128)S(1)}) custom-call(s32[2]{0:T(128)S(1)} %bitcast.41, bf16[2,24,320]{2,1,0:T(8,128)(2,1)S(1)} %get-tuple-element.52.own.after, bf16[1,2,24,320]{3,2,1,0:T(8,128)(2,1)S(1)} %bitcast.38, ...), custom_call_target="tpu_custom_call" | custom-call | bytes 122880 | tf_op jit(solution)/shard_map/row_facts/pallas_call | solution.py:345
  20.5 1.8 %collective-permute-done.7 = f16[80,384]{1,0:T(8,128)(2,1)S(1)} collective-permute-done((f16[80,384]{1,0:T(8,128)(2,1)S(1)}, f16[80,384]{1,0:T(8,128)(2,1)S(1)}, u32[]{:S(2)}, u32[]{:S(2)}) %collective-permute-start.7) | collective-permute-done | bytes 61472 | tf_op jit(solution)/shard_map/ppermute | solution.py:284
  22.3 0.2 hidden.1.near0
  22.5 1.6 %collective-permute-start.10 = (bf16[80,384]{1,0:T(8,128)(2,1)S(1)}, bf16[80,384]{1,0:T(8,128)(2,1)S(1)}, u32[]{:S(2)}, u32[]{:S(2)}) collective-permute-start(bf16[80,384]{1,0:T(8,128)(2,1)S(1)} %hidden.1.near0), channel_id=1, source_target_pairs={{0,12},{2,14},{4,8},{6,10},{8,4},{10,6},{12,0},{14,2},{16,28},{18,... | collective-permute-start | bytes 184328 | tf_op jit(solution)/shard_map/ppermute | solution.py:284
  24.2 0.5 %collective-permute-start.9 = (bf16[80,384]{1,0:T(8,128)(2,1)S(1)}, bf16[80,384]{1,0:T(8,128)(2,1)S(1)}, u32[]{:S(2)}, u32[]{:S(2)}) collective-permute-start(bf16[80,384]{1,0:T(8,128)(2,1)S(1)} %hidden.1.near0), channel_id=1, source_target_pairs={{0,8},{2,10},{4,12},{6,14},{8,0},{10,2},{12,4},{14,6},{16,24},{18,... | collective-permute-start | bytes 184328 | tf_op jit(solution)/shard_map/ppermute | solution.py:284
  24.7 1.4 %collective-permute-start.8 = (bf16[80,384]{1,0:T(8,128)(2,1)S(1)}, bf16[80,384]{1,0:T(8,128)(2,1)S(1)}, u32[]{:S(2)}, u32[]{:S(2)}) collective-permute-start(bf16[80,384]{1,0:T(8,128)(2,1)S(1)} %hidden.1.near0), channel_id=1, source_target_pairs={{0,4},{2,6},{4,0},{6,2},{8,12},{10,14},{12,8},{14,10},{16,20},{18,... | collective-permute-start | bytes 184328 | tf_op jit(solution)/shard_map/ppermute | solution.py:284
  26.1 1.6 %collective-permute-done.10.near3 = bf16[80,384]{1,0:T(8,128)(2,1)S(1)} collective-permute-done((bf16[80,384]{1,0:T(8,128)(2,1)S(1)}, bf16[80,384]{1,0:T(8,128)(2,1)S(1)}, u32[]{:S(2)}, u32[]{:S(2)}) %collective-permute-start.10) | collective-permute-done | bytes 61472 | tf_op jit(solution)/shard_map/ppermute | solution.py:284
  27.7 0.7 %collective-permute-done.9.near2 = bf16[80,384]{1,0:T(8,128)(2,1)S(1)} collective-permute-done((bf16[80,384]{1,0:T(8,128)(2,1)S(1)}, bf16[80,384]{1,0:T(8,128)(2,1)S(1)}, u32[]{:S(2)}, u32[]{:S(2)}) %collective-permute-start.9) | collective-permute-done | bytes 61472 | tf_op jit(solution)/shard_map/ppermute | solution.py:284
  28.4 0.5 %collective-permute-done.8.near1 = bf16[80,384]{1,0:T(8,128)(2,1)S(1)} collective-permute-done((bf16[80,384]{1,0:T(8,128)(2,1)S(1)}, bf16[80,384]{1,0:T(8,128)(2,1)S(1)}, u32[]{:S(2)}, u32[]{:S(2)}) %collective-permute-start.8) | collective-permute-done | bytes 61472 | tf_op jit(solution)/shard_map/ppermute | solution.py:284
  29.0 0.1 collective-permute-start.11
  29.1 1.4 %near_piece.1 = (f32[48,320]{1,0:T(8,128)S(1)}, f32[1,320,1536]{2,1,0:T(8,128)}, f32[1,320,1536]{2,1,0:T(8,128)}, f32[1,320,1536]{2,1,0:T(8,128)}) custom-call(bf16[80,384]{1,0:T(8,128)(2,1)S(1)} %hidden.1.near0, bf16[80,384]{1,0:T(8,128)(2,1)S(1)} %collective-permute-done.8.near1, bf16[80,384]{1,0:T(8,128)(2,1)S(1)} %collective-permute-done.9.near2, ...), custom_call_target="tpu_custom_call" | custom-call | flops 94371840 | bytes 1474560 | tf_op jit(solution)/shard_map/near_piece/pallas_call | solution.py:394
  30.4 0.1 collective-permute-done.11.far
  30.6 0.4 %slot_grad.1 = bf16[2,24,320]{2,1,0:T(8,128)(2,1)S(1)} custom-call(f32[48,320]{1,0:T(8,128)S(1)} %get-tuple-element.38.before, bf16[4,80,384]{2,1,0:T(8,128)(2,1)S(1)} %collective-permute-done.11.far, bf16[3,320,768]{2,1,0:T(8,128)(2,1)S(1)} %get-tuple-element.30.weights), custom_call_target="tpu_custom_call" | custom-call | tf_op jit(solution)/shard_map/slot_grad/pallas_call | solution.py:406
  31.0 1.2 %collective-permute-start.12 = (bf16[24,320]{1,0:T(8,128)(2,1)S(1)}, bf16[24,320]{1,0:T(8,128)(2,1)S(1)}, u32[]{:S(2)}, u32[]{:S(2)}) collective-permute-start(bf16[24,320]{1,0:T(8,128)(2,1)S(1)} %get-tuple-element.53), channel_id=1, source_target_pairs={{0,1},{1,0},{2,3},{3,2},{4,5},{5,4},{6,7},{7,6},{8,9},{9,8},{10,11... | collective-permute-start | bytes 46088 | tf_op jit(solution)/shard_map/ppermute | solution.py:288
  32.2 2.4 %weight_grads.1 = (f32[1,320,1536]{2,1,0:T(8,128)}, f32[1,320,1536]{2,1,0:T(8,128)}, f32[1,320,1536]{2,1,0:T(8,128)}, f32[1,3]{1,0:T(1,128)}) custom-call(bf16[80,384]{1,0:T(8,128)(2,1)S(1)} %hidden.1.near0, bf16[80,384]{1,0:T(8,128)(2,1)S(1)} %collective-permute-done.8.near1, ...), custom_call_target="tpu_custom_call", output_to_operand_aliasing={{0}: (7, {}), {1}: (8, {}), {2}: (9, {})} | custom-call | flops 94371840 | bytes 4423680 | tf_op jit(solution)/shard_map/weight_grads/pallas_call | solution.py:415
  34.6 0.3 collective-permute-done.12
  34.9 1.1 %token_grad.1 = bf16[320,1024]{1,0:T(8,128)(2,1)} custom-call(bf16[24,320]{1,0:T(8,128)(2,1)S(1)} %get-tuple-element.54.own, bf16[1,24,320]{2,1,0:T(8,128)(2,1)S(1)} %bitcast.40, bf16[48,1024]{1,0:T(8,128)(2,1)S(1)} %get-tuple-element.39.onehot), custom_call_target="tpu_custom_call" | custom-call | tf_op jit(solution)/shard_map/token_grad/pallas_call | solution.py:429
  (16 shorter events, 0.2 us)
Async XLA Ops:
  2.6 6.5 %collective-permute-start.3 = (bf16[3,320,768]{2,1,0:T(8,128)(2,1)S(1)}, bf16[3,320,768]{2,1,0:T(8,128)(2,1)S(1)}, u32[]{:S(2)}, u32[]{:S(2)}) collective-permute-start(bf16[3,320,768]{2,1,0:T(8,128)(2,1)S(1)} %get-tuple-element.30.weights), channel_id=1, source_target_pairs={{0,2},{2,0},{4,6},{6,4},{8,10},{10,8},{12,14},{14,12},{16,18},{18,... | collective-permute-start | bytes 4423688 | tf_op jit(solution)/shard_map/ppermute | solution.py:284
  3.1 4.7 %collective-permute-start = (bf16[2,24,320]{2,1,0:T(8,128)(2,1)S(1)}, bf16[2,24,320]{2,1,0:T(8,128)(2,1)S(1)}, u32[]{:S(2)}, u32[]{:S(2)}) collective-permute-start(bf16[2,24,320]{2,1,0:T(8,128)(2,1)S(1)} %get-tuple-element.51), channel_id=1, source_target_pairs={{0,1},{1,0},{2,3},{3,2},{4,5},{5,4},{6,7},{7,6},{8,9},{9,8},{10,11... | collective-permute-start | bytes 92168 | tf_op jit(solution)/shard_map/ppermute | solution.py:288
  5.7 3.4 %collective-permute-start.2 = (bf16[2,24,320]{2,1,0:T(8,128)(2,1)S(1)}, bf16[2,24,320]{2,1,0:T(8,128)(2,1)S(1)}, u32[]{:S(2)}, u32[]{:S(2)}) collective-permute-start(bf16[2,24,320]{2,1,0:T(8,128)(2,1)S(1)} %get-tuple-element.51), channel_id=1, source_target_pairs={{0,3},{1,2},{2,1},{3,0},{4,7},{5,6},{6,5},{7,4},{8,11},{9,10},{10,... | collective-permute-start | bytes 92168 | tf_op jit(solution)/shard_map/ppermute | solution.py:316
  5.9 3.2 %collective-permute-start.1 = (bf16[2,24,320]{2,1,0:T(8,128)(2,1)S(1)}, bf16[2,24,320]{2,1,0:T(8,128)(2,1)S(1)}, u32[]{:S(2)}, u32[]{:S(2)}) collective-permute-start(bf16[2,24,320]{2,1,0:T(8,128)(2,1)S(1)} %get-tuple-element.52.own.after), channel_id=1, source_target_pairs={{0,2},{2,0},{4,6},{6,4},{8,10},{10,8},{12,14},{14,12},{16,18},{18,... | collective-permute-start | bytes 92168 | tf_op jit(solution)/shard_map/ppermute | solution.py:284
  9.1 10.7 %copy-start = (s32[1,2]{1,0:T(1,128)S(1)}, s32[1,2]{1,0:T(1,128)}, u32[]{:S(2)}) copy-start(s32[1,2]{1,0:T(1,128)} %param.11) | copy-start | bytes 28
  9.1 10.7 %copy-start.1 = (f32[1,48]{1,0:T(1,128)S(1)}, f32[1,48]{1,0:T(1,128)}, u32[]{:S(2)}) copy-start(f32[1,48]{1,0:T(1,128)} %prob.1) | copy-start | bytes 580
  9.6 5.3 %collective-permute-start.6 = (f16[80,384]{1,0:T(8,128)(2,1)S(1)}, f16[80,384]{1,0:T(8,128)(2,1)S(1)}, u32[]{:S(2)}, u32[]{:S(2)}) collective-permute-start(f16[80,384]{1,0:T(8,128)(2,1)S(1)} %convert_element_type.26), channel_id=1, source_target_pairs={{0,12},{2,14},{4,8},{6,10},{8,4},{10,6},{12,0},{14,2},{16,28},{18,... | collective-permute-start | bytes 184328 | tf_op jit(solution)/shard_map/ppermute | solution.py:284
  12.2 4.3 %collective-permute-start.5 = (f16[80,384]{1,0:T(8,128)(2,1)S(1)}, f16[80,384]{1,0:T(8,128)(2,1)S(1)}, u32[]{:S(2)}, u32[]{:S(2)}) collective-permute-start(f16[80,384]{1,0:T(8,128)(2,1)S(1)} %convert_element_type.24), channel_id=1, source_target_pairs={{0,8},{2,10},{4,12},{6,14},{8,0},{10,2},{12,4},{14,6},{16,24},{18,... | collective-permute-start | bytes 184328 | tf_op jit(solution)/shard_map/ppermute | solution.py:284
  12.8 4.2 %collective-permute-start.4 = (f16[80,384]{1,0:T(8,128)(2,1)S(1)}, f16[80,384]{1,0:T(8,128)(2,1)S(1)}, u32[]{:S(2)}, u32[]{:S(2)}) collective-permute-start(f16[80,384]{1,0:T(8,128)(2,1)S(1)} %convert_element_type.22), channel_id=1, source_target_pairs={{0,4},{2,6},{4,0},{6,2},{8,12},{10,14},{12,8},{14,10},{16,20},{18,... | collective-permute-start | bytes 184328 | tf_op jit(solution)/shard_map/ppermute | solution.py:284
  17.1 5.2 %collective-permute-start.7 = (f16[80,384]{1,0:T(8,128)(2,1)S(1)}, f16[80,384]{1,0:T(8,128)(2,1)S(1)}, u32[]{:S(2)}, u32[]{:S(2)}) collective-permute-start(f16[80,384]{1,0:T(8,128)(2,1)S(1)} %pad_maximum_fusion.1), channel_id=1, source_target_pairs={{0,16},{2,18},{4,20},{6,22},{8,24},{10,26},{12,28},{14,30},{16,0},... | collective-permute-start | bytes 184328 | tf_op jit(solution)/shard_map/ppermute | solution.py:284
  22.5 5.2 %collective-permute-start.10 = (bf16[80,384]{1,0:T(8,128)(2,1)S(1)}, bf16[80,384]{1,0:T(8,128)(2,1)S(1)}, u32[]{:S(2)}, u32[]{:S(2)}) collective-permute-start(bf16[80,384]{1,0:T(8,128)(2,1)S(1)} %hidden.1.near0), channel_id=1, source_target_pairs={{0,12},{2,14},{4,8},{6,10},{8,4},{10,6},{12,0},{14,2},{16,28},{18,... | collective-permute-start | bytes 184328 | tf_op jit(solution)/shard_map/ppermute | solution.py:284
  24.2 4.2 %collective-permute-start.9 = (bf16[80,384]{1,0:T(8,128)(2,1)S(1)}, bf16[80,384]{1,0:T(8,128)(2,1)S(1)}, u32[]{:S(2)}, u32[]{:S(2)}) collective-permute-start(bf16[80,384]{1,0:T(8,128)(2,1)S(1)} %hidden.1.near0), channel_id=1, source_target_pairs={{0,8},{2,10},{4,12},{6,14},{8,0},{10,2},{12,4},{14,6},{16,24},{18,... | collective-permute-start | bytes 184328 | tf_op jit(solution)/shard_map/ppermute | solution.py:284
  24.7 4.2 %collective-permute-start.8 = (bf16[80,384]{1,0:T(8,128)(2,1)S(1)}, bf16[80,384]{1,0:T(8,128)(2,1)S(1)}, u32[]{:S(2)}, u32[]{:S(2)}) collective-permute-start(bf16[80,384]{1,0:T(8,128)(2,1)S(1)} %hidden.1.near0), channel_id=1, source_target_pairs={{0,4},{2,6},{4,0},{6,2},{8,12},{10,14},{12,8},{14,10},{16,20},{18,... | collective-permute-start | bytes 184328 | tf_op jit(solution)/shard_map/ppermute | solution.py:284
  29.0 1.6 %collective-permute-start.11 = (bf16[4,80,384]{2,1,0:T(8,128)(2,1)S(1)}, bf16[4,80,384]{2,1,0:T(8,128)(2,1)S(1)}, u32[]{:S(2)}, u32[]{:S(2)}) collective-permute-start(bf16[4,80,384]{2,1,0:T(8,128)(2,1)S(1)} %pad_maximum_fusion), channel_id=1, source_target_pairs={{0,2},{2,0},{4,6},{6,4},{8,10},{10,8},{12,14},{14,12},{16,18},{18,... | collective-permute-start | bytes 737288 | tf_op jit(solution)/shard_map/ppermute | solution.py:284
  31.0 3.9 %collective-permute-start.12 = (bf16[24,320]{1,0:T(8,128)(2,1)S(1)}, bf16[24,320]{1,0:T(8,128)(2,1)S(1)}, u32[]{:S(2)}, u32[]{:S(2)}) collective-permute-start(bf16[24,320]{1,0:T(8,128)(2,1)S(1)} %get-tuple-element.53), channel_id=1, source_target_pairs={{0,1},{1,0},{2,3},{3,2},{4,5},{5,4},{6,7},{7,6},{8,9},{9,8},{10,11... | collective-permute-start | bytes 46088 | tf_op jit(solution)/shard_map/ppermute | solution.py:288
